TPU v7x, 128 devices: a whole 4x4x4 slice. The times are simulated.
128 devices in a mesh: seg: 8 (over y, z_lo), blk: 16 (over z_hi, x, core).
Axes of the slice: x: 4, y: 4, z: 4 (z_hi: 2, z_lo: 2; z = z_hi * 2 + z_lo), core: 2. Of those that a mesh axis runs over, the one named last changes fastest.
Arguments:
- queries: bfloat16 [2048, 2048], P('blk'), may hold values from -8 to 8
- new_kv: bfloat16 [2048, 256], P('blk'), may hold values from -8 to 8
- cache_kv: bfloat16 [65536, 256], P(('seg', 'blk')), may hold values from -8 to 8
- cache_len: int32 [128], replicated, may hold values from 256 to 448
- page_owner: int32 [256, 1], replicated, may hold values from 0 to 127; in each aligned block of 256 rows (0 to 255, 256 to 511, ...) at most 8 rows name the same one
Outputs:
- attn_out: bfloat16 [2048, 2048], P('blk', 'seg')
- cache_out: bfloat16 [65536, 256], P(('seg', 'blk'))
Inputs may be any that keep to these rules, and one draw needn't show every extreme that they name: `page_owner`: every device owns at least one page, no device owns more than 8 pages, and some device owns exactly 8.
All inputs are finite; a program needn't handle non-finite values.
Results may differ from a plain program's by a relative error of at most 0.018.
Values may be sent and summed in bfloat16 or wider, within the bound.
No kernel may reach another device: no remote copies, remote signals or barrier semaphores. Data moves between devices by JAX's collectives and lax.ppermute only.
A program may use at most 64 MiB of HBM per device.

v0:
```python
import math

import jax
import jax.numpy as jnp
from jax import lax
from jax.sharding import PartitionSpec as P

PAGE = 8


neg_large = -1e30


def merged(value, axis, join):
    pieces = jax.tree.map(lambda part: lax.all_gather(part, axis), value)
    head = jax.tree.map(lambda part: part[0], pieces)
    tail = jax.tree.map(lambda part: part[1:], pieces)
    total, _ = lax.scan(lambda total, share: (join(total, share), None), head, tail)
    return total


def slot_table(device, cache_len, page_owner, slot_count, page_rows, span_rows):
    owners = page_owner[:, 0]
    page_total = owners.shape[0]
    owned_mask = (owners == device).astype(jnp.int32)
    earlier = jnp.cumsum(owned_mask) - owned_mask
    owned_count = jnp.sum(owned_mask)
    filled = cache_len[device]
    slot_ids = jnp.arange(slot_count, dtype=jnp.int32)
    offset = slot_ids - filled
    is_new = (offset >= 0) & (offset < page_rows * owned_count)
    wanted = offset // page_rows
    page_match = (owned_mask[None, :] == 1) & (earlier[None, :] == wanted[:, None])
    page_ids = jnp.arange(page_total, dtype=jnp.int32)
    page_of = jnp.sum(jnp.where(page_match, page_ids[None, :], 0), axis=1)
    source_row = jnp.where(is_new, page_of * page_rows + offset % page_rows, 0)
    key_pos = jnp.where(slot_ids < filled, -1, jnp.where(is_new, source_row, span_rows))
    return (source_row, key_pos, is_new)


def combine_parts(left, right):
    top_max = jnp.maximum(left[1], right[1])
    left_weight = jnp.exp(left[1] - top_max)
    right_weight = jnp.exp(right[1] - top_max)
    return (
        left[0] * left_weight[:, None] + right[0] * right_weight[:, None],
        top_max,
        left[2] * left_weight + right[2] * right_weight,
    )


def attend(rows_q, q_pos, keys_vals, key_pos, carried, head_dim):
    key_total = keys_vals.shape[0]
    key_block = math.gcd(key_total, 512)
    score_scale = 1.0 / math.sqrt(head_dim)

    def visit_block(index, inner):
        out_acc, row_max, row_sum = inner
        row_start = index * key_block
        key_piece = lax.dynamic_slice_in_dim(keys_vals, row_start, key_block, 0)
        pos_piece = lax.dynamic_slice_in_dim(key_pos, row_start, key_block, 0)
        scores = (
            lax.dot_general(
                rows_q,
                key_piece[:, :head_dim],
                (((1,), (1,)), ((), ())),
                preferred_element_type=jnp.float32,
            )
            * score_scale
        )
        visible = pos_piece[None, :] <= q_pos[:, None]
        block_max = jnp.max(jnp.where(visible, scores, neg_large), axis=1)
        new_max = jnp.maximum(row_max, block_max)
        factor = jnp.exp(row_max - new_max)
        weights = jnp.where(visible, jnp.exp(scores - new_max[:, None]), 0.0)
        row_sum = row_sum * factor + jnp.sum(weights, axis=1)
        out_acc = out_acc * factor[:, None] + jnp.dot(
            weights.astype(jnp.bfloat16),
            key_piece[:, head_dim:],
            preferred_element_type=jnp.float32,
        )
        return (out_acc, new_max, row_sum)

    return lax.fori_loop(0, key_total // key_block, visit_block, carried)


def on_device(queries, new_kv, cache_kv, cache_len, page_owner):
    head_dim = new_kv.shape[1] // 2
    q_rows = queries.shape[0]
    head_count = queries.shape[1] // head_dim
    slot_count = cache_kv.shape[0]
    cycle_size = lax.axis_size("blk")
    group_count = lax.axis_size("seg")
    seg_id = lax.axis_index("seg")
    blk_id = lax.axis_index("blk")
    device = seg_id * cycle_size + blk_id
    span_rows = q_rows * cycle_size
    gathered = lax.all_gather(new_kv, "blk", axis=0, tiled=True)
    source_row, key_pos, is_new = slot_table(
        device, cache_len, page_owner, slot_count, PAGE, span_rows
    )
    cache_new = jnp.where(is_new[:, None], jnp.take(gathered, source_row, axis=0), cache_kv)
    rows_total = q_rows * head_count
    start_state = (
        jnp.zeros((rows_total, head_dim), jnp.float32),
        jnp.full((rows_total,), neg_large, jnp.float32),
        jnp.zeros((rows_total,), jnp.float32),
    )
    own_q = queries.reshape(rows_total, head_dim)
    row_token = jnp.arange(rows_total, dtype=jnp.int32) // head_count
    own_pos = blk_id * q_rows + row_token
    group_pos = jax.vmap(
        lambda member: slot_table(
            seg_id * cycle_size + member, cache_len, page_owner, slot_count, PAGE, span_rows
        )[1]
    )(jnp.arange(cycle_size, dtype=jnp.int32)).reshape(-1)
    out_acc, row_max, row_sum = attend(
        own_q,
        own_pos,
        lax.all_gather(cache_new, "blk", axis=0, tiled=True),
        group_pos,
        start_state,
        head_dim,
    )
    heads_here = head_count // group_count
    merged_out, merged_max, merged_sum = merged((out_acc, row_max, row_sum), "seg", combine_parts)
    whole = (merged_out / merged_sum[:, None]).reshape(q_rows, head_count, head_dim)
    result = lax.dynamic_slice_in_dim(whole, seg_id * heads_here, heads_here, 1)
    attended = result.reshape(q_rows, heads_here * head_dim).astype(jnp.bfloat16)
    return (attended, cache_new)


def solution(mesh):
    placed = (P("blk", None), P("blk", None), P(("seg", "blk"), None), P(), P())
    return jax.shard_map(
        on_device,
        mesh=mesh,
        in_specs=placed,
        out_specs=(P("blk", "seg"), P(("seg", "blk"), None)),
        check_vma=False,
    )
```

profile of v0, /device:TPU:1, one launch (start us, length us, event | category | flops | bytes accessed | tf_op | source)
XLA Modules:
  0.0 486.8 jit_solution(15889171043484408463)
XLA Ops:
  15.6 43.6 %all-gather.7.cloned.1.call-done = bf16[2048,256]{1,0:T(8,128)(2,1)} async-done(((bf16[128,256]{1,0:T(8,128)(2,1)}), bf16[2048,256]{1,0:T(8,128)(2,1)}) %all-gather.7.cloned.1.call-update) | async-done | bytes 1048592 | tf_op jit(solution)/shard_map/all_gather | solution.py:98
  71.5 47.4 %all-gather.9.cloned.1.call-done = bf16[8192,256]{1,0:T(8,128)(2,1)} async-done(((bf16[512,256]{1,0:T(8,128)(2,1)}), bf16[8192,256]{1,0:T(8,128)(2,1)}) %all-gather.9.cloned.1.call-update) | async-done | bytes 4194320 | tf_op jit(solution)/shard_map/all_gather | solution.py:120
  118.9 169.9 %while.33 = (s32[]{:T(128)}, f32[2048,128]{1,0:T(8,128)S(1)}, f32[2048]{0:T(1024)S(1)}, f32[2048]{0:T(1024)S(1)}, s32[8192]{0:T(1024)S(1)}, /*index=5*/bf16[8192...) while((s32[]{:T(128)}, f32[2048,128]{1,0:T(8,128)S(1)}, ...), condition=%wide.region_11.12_spmd.clone, body=%wide.region_8.11_spmd.clone.sunk | while | flops 552366080 | bytes 15640791 | solution.py:84
  119.0 3.6 fusion.58
  122.6 3.2 fusion.59
  125.8 3.7 convolution_add_fusion.2
  129.6 3.6 fusion.58
  133.2 3.2 fusion.59
  136.4 3.7 convolution_add_fusion.2
  140.2 3.6 fusion.58
  143.8 3.2 fusion.59
  147.0 3.7 convolution_add_fusion.2
  150.8 3.6 fusion.58
  154.4 3.2 fusion.59
  157.6 3.7 convolution_add_fusion.2
  161.4 3.6 fusion.58
  165.1 3.2 fusion.59
  168.2 3.7 convolution_add_fusion.2
  172.1 3.6 fusion.58
  175.7 3.2 fusion.59
  178.9 3.7 convolution_add_fusion.2
  182.7 3.6 fusion.58
  186.3 3.2 fusion.59
  189.5 3.7 convolution_add_fusion.2
  193.3 3.6 fusion.58
  196.9 3.2 fusion.59
  200.1 3.7 convolution_add_fusion.2
  203.9 3.6 fusion.58
  210.7 3.7 convolution_add_fusion.2
  214.6 3.6 fusion.58
  221.4 3.7 convolution_add_fusion.2
  225.2 3.6 fusion.58
  232.0 3.7 convolution_add_fusion.2
  235.8 3.6 fusion.58
  242.6 3.7 convolution_add_fusion.2
  246.4 3.6 fusion.58
  253.2 3.7 convolution_add_fusion.2
  257.1 3.6 fusion.58
  263.9 3.7 convolution_add_fusion.2
  267.7 3.6 fusion.58
  274.5 3.7 convolution_add_fusion.2
  278.3 3.6 fusion.58
  285.1 3.7 convolution_add_fusion.2
  289.9 31.2 %all-gather.1 = f32[16384]{0:T(1024)S(1)} all-gather(f32[2048]{0:T(1024)S(1)} %get-tuple-element.182), channel_id=3, replica_groups=mesh['seg'=8,'blk'=16] {'seg'}, dimensions={0}, use_global_device_ids=true | all-gather | bytes 73728 | tf_op jit(solution)/shard_map/all_gather | solution.py:15
  321.1 36.4 %all-gather.2 = f32[16384]{0:T(1024)S(1)} all-gather(f32[2048]{0:T(1024)S(1)} %get-tuple-element.183), channel_id=4, replica_groups=mesh['seg'=8,'blk'=16] {'seg'}, dimensions={0}, use_global_device_ids=true | all-gather | bytes 73728 | tf_op jit(solution)/shard_map/all_gather | solution.py:15
  357.5 101.2 %all-gather.11.cloned.1.call-done = f32[16384,128]{1,0:T(8,128)} async-done(((f32[2048,128]{1,0:T(8,128)}), f32[16384,128]{1,0:T(8,128)}) %all-gather.11.cloned.1.call-update) | async-done | bytes 8388624 | tf_op jit(solution)/shard_map/all_gather | solution.py:15
  458.8 5.4 %slice.72 = f32[14336,128]{1,0:T(8,128)} slice(f32[16384,128]{1,0:T(8,128)} %all-gather.11.cloned.1.call-done), slice={[2048:16384], [0:128]} | slice | bytes 14680064 | tf_op jit(solution)/shard_map/slice | solution.py:17
  464.2 15.1 %while.32 = (s32[]{:T(128)}, f32[2048,128]{1,0:T(8,128)S(1)}, f32[2048]{0:T(1024)S(1)}, f32[2048]{0:T(1024)S(1)}, f32[7,2048]{1,0:T(8,128)S(1)}, /*index=5*/f32[...) while((s32[]{:T(128)}, f32[2048,128]{1,0:T(8,128)S(1)}, f32[2048]{0:T(1024)S(1)}, f32[2048]{0:T(1024)S(1)}, ...), condition=%wide.region_13.14_spmd, body=%wide.region_12.13_spmd.sunk | while | flops 798722 | bytes 3260509 | solution.py:18
  (174 shorter events, 63.8 us)
Async XLA Ops:
  7.2 60.7 %copy-start.2 = (s32[256,1]{0,1:T(1,128)S(1)}, s32[256,1]{0,1:T(1,128)}, u32[]{:S(2)}) copy-start(s32[256,1]{0,1:T(1,128)} %param.13) | copy-start | bytes 3076
  7.2 64.0 %copy-start.1 = (bf16[128,2048]{1,0:T(8,128)(2,1)S(1)}, bf16[128,2048]{1,0:T(8,128)(2,1)}, u32[]{:S(2)}) copy-start(bf16[128,2048]{1,0:T(8,128)(2,1)} %param.9) | copy-start | bytes 1572868
  7.2 52.1 %all-gather.7.cloned.1.call-start = ((), (), s32[]{:S(2)}) async-start(), calls=%async_computation | async-start | bytes 1114112 | tf_op jit(solution)/shard_map/all_gather | solution.py:98
  7.9 111.0 %all-gather.9.cloned.1.call-start = ((), (), s32[]{:S(2)}) async-start(), calls=%async_computation.1 | async-start | bytes 4456448 | tf_op jit(solution)/shard_map/all_gather | solution.py:120
  64.1 394.7 %all-gather.11.cloned.1.call-start = ((), (), s32[]{:S(2)}) async-start(), calls=%async_computation.2 | async-start | bytes 9437184 | tf_op jit(solution)/shard_map/all_gather | solution.py:15
  288.8 1.1 copy-start
  458.8 5.4 %slice-start = ((f32[16384,128]{1,0:T(8,128)}), f32[2048,128]{1,0:T(8,128)S(1)}, s32[]{:S(2)}) async-start(f32[16384,128]{1,0:T(8,128)} %all-gather.11.cloned.1.call-done), calls=%async_computation.3 | async-start | bytes 2097152 | tf_op jit(solution)/shard_map/slice | solution.py:16
Sparse Core Ops, SparseCore 0:
  10.5 48.7 all-gather.6
  64.2 54.6 all-gather.8
  290.0 168.7 all-gather.10
where the time goes:
time: 492 us; the launch traced here: 487 us
  waiting for transfers between devices  193 us (39%)
  matrix products  117 us (24%)
  other arithmetic  78.7 us (16%)
  blocking collectives  67.6 us (14%)
  local copies, waits for them, and re-layouts  14.9 us (3%)
  between operations  14.7 us (3%)
    all_gather x1, waiting for transfers between devices, merged(): pieces = jax.tree.map(lambda part: lax.all_gather(part, axis), value)  101 us
    all_gather x2, blocking collectives, merged(): pieces = jax.tree.map(lambda part: lax.all_gather(part, axis), value)  67.6 us
    dot_general x16, matrix products, visit_block(): jnp.dot(weights.astype(jnp.bfloat16), key_piece[:, head_dim:], preferred_...  59.3 us
    dot_general x16, matrix products, visit_block(): lax.dot_general(rows_q, key_piece[:, :head_dim], (((1,), (1,)), ((), ()))...  57.7 us
    reduce_sum x16, other arithmetic, visit_block(): row_sum = row_sum * factor + jnp.sum(weights, axis=1)  50.6 us
    all_gather x1, waiting for transfers between devices, on_device(): lax.all_gather(cache_new, 'blk', axis=0, tiled=True)  47.4 us
    all_gather x1, waiting for transfers between devices, on_device(): gathered = lax.all_gather(new_kv, 'blk', axis=0, tiled=True)  43.6 us
    add x7, other arithmetic, combine_parts(): left[0] * left_weight[:, None] + right[0] * right_weight[:, None]  14.6 us
  transfers between devices with their start and end apart: 3, of which 3 were waited for; matrix products, arithmetic and copies ran while one was open for 3% of the time, Pallas kernels for 0%

commit v1 on v0

v1 whole, which is shorter than its diff:
```python
import functools

import jax
import jax.numpy as jnp
from jax import lax
from jax.experimental import pallas as pl
from jax.experimental.pallas import tpu as pltpu
from jax.sharding import PartitionSpec as P


F32 = jnp.float32
BF16 = jnp.bfloat16
HEADS = 16
HD = 128
TOK = 128
ROWS = HEADS * TOK
SLOTS = 512
FILL = 448
PAGE = 8
NSEG = 8
NBLK = 16
SHARE = TOK // NSEG
CHUNK = 2 * HD + 16
ACC = HD + 16
NEG = -1e30
SCALE = 1.4426950408889634 / HD**0.5
VMEM = pl.BlockSpec(memory_space=pltpu.VMEM)
SMEM = pl.BlockSpec(memory_space=pltpu.SMEM)
AXES = ("seg", "blk")


def neighbours(dx=0, flip_z=False, flip_core=False):
    pairs = []
    for here in range(NSEG * NBLK):
        seg, blk = divmod(here, NBLK)
        pairs.append((here, device_at(seg, blk, dx, flip_z, flip_core)))
    return pairs


def device_at(seg, blk, dx, flip_z, flip_core):
    y, z_lo = seg // 2, seg % 2
    z_hi, x, core = blk // 8, (blk // 2) % 4, blk % 2
    if flip_z:
        z_lo, z_hi = 1 - z_lo, 1 - z_hi
    if flip_core:
        core = 1 - core
    x = (x + dx) % 4
    return (y * 2 + z_lo) * NBLK + z_hi * 8 + x * 2 + core


def origin(slot):
    return device_at(lax.axis_index("seg"), lax.axis_index("blk"), *slot)


def queries_kernel(q_ref, qt_ref):
    for h in range(HEADS):
        cols = slice(h * HD, (h + 1) * HD)
        scaled = q_ref[:, cols].astype(F32).T * SCALE
        high = scaled.astype(BF16)
        qt_ref[0:HD, cols] = high
        qt_ref[HD : 2 * HD, cols] = (scaled - high.astype(F32)).astype(BF16)


def flash_kernel(slots, first, last, width, *refs):
    count = len(slots)
    len_ref, qt_ref = refs[0], refs[1]
    blocks = refs[2 : 2 + count]
    at = 2 + count
    if last:
        fresh_ref = refs[at]
        at += 1
    if not first:
        m_in, acc_in = refs[at], refs[at + 1]
        at += 2
    if last:
        part_ref = refs[at]
        at += 1
    else:
        m_ref, acc_ref = refs[at], refs[at + 1]
        at += 2
    keys, vals, vals_t = refs[at:]
    total = keys.shape[0]
    for j, slot in enumerate(slots):
        filled = len_ref[origin(slot)]
        ok = lax.broadcasted_iota(jnp.int32, (FILL, HD), 0) < filled
        key = blocks[j][0:FILL, 0:HD]
        value = blocks[j][0:FILL, HD : 2 * HD]
        key = jnp.where(ok, key, jnp.broadcast_to(key[0:1], (FILL, HD)))
        rows = slice(j * FILL, (j + 1) * FILL)
        keys[rows, 0:HD] = key
        keys[rows, HD : 2 * HD] = key
        vals[rows, 0:HD] = jnp.where(ok, value, jnp.zeros_like(value))
        vals[rows, HD : 2 * HD] = ok.astype(BF16)
    tiles = [(j * FILL, FILL) for j in range(count)]
    if last:
        rows = slice(count * FILL, total)
        tiles.append((count * FILL, total - count * FILL))
        keys[rows, 0:HD] = fresh_ref[:, 0:HD]
        keys[rows, HD : 2 * HD] = fresh_ref[:, 0:HD]
        vals[rows, 0:HD] = fresh_ref[:, HD : 2 * HD]
        vals[rows, HD : 2 * HD] = jnp.ones((total - count * FILL, HD), BF16)
        seg = lax.axis_index("seg")
        shape = (NBLK * SHARE, width)
        key_id = lax.broadcasted_iota(jnp.int32, shape, 0)
        key_pos = key_id // SHARE * TOK + seg * SHARE + key_id % SHARE
        token = lax.axis_index("blk") * TOK + lax.broadcasted_iota(jnp.int32, shape, 1) % TOK
        seen = key_pos <= token
    for c in range(total // 128):
        rows = slice(c * 128, (c + 1) * 128)
        vals_t[0:HD, rows] = vals[rows, 0:HD].T
        vals_t[HD:ACC, rows] = vals[rows, HD : 2 * HD].T[0 : ACC - HD]
    for r in range(ROWS // width):
        cols = slice(r * width, (r + 1) * width)
        query = qt_ref[:, cols]
        scores = []
        top = None if first else m_in[0:1, cols]
        for start, size in tiles:
            s = jnp.dot(keys[start : start + size, :], query, preferred_element_type=F32)
            if start == count * FILL:
                s = jnp.where(seen, s, NEG)
            scores.append(s)
            tile_top = jnp.max(s, axis=0, keepdims=True)
            top = tile_top if top is None else jnp.maximum(top, tile_top)
        out = None if first else acc_in[:, cols] * jnp.exp2(m_in[0:1, cols] - top)
        for s, (start, size) in zip(scores, tiles):
            w = jnp.exp2(s - top).astype(BF16)
            term = jnp.dot(vals_t[:, start : start + size], w, preferred_element_type=F32)
            out = term if out is None else out + term
        if not last:
            acc_ref[:, cols] = out
            m_ref[:, cols] = jnp.broadcast_to(top, (8, width))
        else:
            total_w = out[HD : HD + 1]
            normal = (out[0:HD] * (1.0 / total_w)).astype(BF16)
            log_sum = top + jnp.log2(total_w)
            a = log_sum.astype(BF16)
            rest = log_sum - a.astype(F32)
            b = rest.astype(BF16)
            c = (rest - b.astype(F32)).astype(BF16)
            for i in range(width // TOK):
                head = r * (width // TOK) + i
                lanes = slice(i * TOK, (i + 1) * TOK)
                part_ref[head // 2, head % 2 * HD : (head % 2 + 1) * HD, :] = normal[:, lanes]
                stat = 2 * HD + head % 2 * 3
                part_ref[head // 2, stat : stat + 1, :] = a[:, lanes]
                part_ref[head // 2, stat + 1 : stat + 2, :] = b[:, lanes]
                part_ref[head // 2, stat + 2 : stat + 3, :] = c[:, lanes]


def flash(slots, cache_len, qt, blocks, state, fresh=None, width=512):
    first, last = state is None, fresh is not None
    total = len(slots) * FILL + (NBLK * SHARE if last else 0)
    operands = [cache_len, qt, *blocks]
    if last:
        operands.append(fresh)
    if not first:
        operands += list(state)
    if last:
        out_shape = jax.ShapeDtypeStruct((NSEG, CHUNK, TOK), BF16)
        out_specs = VMEM
    else:
        out_shape = [jax.ShapeDtypeStruct((8, ROWS), F32), jax.ShapeDtypeStruct((ACC, ROWS), F32)]
        out_specs = [VMEM, VMEM]
    return pl.pallas_call(
        functools.partial(flash_kernel, slots, first, last, width),
        in_specs=[SMEM] + [VMEM] * (len(operands) - 1),
        out_specs=out_specs,
        out_shape=out_shape,
        scratch_shapes=[
            pltpu.VMEM((total, 2 * HD), BF16),
            pltpu.VMEM((total, 2 * HD), BF16),
            pltpu.VMEM((ACC, total), BF16),
        ],
        compiler_params=pltpu.CompilerParams(vmem_limit_bytes=32 * 1024 * 1024),
        cost_estimate=pl.CostEstimate(
            flops=4 * total * ROWS * 256, bytes_accessed=1 << 20, transcendentals=total * ROWS
        ),
        name=f"flash_{len(slots)}",
    )(*operands)


def pages_kernel(slots, len_ref, owner_ref, cache_ref, *refs):
    blocks, out_ref, rows_ref = refs[: len(slots)], refs[-2], refs[-1]
    for block, slot in zip(blocks, slots):
        blk = origin(slot) % NBLK
        rows_ref[pl.ds(pl.multiple_of(blk * TOK, TOK), TOK), :] = block[FILL : FILL + TOK, :]
    device = lax.axis_index("seg") * NBLK + lax.axis_index("blk")
    filled = len_ref[device]
    pages = owner_ref.shape[0]
    new_rows = pages * PAGE
    owned = jnp.broadcast_to((owner_ref[...] == device).astype(F32), (pages, 128)).T[0:16].astype(BF16)
    before = (
        lax.broadcasted_iota(jnp.int32, (pages, pages), 0) < lax.broadcasted_iota(jnp.int32, (pages, pages), 1)
    ).astype(BF16)
    rank = jnp.dot(owned, before, preferred_element_type=F32)
    rank = jnp.where(owned > 0, rank, -1.0).astype(BF16)
    spread = (
        lax.broadcasted_iota(jnp.int32, (pages, new_rows), 1) // PAGE
        == lax.broadcasted_iota(jnp.int32, (pages, new_rows), 0)
    ).astype(BF16)
    row_rank = jnp.dot(rank, spread, preferred_element_type=F32)[0:1].astype(jnp.int32)
    target = filled + row_rank * PAGE + lax.broadcasted_iota(jnp.int32, (1, new_rows), 1) % PAGE
    target = jnp.where(row_rank >= 0, target, -1)
    half = SLOTS // 2
    pick = (lax.broadcasted_iota(jnp.int32, (half, new_rows), 0) + half == target).astype(BF16)
    written = jnp.dot(pick, rows_ref[...], preferred_element_type=F32).astype(BF16)
    count = jnp.max(row_rank) + 1
    slot_id = lax.broadcasted_iota(jnp.int32, (half, 2 * HD), 0) + half
    is_new = (slot_id >= filled) & (slot_id < filled + count * PAGE)
    out_ref[0:half, :] = cache_ref[0:half, :]
    out_ref[half:SLOTS, :] = jnp.where(is_new, written, cache_ref[half:SLOTS, :])


def write_pages(slots, cache_len, page_owner, cache_kv, blocks):
    return pl.pallas_call(
        functools.partial(pages_kernel, slots),
        in_specs=[SMEM] + [VMEM] * (2 + len(blocks)),
        out_specs=VMEM,
        out_shape=jax.ShapeDtypeStruct(cache_kv.shape, BF16),
        scratch_shapes=[pltpu.VMEM((NBLK * TOK, 2 * HD), BF16)],
        compiler_params=pltpu.CompilerParams(vmem_limit_bytes=32 * 1024 * 1024),
        cost_estimate=pl.CostEstimate(flops=10**9, bytes_accessed=4 << 20, transcendentals=0),
        name="write_pages",
    )(cache_len, page_owner, cache_kv, *blocks)


def fresh_kernel(slots, *refs):
    blocks, out_ref = refs[:-1], refs[-1]
    start = pl.multiple_of(FILL + lax.axis_index("seg") * SHARE, SHARE)
    for block, slot in zip(blocks, slots):
        blk = origin(slot) % NBLK
        out_ref[pl.ds(pl.multiple_of(blk * SHARE, SHARE), SHARE), :] = block[pl.ds(start, SHARE), :]


def fresh_share(slots, blocks):
    return pl.pallas_call(
        functools.partial(fresh_kernel, slots),
        in_specs=[VMEM] * len(blocks),
        out_specs=VMEM,
        out_shape=jax.ShapeDtypeStruct((NBLK * SHARE, 2 * HD), BF16),
        name="fresh_share",
    )(*blocks)


def merge_kernel(parts_ref, out_ref):
    for head in range(2):
        stat = 2 * HD + head * 3
        logs = []
        for s in range(NSEG):
            three = [parts_ref[s, stat + i : stat + i + 1, :].astype(F32) for i in range(3)]
            logs.append(three[0] + three[1] + three[2])
        top = functools.reduce(jnp.maximum, logs)
        weights = [jnp.exp2(v - top) for v in logs]
        scale = 1.0 / functools.reduce(jnp.add, weights)
        out = None
        for s in range(NSEG):
            term = parts_ref[s, head * HD : (head + 1) * HD, :].astype(F32) * (weights[s] * scale)
            out = term if out is None else out + term
        out_ref[:, head * HD : (head + 1) * HD] = out.T.astype(BF16)


def merge(parts):
    return pl.pallas_call(
        merge_kernel,
        in_specs=[VMEM],
        out_specs=VMEM,
        out_shape=jax.ShapeDtypeStruct((TOK, 2 * HD), BF16),
        name="merge",
    )(parts)


def swap(block):
    return lax.ppermute(block, AXES, neighbours(flip_core=True))


def on_device(queries, new_kv, cache_kv, cache_len, page_owner):
    own = jnp.concatenate([cache_kv[:FILL], new_kv], axis=0)
    held = {}
    held[0, False] = own
    held[1, False] = lax.ppermute(own, AXES, neighbours(-1))
    held[-1, False] = lax.ppermute(own, AXES, neighbours(1))
    held[0, True] = lax.ppermute(own, AXES, neighbours(0, True))
    held[2, False] = lax.ppermute(own, AXES, neighbours(2))
    held[1, True] = lax.ppermute(held[0, True], AXES, neighbours(-1))
    held[-1, True] = lax.ppermute(held[0, True], AXES, neighbours(1))
    held[2, True] = lax.ppermute(held[0, True], AXES, neighbours(2))
    full = {}
    for (dx, flip_z), block in held.items():
        full[dx, flip_z, False] = block
        full[dx, flip_z, True] = swap(block)
    rounds = [
        [(0, False)],
        [(1, False), (-1, False), (0, True)],
        [(2, False), (1, True), (-1, True)],
        [(2, True)],
    ]
    qt = pl.pallas_call(
        queries_kernel,
        in_specs=[VMEM],
        out_specs=VMEM,
        out_shape=jax.ShapeDtypeStruct((2 * HD, ROWS), BF16),
        name="scaled_queries",
    )(queries)
    all_slots = list(full)
    fresh = fresh_share(all_slots, [full[s] for s in all_slots])
    state = None
    for number, group in enumerate(rounds):
        slots = [(dx, flip_z, core) for dx, flip_z in group for core in (False, True)]
        state = flash(
            slots, cache_len, qt, [full[s] for s in slots], state, fresh if number == len(rounds) - 1 else None
        )
    parts = lax.all_to_all(state, "seg", 0, 0)
    cache_out = write_pages(all_slots, cache_len, page_owner, cache_kv, [full[s] for s in all_slots])
    return merge(parts), cache_out


def solution(mesh):
    placed = (P("blk", None), P("blk", None), P(("seg", "blk"), None), P(), P())
    return jax.shard_map(
        on_device,
        mesh=mesh,
        in_specs=placed,
        out_specs=(P("blk", "seg"), P(("seg", "blk"), None)),
        check_vma=False,
    )
```

time: 492 us -> 91.2 us (0.19)
  waiting for transfers between devices: 193 us -> 11.9 us
  matrix products: 117 us -> 0 us
  other arithmetic: 78.7 us -> 0.87 us
  blocking collectives: 67.6 us -> 0 us
  Pallas kernels: 0 us -> 37.6 us
  starting transfers between devices: 0.12 us -> 25.6 us
  between operations: 14.7 us -> 1.02 us
    all_gather x3 -> x0, waiting for transfers between devices: 192 us -> none  [the longest x1 101 us: merged(): pieces = jax.tree.map(lambda part: lax.all_gather(part, axis), value)]
    dot_general x32 -> x0, matrix products: 117 us -> none  [the longest x16 59.3 us: visit_block(): jnp.dot(weights.astype(jnp.bfloat16), key_piece[:, head_dim:], preferred_...]
    all_gather x2 -> x0, blocking collectives: 67.6 us -> none  [merged(): pieces = jax.tree.map(lambda part: lax.all_gather(part, axis), value)]
    reduce_sum x20 -> x0, other arithmetic: 55.2 us -> none  [the longest x16 50.6 us: visit_block(): row_sum = row_sum * factor + jnp.sum(weights, axis=1)]
    pallas_call x0 -> x8, Pallas kernels: none -> 37.6 us  [the longest x4 27.7 us: flash(): pl.pallas_call(functools.partial(flash_kernel, slots, first, last, width)...]
    ppermute x0 -> x15, starting transfers between devices: none -> 19.8 us  [the longest x8 6.25 us: swap(): return lax.ppermute(block, AXES, neighbours(flip_core=True))]
    add x47 -> x0, other arithmetic: 15 us -> none  [the longest x7 14.6 us: combine_parts(): left[0] * left_weight[:, None] + right[0] * right_weight[:, None]]
    unnamed x12 -> x83, local copies, waits for them, and re-layouts: 1.83 us -> 12.5 us
  transfers between devices with their start and end apart: 3 -> 16, of which waited for: 3 -> 5; matrix products, arithmetic and copies ran while one was open for 3% -> 1% of each run, Pallas kernels for 0% -> 20%
where the time goes in v1:
time: 91.2 us; the launch traced here: 90.5 us
  Pallas kernels  37.6 us (41%)
  starting transfers between devices  25.6 us (28%)
  local copies, waits for them, and re-layouts  13.5 us (15%)
  waiting for transfers between devices  11.9 us (13%)
  between operations  1.02 us (1%)
    pallas_call x4, Pallas kernels, flash(): pl.pallas_call(functools.partial(flash_kernel, slots, first, last, width)...  27.7 us
    unnamed x83, local copies, waits for them, and re-layouts  12.5 us
    ppermute x8, starting transfers between devices, swap(): return lax.ppermute(block, AXES, neighbours(flip_core=True))  6.25 us
    all_to_all x1, starting transfers between devices, on_device(): parts = lax.all_to_all(state, 'seg', 0, 0)  5.81 us
    ppermute x1, starting transfers between devices, on_device(): held[0, True] = lax.ppermute(own, AXES, neighbours(0, True))  3.87 us
    ppermute x1, waiting for transfers between devices, on_device(): held[2, False] = lax.ppermute(own, AXES, neighbours(2))  3.59 us
    ppermute x1, starting transfers between devices, on_device(): held[1, True] = lax.ppermute(held[0, True], AXES, neighbours(-1))  3.44 us
    all_to_all x1, waiting for transfers between devices, on_device(): parts = lax.all_to_all(state, 'seg', 0, 0)  3.37 us
  transfers between devices with their start and end apart: 16, of which 5 were waited for; matrix products, arithmetic and copies ran while one was open for 1% of the time, Pallas kernels for 20%

profile of v1, /device:TPU:1, one launch (start us, length us, event | category | flops | bytes accessed | tf_op | source)
XLA Modules:
  0.0 90.5 jit_solution(12885989304166361916)
XLA Ops:
  0.6 1.0 %slice.3 = bf16[448,256]{1,0:T(8,128)(2,1)S(1)} slice(bf16[512,256]{1,0:T(8,128)(2,1)} %cache_ref.1), slice={[0:448], [0:256]} | slice | bytes 458752 | tf_op jit(solution)/shard_map/slice | solution.py:277
  1.6 0.0 copy-start.37
  1.6 0.9 pad_maximum_fusion.refs_0_.refs_2_
  2.5 2.1 %collective-permute-start.6 = (bf16[576,256]{1,0:T(8,128)(2,1)S(1)}, bf16[576,256]{1,0:T(8,128)(2,1)S(1)}, u32[]{:S(2)}, u32[]{:S(2)}) collective-permute-start(bf16[576,256]{1,0:T(8,128)(2,1)S(1)} %pad_maximum_fusion.refs_0_.refs_2_), channel_id=1, source_target_pairs={{0,2},{1,3},{2,4},{3,5},{4,6},{5,7},{6,0},{7,1},{8,10},{9,11},{10,... | collective-permute-start | bytes 884744 | tf_op jit(solution)/shard_map/ppermute | solution.py:281
  4.6 1.3 %collective-permute-start.4 = (bf16[576,256]{1,0:T(8,128)(2,1)S(1)}, bf16[576,256]{1,0:T(8,128)(2,1)S(1)}, u32[]{:S(2)}, u32[]{:S(2)}) collective-permute-start(bf16[576,256]{1,0:T(8,128)(2,1)S(1)} %pad_maximum_fusion.refs_0_.refs_2_), channel_id=1, source_target_pairs={{0,6},{1,7},{2,0},{3,1},{4,2},{5,3},{6,4},{7,5},{8,14},{9,15},{10,... | collective-permute-start | bytes 884744 | tf_op jit(solution)/shard_map/ppermute | solution.py:280
  5.9 3.9 %collective-permute-start = (bf16[576,256]{1,0:T(8,128)(2,1)S(1)}, bf16[576,256]{1,0:T(8,128)(2,1)S(1)}, u32[]{:S(2)}, u32[]{:S(2)}) collective-permute-start(bf16[576,256]{1,0:T(8,128)(2,1)S(1)} %pad_maximum_fusion.refs_0_.refs_2_), channel_id=1, source_target_pairs={{0,24},{1,25},{2,26},{3,27},{4,28},{5,29},{6,30},{7,31},{8,16},{9,... | collective-permute-start | bytes 884744 | tf_op jit(solution)/shard_map/ppermute | solution.py:282
  9.8 1.5 %collective-permute-start.9 = (bf16[576,256]{1,0:T(8,128)(2,1)S(1)}, bf16[576,256]{1,0:T(8,128)(2,1)}, u32[]{:S(2)}, u32[]{:S(2)}) collective-permute-start(bf16[576,256]{1,0:T(8,128)(2,1)S(1)} %pad_maximum_fusion.refs_0_.refs_2_), channel_id=1, source_target_pairs={{0,4},{1,5},{2,6},{3,7},{4,0},{5,1},{6,2},{7,3},{8,12},{9,13},{10,... | collective-permute-start | bytes 884744 | tf_op jit(solution)/shard_map/ppermute | solution.py:283
  11.3 1.8 %collective-permute-start.3 = (bf16[576,256]{1,0:T(8,128)(2,1)S(1)}, bf16[576,256]{1,0:T(8,128)(2,1)S(1)}, u32[]{:S(2)}, u32[]{:S(2)}) collective-permute-start(bf16[576,256]{1,0:T(8,128)(2,1)S(1)} %pad_maximum_fusion.refs_0_.refs_2_), channel_id=1, source_target_pairs={{0,1},{1,0},{2,3},{3,2},{4,5},{5,4},{6,7},{7,6},{8,9},{9,8},{10,11... | collective-permute-start | bytes 884744 | tf_op jit(solution)/shard_map/ppermute | solution.py:273
  13.1 0.7 collective-permute-start.7
  13.8 0.8 collective-permute-start.5
  14.7 1.2 %collective-permute-done.refs_6_ = bf16[576,256]{1,0:T(8,128)(2,1)S(1)} collective-permute-done((bf16[576,256]{1,0:T(8,128)(2,1)S(1)}, bf16[576,256]{1,0:T(8,128)(2,1)S(1)}, u32[]{:S(2)}, u32[]{:S(2)}) %collective-permute-start) | collective-permute-done | bytes 294944 | tf_op jit(solution)/shard_map/ppermute | solution.py:282
  15.9 0.1 collective-permute-start.13
  16.0 3.6 %collective-permute-done.9.refs_8_.refs_2_ = bf16[576,256]{1,0:T(8,128)(2,1)} collective-permute-done((bf16[576,256]{1,0:T(8,128)(2,1)S(1)}, bf16[576,256]{1,0:T(8,128)(2,1)}, u32[]{:S(2)}, u32[]{:S(2)}) %collective-permute-start.9) | collective-permute-done | bytes 294944 | tf_op jit(solution)/shard_map/ppermute | solution.py:283
  19.6 3.4 %collective-permute-start.11 = (bf16[576,256]{1,0:T(8,128)(2,1)S(1)}, bf16[576,256]{1,0:T(8,128)(2,1)}, u32[]{:S(2)}, u32[]{:S(2)}) collective-permute-start(bf16[576,256]{1,0:T(8,128)(2,1)S(1)} %collective-permute-done.refs_6_), channel_id=1, source_target_pairs={{0,6},{1,7},{2,0},{3,1},{4,2},{5,3},{6,4},{7,5},{8,14},{9,15},{10,... | collective-permute-start | bytes 884744 | tf_op jit(solution)/shard_map/ppermute | solution.py:284
  23.0 1.2 %collective-permute-start.1 = (bf16[576,256]{1,0:T(8,128)(2,1)S(1)}, bf16[576,256]{1,0:T(8,128)(2,1)S(1)}, u32[]{:S(2)}, u32[]{:S(2)}) collective-permute-start(bf16[576,256]{1,0:T(8,128)(2,1)S(1)} %collective-permute-done.refs_6_), channel_id=1, source_target_pairs={{0,4},{1,5},{2,6},{3,7},{4,0},{5,1},{6,2},{7,3},{8,12},{9,13},{10,... | collective-permute-start | bytes 884744 | tf_op jit(solution)/shard_map/ppermute | solution.py:286
  24.2 0.6 collective-permute-start.8
  24.8 2.3 %scaled_queries.1.refs_1_ = bf16[256,2048]{1,0:T(8,128)(2,1)} custom-call(bf16[128,2048]{1,0:T(8,128)(2,1)} %q_ref.1), custom_call_target="tpu_custom_call" | custom-call | tf_op jit(solution)/shard_map/scaled_queries/pallas_call | solution.py:297
  27.2 1.2 %copy-done.30 = bf16[256,2048]{1,0:T(8,128)(2,1)S(1)} copy-done((bf16[256,2048]{1,0:T(8,128)(2,1)S(1)}, bf16[256,2048]{1,0:T(8,128)(2,1)}, u32[]{:S(2)}) %copy-start.30) | copy-done | bytes 1048600
  28.4 3.9 %flash_2.2 = (f32[8,2048]{1,0:T(8,128)S(1)}, f32[144,2048]{1,0:T(8,128)S(1)}) custom-call(s32[128]{0:T(128)S(1)} %copy-done.37, bf16[256,2048]{1,0:T(8,128)(2,1)S(1)} %copy-done.30, bf16[576,256]{1,0:T(8,128)(2,1)S(1)} %pad_maximum_fusion.refs_0_.refs_2_, bf16[576,256]{1,0:T(8,128)(2,1)S(1)} %collective-permute-done.3.refs_1_.refs_3_), custom_call_target="tpu_custom_call" | custom-call | flops 1879048192 | bytes 1048576 | tf_op jit(solution)/shard_map/flash_2/pallas_call | solution.py:164
  32.3 0.2 collective-permute-start.10
  32.5 0.4 collective-permute-start.14
  32.9 2.7 %collective-permute-done.11.refs_10_.refs_4_ = bf16[576,256]{1,0:T(8,128)(2,1)} collective-permute-done((bf16[576,256]{1,0:T(8,128)(2,1)S(1)}, bf16[576,256]{1,0:T(8,128)(2,1)}, u32[]{:S(2)}, u32[]{:S(2)}) %collective-permute-start.11) | collective-permute-done | bytes 294944 | tf_op jit(solution)/shard_map/ppermute | solution.py:284
  35.7 0.9 collective-permute-start.12
  36.5 1.0 %collective-permute-done.1.refs_14_.refs_2_ = bf16[576,256]{1,0:T(8,128)(2,1)S(1)} collective-permute-done((bf16[576,256]{1,0:T(8,128)(2,1)S(1)}, bf16[576,256]{1,0:T(8,128)(2,1)S(1)}, u32[]{:S(2)}, u32[]{:S(2)}) %collective-permute-start.1) | collective-permute-done | bytes 294944 | tf_op jit(solution)/shard_map/ppermute | solution.py:286
  37.5 0.9 collective-permute-start.2
  38.4 9.2 %flash_6.2 = (f32[8,2048]{1,0:T(8,128)S(1)}, f32[144,2048]{1,0:T(8,128)S(1)}) custom-call(s32[128]{0:T(128)S(1)} %copy-done.37, bf16[256,2048]{1,0:T(8,128)(2,1)S(1)} %copy-done.30, bf16[576,256]{1,0:T(8,128)(2,1)S(1)} %collective-permute-done.4.refs_2_, bf16[576,256]{1,0:T(8,128)(2,1)S(1)} %collective-permute-done.5.refs_3_, ...), custom_call_target="tpu_custom_call" | custom-call | flops 5637144576 | bytes 1048576 | tf_op jit(solution)/shard_map/flash_6/pallas_call | solution.py:164
  47.6 1.0 %copy-done.38 = f32[144,2048]{1,0:T(8,128)} copy-done((f32[144,2048]{1,0:T(8,128)}, f32[144,2048]{1,0:T(8,128)S(1)}, u32[]{:S(2)}) %copy-start.38) | copy-done | bytes 1179672
  48.7 0.7 copy-done.18
  49.4 0.1 copy-done.21
  49.5 0.1 copy-done.24
  49.6 0.7 copy-done.27
  50.3 3.0 %fresh_share.1.refs_4_ = bf16[256,256]{1,0:T(8,128)(2,1)} custom-call(bf16[576,256]{1,0:T(8,128)(2,1)} %copy-done, bf16[576,256]{1,0:T(8,128)(2,1)} %copy-done.8, bf16[576,256]{1,0:T(8,128)(2,1)} %copy-done.4, bf16[576,256]{1,0:T(8,128)(2,1)} %copy-done.12, bf16[576,256]{1,0:T(8,128)(2,1)} %copy-done.2, bf16[576,256]{1,0:T(8,128)(2,1)} %copy-done.10, ...), custom_call_target="tpu_custom_call" | custom-call | tf_op jit(solution)/shard_map/fresh_share/pallas_call | solution.py:236
  53.2 1.0 %copy-done.19 = bf16[576,256]{1,0:T(8,128)(2,1)S(1)} copy-done((bf16[576,256]{1,0:T(8,128)(2,1)S(1)}, bf16[576,256]{1,0:T(8,128)(2,1)}, u32[]{:S(2)}) %copy-start.19) | copy-done | bytes 294936
  54.2 1.0 %copy-done.22 = bf16[576,256]{1,0:T(8,128)(2,1)S(1)} copy-done((bf16[576,256]{1,0:T(8,128)(2,1)S(1)}, bf16[576,256]{1,0:T(8,128)(2,1)}, u32[]{:S(2)}) %copy-start.22) | copy-done | bytes 294936
  55.2 1.0 %copy-done.25 = bf16[576,256]{1,0:T(8,128)(2,1)S(1)} copy-done((bf16[576,256]{1,0:T(8,128)(2,1)S(1)}, bf16[576,256]{1,0:T(8,128)(2,1)}, u32[]{:S(2)}) %copy-start.25) | copy-done | bytes 294936
  56.1 1.3 %copy-done.39 = f32[144,2048]{1,0:T(8,128)S(1)} copy-done((f32[144,2048]{1,0:T(8,128)S(1)}, f32[144,2048]{1,0:T(8,128)}, u32[]{:S(2)}) %copy-start.39) | copy-done | bytes 1179672
  57.4 10.1 %flash_6.3 = (f32[8,2048]{1,0:T(8,128)S(1)}, f32[144,2048]{1,0:T(8,128)S(1)}) custom-call(s32[128]{0:T(128)S(1)} %copy-done.37, bf16[256,2048]{1,0:T(8,128)(2,1)S(1)} %copy-done.31, bf16[576,256]{1,0:T(8,128)(2,1)} %collective-permute-done.9.refs_8_.refs_2_, bf16[576,256]{1,0:T(8,128)(2,1)S(1)} %copy-done.19, ...), custom_call_target="tpu_custom_call" | custom-call | flops 5637144576 | bytes 1048576 | tf_op jit(solution)/shard_map/flash_6/pallas_call | solution.py:164
  67.6 0.0 copy-start.40
  67.6 4.6 %flash_2.3 = bf16[8,272,128]{2,1,0:T(8,128)(2,1)S(1)} custom-call(s32[128]{0:T(128)S(1)} %copy-done.37, bf16[256,2048]{1,0:T(8,128)(2,1)S(1)} %copy-done.32, bf16[576,256]{1,0:T(8,128)(2,1)S(1)} %copy-done.15, bf16[576,256]{1,0:T(8,128)(2,1)S(1)} %copy-done.28, bf16[256,256]{1,0:T(8,128)(2,1)S(1)} %copy-done.36, f32[8,2048]{1,0:T(8,128)S(1)} %get-tuple-element.12.refs_5_, ...), custom_call_target="tpu_custom_call" | custom-call | flops 2415919104 | bytes 1048576 | tf_op jit(solution)/shard_map/flash_2/pallas_call | solution.py:164
  72.2 0.8 copy-done.34
  73.1 5.8 %all-to-all-start = ((bf16[8,272,128]{2,1,0:T(8,128)(2,1)}), bf16[8,272,128]{2,1,0:T(8,128)(2,1)}, u32[]{:S(2)}, u32[]{:S(2)}) async-start(bf16[8,272,128]{2,1,0:T(8,128)(2,1)} %copy-done.34), calls=%async_computation | async-start | bytes 1114112 | tf_op jit(solution)/shard_map/all_to_all | solution.py:312
  78.9 0.8 copy.7.owner_ref
  79.8 1.0 %copy-done.29 = bf16[576,256]{1,0:T(8,128)(2,1)S(1)} copy-done((bf16[576,256]{1,0:T(8,128)(2,1)S(1)}, bf16[576,256]{1,0:T(8,128)(2,1)}, u32[]{:S(2)}) %copy-start.29) | copy-done | bytes 294936
  80.7 0.9 %copy-done.33 = bf16[512,256]{1,0:T(8,128)(2,1)S(1)} copy-done((bf16[512,256]{1,0:T(8,128)(2,1)S(1)}, bf16[512,256]{1,0:T(8,128)(2,1)}, u32[]{:S(2)}) %copy-start.33) | copy-done | bytes 262168
  81.7 0.9 copy-done.35
  82.6 2.7 %write_pages.1 = bf16[512,256]{1,0:T(8,128)(2,1)} custom-call(s32[128]{0:T(128)S(1)} %copy-done.37, s32[256,1]{1,0:T(8,128)S(1)} %copy-done.35, bf16[512,256]{1,0:T(8,128)(2,1)S(1)} %copy-done.33, bf16[576,256]{1,0:T(8,128)(2,1)S(1)} %copy-done.1, bf16[576,256]{1,0:T(8,128)(2,1)S(1)} %copy-done.9, bf16[576,256]{1,0:T(8,128)(2,1)S(1)} %copy-done.5, ...), custom_call_target="tpu_custom_call" | custom-call | flops 1000000000 | bytes 4194304 | tf_op jit(solution)/shard_map/write_pages/pallas_call | solution.py:215
  85.3 3.4 %all-to-all-done.parts_ref = bf16[8,272,128]{2,1,0:T(8,128)(2,1)} async-done(((bf16[8,272,128]{2,1,0:T(8,128)(2,1)}), bf16[8,272,128]{2,1,0:T(8,128)(2,1)}, u32[]{:S(2)}, u32[]{:S(2)}) %all-to-all-start) | async-done | bytes 557088 | tf_op jit(solution)/shard_map/all_to_all | solution.py:312
  88.6 1.9 %merge.1 = bf16[128,256]{1,0:T(8,128)(2,1)} custom-call(bf16[8,272,128]{2,1,0:T(8,128)(2,1)} %all-to-all-done.parts_ref), custom_call_target="tpu_custom_call" | custom-call | tf_op jit(solution)/shard_map/merge/pallas_call | solution.py:263
  (77 shorter events, 0.2 us)
Async XLA Ops:
  1.6 25.6 %copy-start.37 = (s32[128]{0:T(128)S(1)}, s32[128]{0:T(128)}, u32[]{:S(2)}) copy-start(s32[128]{0:T(128)} %len_ref.1) | copy-start | bytes 1540
  2.5 29.8 %copy-start = (bf16[576,256]{1,0:T(8,128)(2,1)}, bf16[576,256]{1,0:T(8,128)(2,1)S(1)}, u32[]{:S(2)}) copy-start(bf16[576,256]{1,0:T(8,128)(2,1)S(1)} %pad_maximum_fusion.refs_0_.refs_2_) | copy-start | bytes 884740
  2.5 10.7 %collective-permute-start.6 = (bf16[576,256]{1,0:T(8,128)(2,1)S(1)}, bf16[576,256]{1,0:T(8,128)(2,1)S(1)}, u32[]{:S(2)}, u32[]{:S(2)}) collective-permute-start(bf16[576,256]{1,0:T(8,128)(2,1)S(1)} %pad_maximum_fusion.refs_0_.refs_2_), channel_id=1, source_target_pairs={{0,2},{1,3},{2,4},{3,5},{4,6},{5,7},{6,0},{7,1},{8,10},{9,11},{10,... | collective-permute-start | bytes 884744 | tf_op jit(solution)/shard_map/ppermute | solution.py:281
  4.6 9.2 %collective-permute-start.4 = (bf16[576,256]{1,0:T(8,128)(2,1)S(1)}, bf16[576,256]{1,0:T(8,128)(2,1)S(1)}, u32[]{:S(2)}, u32[]{:S(2)}) collective-permute-start(bf16[576,256]{1,0:T(8,128)(2,1)S(1)} %pad_maximum_fusion.refs_0_.refs_2_), channel_id=1, source_target_pairs={{0,6},{1,7},{2,0},{3,1},{4,2},{5,3},{6,4},{7,5},{8,14},{9,15},{10,... | collective-permute-start | bytes 884744 | tf_op jit(solution)/shard_map/ppermute | solution.py:280
  5.9 10.0 %collective-permute-start = (bf16[576,256]{1,0:T(8,128)(2,1)S(1)}, bf16[576,256]{1,0:T(8,128)(2,1)S(1)}, u32[]{:S(2)}, u32[]{:S(2)}) collective-permute-start(bf16[576,256]{1,0:T(8,128)(2,1)S(1)} %pad_maximum_fusion.refs_0_.refs_2_), channel_id=1, source_target_pairs={{0,24},{1,25},{2,26},{3,27},{4,28},{5,29},{6,30},{7,31},{8,16},{9,... | collective-permute-start | bytes 884744 | tf_op jit(solution)/shard_map/ppermute | solution.py:282
  9.8 9.7 %collective-permute-start.9 = (bf16[576,256]{1,0:T(8,128)(2,1)S(1)}, bf16[576,256]{1,0:T(8,128)(2,1)}, u32[]{:S(2)}, u32[]{:S(2)}) collective-permute-start(bf16[576,256]{1,0:T(8,128)(2,1)S(1)} %pad_maximum_fusion.refs_0_.refs_2_), channel_id=1, source_target_pairs={{0,4},{1,5},{2,6},{3,7},{4,0},{5,1},{6,2},{7,3},{8,12},{9,13},{10,... | collective-permute-start | bytes 884744 | tf_op jit(solution)/shard_map/ppermute | solution.py:283
  11.3 11.7 %collective-permute-start.3 = (bf16[576,256]{1,0:T(8,128)(2,1)S(1)}, bf16[576,256]{1,0:T(8,128)(2,1)S(1)}, u32[]{:S(2)}, u32[]{:S(2)}) collective-permute-start(bf16[576,256]{1,0:T(8,128)(2,1)S(1)} %pad_maximum_fusion.refs_0_.refs_2_), channel_id=1, source_target_pairs={{0,1},{1,0},{2,3},{3,2},{4,5},{5,4},{6,7},{7,6},{8,9},{9,8},{10,11... | collective-permute-start | bytes 884744 | tf_op jit(solution)/shard_map/ppermute | solution.py:273
  13.1 25.2 %copy-start.2 = (bf16[576,256]{1,0:T(8,128)(2,1)}, bf16[576,256]{1,0:T(8,128)(2,1)S(1)}, u32[]{:S(2)}) copy-start(bf16[576,256]{1,0:T(8,128)(2,1)S(1)} %collective-permute-done.6.refs_4_) | copy-start | bytes 884740
  13.1 11.1 %collective-permute-start.7 = (bf16[576,256]{1,0:T(8,128)(2,1)S(1)}, bf16[576,256]{1,0:T(8,128)(2,1)S(1)}, u32[]{:S(2)}, u32[]{:S(2)}) collective-permute-start(bf16[576,256]{1,0:T(8,128)(2,1)S(1)} %collective-permute-done.6.refs_4_), channel_id=1, source_target_pairs={{0,1},{1,0},{2,3},{3,2},{4,5},{5,4},{6,7},{7,6},{8,9},{9,8},{10,11... | collective-permute-start | bytes 884744 | tf_op jit(solution)/shard_map/ppermute | solution.py:273
  13.8 24.6 %copy-start.4 = (bf16[576,256]{1,0:T(8,128)(2,1)}, bf16[576,256]{1,0:T(8,128)(2,1)S(1)}, u32[]{:S(2)}) copy-start(bf16[576,256]{1,0:T(8,128)(2,1)S(1)} %collective-permute-done.4.refs_2_) | copy-start | bytes 884740
  13.8 18.5 %collective-permute-start.5 = (bf16[576,256]{1,0:T(8,128)(2,1)S(1)}, bf16[576,256]{1,0:T(8,128)(2,1)S(1)}, u32[]{:S(2)}, u32[]{:S(2)}) collective-permute-start(bf16[576,256]{1,0:T(8,128)(2,1)S(1)} %collective-permute-done.4.refs_2_), channel_id=1, source_target_pairs={{0,1},{1,0},{2,3},{3,2},{4,5},{5,4},{6,7},{7,6},{8,9},{9,8},{10,11... | collective-permute-start | bytes 884744 | tf_op jit(solution)/shard_map/ppermute | solution.py:273
  15.9 22.5 %copy-start.6 = (bf16[576,256]{1,0:T(8,128)(2,1)}, bf16[576,256]{1,0:T(8,128)(2,1)S(1)}, u32[]{:S(2)}) copy-start(bf16[576,256]{1,0:T(8,128)(2,1)S(1)} %collective-permute-done.refs_6_) | copy-start | bytes 884740
  15.9 16.6 %collective-permute-start.13 = (bf16[576,256]{1,0:T(8,128)(2,1)S(1)}, bf16[576,256]{1,0:T(8,128)(2,1)}, u32[]{:S(2)}, u32[]{:S(2)}) collective-permute-start(bf16[576,256]{1,0:T(8,128)(2,1)S(1)} %collective-permute-done.refs_6_), channel_id=1, source_target_pairs={{0,2},{1,3},{2,4},{3,5},{4,6},{5,7},{6,0},{7,1},{8,10},{9,11},{10,... | collective-permute-start | bytes 884744 | tf_op jit(solution)/shard_map/ppermute | solution.py:285
  19.6 16.1 %collective-permute-start.11 = (bf16[576,256]{1,0:T(8,128)(2,1)S(1)}, bf16[576,256]{1,0:T(8,128)(2,1)}, u32[]{:S(2)}, u32[]{:S(2)}) collective-permute-start(bf16[576,256]{1,0:T(8,128)(2,1)S(1)} %collective-permute-done.refs_6_), channel_id=1, source_target_pairs={{0,6},{1,7},{2,0},{3,1},{4,2},{5,3},{6,4},{7,5},{8,14},{9,15},{10,... | collective-permute-start | bytes 884744 | tf_op jit(solution)/shard_map/ppermute | solution.py:284
  23.0 9.3 %copy-start.8 = (bf16[576,256]{1,0:T(8,128)(2,1)}, bf16[576,256]{1,0:T(8,128)(2,1)S(1)}, u32[]{:S(2)}) copy-start(bf16[576,256]{1,0:T(8,128)(2,1)S(1)} %collective-permute-done.3.refs_1_.refs_3_) | copy-start | bytes 884740
  23.0 14.5 %collective-permute-start.1 = (bf16[576,256]{1,0:T(8,128)(2,1)S(1)}, bf16[576,256]{1,0:T(8,128)(2,1)S(1)}, u32[]{:S(2)}, u32[]{:S(2)}) collective-permute-start(bf16[576,256]{1,0:T(8,128)(2,1)S(1)} %collective-permute-done.refs_6_), channel_id=1, source_target_pairs={{0,4},{1,5},{2,6},{3,7},{4,0},{5,1},{6,2},{7,3},{8,12},{9,13},{10,... | collective-permute-start | bytes 884744 | tf_op jit(solution)/shard_map/ppermute | solution.py:286
  24.2 14.2 %copy-start.10 = (bf16[576,256]{1,0:T(8,128)(2,1)}, bf16[576,256]{1,0:T(8,128)(2,1)S(1)}, u32[]{:S(2)}) copy-start(bf16[576,256]{1,0:T(8,128)(2,1)S(1)} %collective-permute-done.7.refs_5_) | copy-start | bytes 884740
  24.2 14.2 %collective-permute-start.8 = (bf16[576,256]{1,0:T(8,128)(2,1)S(1)}, bf16[576,256]{1,0:T(8,128)(2,1)S(1)}, u32[]{:S(2)}, u32[]{:S(2)}) collective-permute-start(bf16[576,256]{1,0:T(8,128)(2,1)S(1)} %collective-permute-done.refs_6_), channel_id=1, source_target_pairs={{0,1},{1,0},{2,3},{3,2},{4,5},{5,4},{6,7},{7,6},{8,9},{9,8},{10,11... | collective-permute-start | bytes 884744 | tf_op jit(solution)/shard_map/ppermute | solution.py:273
  27.2 1.2 %copy-start.30 = (bf16[256,2048]{1,0:T(8,128)(2,1)S(1)}, bf16[256,2048]{1,0:T(8,128)(2,1)}, u32[]{:S(2)}) copy-start(bf16[256,2048]{1,0:T(8,128)(2,1)} %scaled_queries.1.refs_1_) | copy-start | bytes 3145732
  32.3 15.2 %copy-start.12 = (bf16[576,256]{1,0:T(8,128)(2,1)}, bf16[576,256]{1,0:T(8,128)(2,1)S(1)}, u32[]{:S(2)}) copy-start(bf16[576,256]{1,0:T(8,128)(2,1)S(1)} %collective-permute-done.5.refs_3_) | copy-start | bytes 884740
  32.3 16.3 %collective-permute-start.10 = (bf16[576,256]{1,0:T(8,128)(2,1)}, bf16[576,256]{1,0:T(8,128)(2,1)S(1)}, u32[]{:S(2)}, u32[]{:S(2)}) collective-permute-start(bf16[576,256]{1,0:T(8,128)(2,1)} %collective-permute-done.9.refs_8_.refs_2_), channel_id=1, source_target_pairs={{0,1},{1,0},{2,3},{3,2},{4,5},{5,4},{6,7},{7,6},{8,9},{9,8},{10,11... | collective-permute-start | bytes 884744 | tf_op jit(solution)/shard_map/ppermute | solution.py:273
  32.5 16.1 %collective-permute-start.14 = (bf16[576,256]{1,0:T(8,128)(2,1)}, bf16[576,256]{1,0:T(8,128)(2,1)S(1)}, u32[]{:S(2)}, u32[]{:S(2)}) collective-permute-start(bf16[576,256]{1,0:T(8,128)(2,1)} %collective-permute-done.13.refs_12_.refs_6_), channel_id=1, source_target_pairs={{0,1},{1,0},{2,3},{3,2},{4,5},{5,4},{6,7},{7,6},{8,9},{9,8},{10,11... | collective-permute-start | bytes 884744 | tf_op jit(solution)/shard_map/ppermute | solution.py:273
  35.7 13.0 %collective-permute-start.12 = (bf16[576,256]{1,0:T(8,128)(2,1)}, bf16[576,256]{1,0:T(8,128)(2,1)S(1)}, u32[]{:S(2)}, u32[]{:S(2)}) collective-permute-start(bf16[576,256]{1,0:T(8,128)(2,1)} %collective-permute-done.11.refs_10_.refs_4_), channel_id=1, source_target_pairs={{0,1},{1,0},{2,3},{3,2},{4,5},{5,4},{6,7},{7,6},{8,9},{9,8},{10,11... | collective-permute-start | bytes 884744 | tf_op jit(solution)/shard_map/ppermute | solution.py:273
  37.5 10.1 %copy-start.14 = (bf16[576,256]{1,0:T(8,128)(2,1)}, bf16[576,256]{1,0:T(8,128)(2,1)S(1)}, u32[]{:S(2)}) copy-start(bf16[576,256]{1,0:T(8,128)(2,1)S(1)} %collective-permute-done.1.refs_14_.refs_2_) | copy-start | bytes 884740
  37.5 11.2 %collective-permute-start.2 = (bf16[576,256]{1,0:T(8,128)(2,1)S(1)}, bf16[576,256]{1,0:T(8,128)(2,1)S(1)}, u32[]{:S(2)}, u32[]{:S(2)}) collective-permute-start(bf16[576,256]{1,0:T(8,128)(2,1)S(1)} %collective-permute-done.1.refs_14_.refs_2_), channel_id=1, source_target_pairs={{0,1},{1,0},{2,3},{3,2},{4,5},{5,4},{6,7},{7,6},{8,9},{9,8},{10,11... | collective-permute-start | bytes 884744 | tf_op jit(solution)/shard_map/ppermute | solution.py:273
  38.4 9.2 %copy-start.16 = (bf16[576,256]{1,0:T(8,128)(2,1)}, bf16[576,256]{1,0:T(8,128)(2,1)S(1)}, u32[]{:S(2)}) copy-start(bf16[576,256]{1,0:T(8,128)(2,1)S(1)} %collective-permute-done.8.refs_7_) | copy-start | bytes 884740
  47.6 1.0 %copy-start.38 = (f32[144,2048]{1,0:T(8,128)}, f32[144,2048]{1,0:T(8,128)S(1)}, u32[]{:S(2)}) copy-start(f32[144,2048]{1,0:T(8,128)S(1)} %get-tuple-element.11.refs_9_) | copy-start | bytes 3538948
  48.7 4.6 %copy-start.31 = (bf16[256,2048]{1,0:T(8,128)(2,1)S(1)}, bf16[256,2048]{1,0:T(8,128)(2,1)}, u32[]{:S(2)}) copy-start(bf16[256,2048]{1,0:T(8,128)(2,1)} %scaled_queries.1.refs_1_) | copy-start | bytes 3145732
  53.2 1.0 %copy-start.19 = (bf16[576,256]{1,0:T(8,128)(2,1)S(1)}, bf16[576,256]{1,0:T(8,128)(2,1)}, u32[]{:S(2)}) copy-start(bf16[576,256]{1,0:T(8,128)(2,1)} %copy-done.18) | copy-start | bytes 884740
  56.1 1.3 %copy-start.39 = (f32[144,2048]{1,0:T(8,128)S(1)}, f32[144,2048]{1,0:T(8,128)}, u32[]{:S(2)}) copy-start(f32[144,2048]{1,0:T(8,128)} %copy-done.38) | copy-start | bytes 3538948
  57.4 10.1 %copy-start.15 = (bf16[576,256]{1,0:T(8,128)(2,1)S(1)}, bf16[576,256]{1,0:T(8,128)(2,1)}, u32[]{:S(2)}) copy-start(bf16[576,256]{1,0:T(8,128)(2,1)} %copy-done.14) | copy-start | bytes 884740
  57.4 10.1 %copy-start.28 = (bf16[576,256]{1,0:T(8,128)(2,1)S(1)}, bf16[576,256]{1,0:T(8,128)(2,1)}, u32[]{:S(2)}) copy-start(bf16[576,256]{1,0:T(8,128)(2,1)} %copy-done.27) | copy-start | bytes 884740
  57.4 10.1 %copy-start.32 = (bf16[256,2048]{1,0:T(8,128)(2,1)S(1)}, bf16[256,2048]{1,0:T(8,128)(2,1)}, u32[]{:S(2)}) copy-start(bf16[256,2048]{1,0:T(8,128)(2,1)} %scaled_queries.1.refs_1_) | copy-start | bytes 3145732
  57.4 10.1 %copy-start.36 = (bf16[256,256]{1,0:T(8,128)(2,1)S(1)}, bf16[256,256]{1,0:T(8,128)(2,1)}, u32[]{:S(2)}) copy-start(bf16[256,256]{1,0:T(8,128)(2,1)} %fresh_share.1.refs_4_) | copy-start | bytes 393220
  67.6 11.3 %copy-start.40 = (s32[256,1]{0,1:T(1,128)S(1)}, s32[256,1]{0,1:T(1,128)}, u32[]{:S(2)}) copy-start(s32[256,1]{0,1:T(1,128)} %param.9) | copy-start | bytes 3076
  67.6 12.1 %copy-start.9 = (bf16[576,256]{1,0:T(8,128)(2,1)S(1)}, bf16[576,256]{1,0:T(8,128)(2,1)}, u32[]{:S(2)}) copy-start(bf16[576,256]{1,0:T(8,128)(2,1)} %copy-done.8) | copy-start | bytes 884740
  67.6 12.1 %copy-start.11 = (bf16[576,256]{1,0:T(8,128)(2,1)S(1)}, bf16[576,256]{1,0:T(8,128)(2,1)}, u32[]{:S(2)}) copy-start(bf16[576,256]{1,0:T(8,128)(2,1)} %copy-done.10) | copy-start | bytes 884740
  67.6 12.1 %copy-start.13 = (bf16[576,256]{1,0:T(8,128)(2,1)S(1)}, bf16[576,256]{1,0:T(8,128)(2,1)}, u32[]{:S(2)}) copy-start(bf16[576,256]{1,0:T(8,128)(2,1)} %copy-done.12) | copy-start | bytes 884740
  67.6 12.1 %copy-start.17 = (bf16[576,256]{1,0:T(8,128)(2,1)S(1)}, bf16[576,256]{1,0:T(8,128)(2,1)}, u32[]{:S(2)}) copy-start(bf16[576,256]{1,0:T(8,128)(2,1)} %copy-done.16) | copy-start | bytes 884740
  67.6 12.1 %copy-start.20 = (bf16[576,256]{1,0:T(8,128)(2,1)S(1)}, bf16[576,256]{1,0:T(8,128)(2,1)}, u32[]{:S(2)}) copy-start(bf16[576,256]{1,0:T(8,128)(2,1)} %copy-done.18) | copy-start | bytes 884740
  67.6 12.1 %copy-start.23 = (bf16[576,256]{1,0:T(8,128)(2,1)S(1)}, bf16[576,256]{1,0:T(8,128)(2,1)}, u32[]{:S(2)}) copy-start(bf16[576,256]{1,0:T(8,128)(2,1)} %copy-done.21) | copy-start | bytes 884740
  67.6 12.1 %copy-start.26 = (bf16[576,256]{1,0:T(8,128)(2,1)S(1)}, bf16[576,256]{1,0:T(8,128)(2,1)}, u32[]{:S(2)}) copy-start(bf16[576,256]{1,0:T(8,128)(2,1)} %copy-done.24) | copy-start | bytes 884740
  73.0 6.7 %copy-start.1 = (bf16[576,256]{1,0:T(8,128)(2,1)S(1)}, bf16[576,256]{1,0:T(8,128)(2,1)}, u32[]{:S(2)}) copy-start(bf16[576,256]{1,0:T(8,128)(2,1)} %copy-done) | copy-start | bytes 884740
  73.1 6.7 %copy-start.3 = (bf16[576,256]{1,0:T(8,128)(2,1)S(1)}, bf16[576,256]{1,0:T(8,128)(2,1)}, u32[]{:S(2)}) copy-start(bf16[576,256]{1,0:T(8,128)(2,1)} %copy-done.2) | copy-start | bytes 884740
  73.1 6.7 %copy-start.5 = (bf16[576,256]{1,0:T(8,128)(2,1)S(1)}, bf16[576,256]{1,0:T(8,128)(2,1)}, u32[]{:S(2)}) copy-start(bf16[576,256]{1,0:T(8,128)(2,1)} %copy-done.4) | copy-start | bytes 884740
  73.1 6.7 %copy-start.7 = (bf16[576,256]{1,0:T(8,128)(2,1)S(1)}, bf16[576,256]{1,0:T(8,128)(2,1)}, u32[]{:S(2)}) copy-start(bf16[576,256]{1,0:T(8,128)(2,1)} %copy-done.6) | copy-start | bytes 884740
  73.1 15.6 %all-to-all-start = ((bf16[8,272,128]{2,1,0:T(8,128)(2,1)}), bf16[8,272,128]{2,1,0:T(8,128)(2,1)}, u32[]{:S(2)}, u32[]{:S(2)}) async-start(bf16[8,272,128]{2,1,0:T(8,128)(2,1)} %copy-done.34), calls=%async_computation | async-start | bytes 1114112 | tf_op jit(solution)/shard_map/all_to_all | solution.py:312
  79.8 1.0 %copy-start.29 = (bf16[576,256]{1,0:T(8,128)(2,1)S(1)}, bf16[576,256]{1,0:T(8,128)(2,1)}, u32[]{:S(2)}) copy-start(bf16[576,256]{1,0:T(8,128)(2,1)} %copy-done.27) | copy-start | bytes 884740
  (9 other events, 7.7 us)

commit v2 on v1

v2 whole, which is shorter than its diff:
```python
import functools

import jax
import jax.numpy as jnp
from jax import lax
from jax.experimental import pallas as pl
from jax.experimental.pallas import tpu as pltpu
from jax.sharding import PartitionSpec as P


F32 = jnp.float32
BF16 = jnp.bfloat16
HEADS = 16
HD = 128
TOK = 128
ROWS = 2 * HEADS * TOK
PART = HEADS * TOK
SLOTS = 512
FILL = 448
PAGE = 8
NSEG = 8
NBLK = 16
SHARE = TOK // NSEG
CHUNK = 2 * HD + 32
ACC = HD + 16
NEG = -1e30
SCALE = 1.4426950408889634 / HD**0.5
VMEM = pl.BlockSpec(memory_space=pltpu.VMEM)
SMEM = pl.BlockSpec(memory_space=pltpu.SMEM)
AXES = ("seg", "blk")


def neighbours(dx=0, flip_z=False, flip_core=False):
    pairs = []
    for here in range(NSEG * NBLK):
        seg, blk = divmod(here, NBLK)
        pairs.append((here, device_at(seg, blk, dx, flip_z, flip_core)))
    return pairs


def device_at(seg, blk, dx, flip_z, flip_core):
    y, z_lo = seg // 2, seg % 2
    z_hi, x, core = blk // 8, (blk // 2) % 4, blk % 2
    if flip_z:
        z_lo, z_hi = 1 - z_lo, 1 - z_hi
    if flip_core:
        core = 1 - core
    x = (x + dx) % 4
    return (y * 2 + z_lo) * NBLK + z_hi * 8 + x * 2 + core


def origin(slot):
    return device_at(lax.axis_index("seg"), lax.axis_index("blk"), *slot)


def queries_kernel(twin_ref, own_ref, qt_ref):
    for number, q_ref in enumerate((twin_ref, own_ref)):
        for h in range(HEADS):
            scaled = q_ref[:, h * HD : (h + 1) * HD].astype(F32).T * SCALE
            high = scaled.astype(BF16)
            cols = slice(number * PART + h * TOK, number * PART + (h + 1) * TOK)
            qt_ref[0:HD, cols] = high
            qt_ref[HD : 2 * HD, cols] = (scaled - high.astype(F32)).astype(BF16)


def in_hbm(array):
    return pltpu.with_memory_space_constraint(array, pltpu.HBM)


def pack_kernel(cache_ref, new_ref, out_ref, sems):
    copies = [
        pltpu.make_async_copy(cache_ref.at[0:FILL], out_ref.at[0:FILL], sems.at[0]),
        pltpu.make_async_copy(new_ref, out_ref.at[FILL : FILL + TOK], sems.at[1]),
    ]
    for copy in copies:
        copy.start()
    for copy in copies:
        copy.wait()


def pack(cache_kv, new_kv):
    return pl.pallas_call(
        pack_kernel,
        in_specs=[pl.BlockSpec(memory_space=pltpu.HBM)] * 2,
        out_specs=VMEM,
        out_shape=jax.ShapeDtypeStruct((FILL + TOK, 2 * HD), BF16),
        scratch_shapes=[pltpu.SemaphoreType.DMA((2,))],
        compiler_params=pltpu.CompilerParams(vmem_limit_bytes=1 << 20),
        name="pack",
    )(in_hbm(cache_kv), in_hbm(new_kv))


def flash_kernel(slots, operand_count, first, last, width, *refs):
    count = len(slots)
    len_ref, qt_ref = refs[0], refs[1]
    blocks = refs[2 : 2 + operand_count]
    at = 2 + operand_count
    if last:
        fresh_ref = refs[at]
        at += 1
    if not first:
        m_in, acc_in = refs[at], refs[at + 1]
        at += 2
    if last:
        part_refs = refs[at : at + 2]
        at += 2
    else:
        m_ref, acc_ref = refs[at], refs[at + 1]
        at += 2
    keys, vals, vals_t, scores_ref = refs[at:]
    total = keys.shape[0]
    old = count * FILL
    for j, (slot, pieces) in enumerate(slots):
        filled = len_ref[origin(slot)]
        valid = blocks[pieces[0][0]][pieces[0][1] : pieces[0][1] + 1, 0:HD]
        done = 0
        for which, start, stop in pieces:
            stop = min(stop, start + FILL - done)
            size = stop - start
            ok = lax.broadcasted_iota(jnp.int32, (size, HD), 0) + done < filled
            key = blocks[which][start:stop, 0:HD]
            value = blocks[which][start:stop, HD : 2 * HD]
            key = jnp.where(ok, key, jnp.broadcast_to(valid, (size, HD)))
            rows = slice(j * FILL + done, j * FILL + done + size)
            keys[rows, 0:HD] = key
            keys[rows, HD : 2 * HD] = key
            vals[rows, 0:HD] = jnp.where(ok, value, jnp.zeros_like(value))
            vals[rows, HD : 2 * HD] = ok.astype(BF16)
            done += size
    used = old
    if last:
        used = old + fresh_ref.shape[0]
        keys[old:used, 0:HD] = fresh_ref[:, 0:HD]
        keys[old:used, HD : 2 * HD] = fresh_ref[:, 0:HD]
        vals[old:used, 0:HD] = fresh_ref[:, HD : 2 * HD]
        vals[old:used, HD : 2 * HD] = jnp.ones((used - old, HD), BF16)
    if total > used:
        keys[used:total, :] = jnp.broadcast_to(keys[0:1, :], (total - used, 2 * HD))
        vals[used:total, :] = jnp.zeros((total - used, 2 * HD), BF16)
    for c in range(total // 128):
        rows = slice(c * 128, (c + 1) * 128)
        vals_t[0:HD, rows] = vals[rows, 0:HD].T
        vals_t[HD:ACC, rows] = vals[rows, HD : 2 * HD].T[0 : ACC - HD]

    def chunk(r):
        return pl.ds(pl.multiple_of(r * width, width), width)

    def score(r):
        s = jnp.dot(keys[...], qt_ref[:, chunk(r)], preferred_element_type=F32)
        if last:
            shape = (total - old, width)
            key_id = lax.broadcasted_iota(jnp.int32, shape, 0)
            blk = lax.axis_index("blk")
            key_blk = key_id // SHARE * 2 + blk % 2
            key_pos = key_blk * TOK + lax.axis_index("seg") * SHARE + key_id % SHARE
            query_blk = jnp.where(r < PART // width, blk + 1 - blk % 2 * 2, blk)
            token = query_blk * TOK + lax.broadcasted_iota(jnp.int32, shape, 1) % TOK
            fresh = jnp.where(key_pos <= token, s[old:total], NEG)
            scores_ref[0:old] = s[0:old]
            scores_ref[old:total] = fresh
            return jnp.maximum(column_max(s[0:old]), column_max(fresh))
        scores_ref[...] = s
        return column_max(s)

    def column_max(s):
        return jnp.max(s.reshape(s.shape[0] // 8, 8, width), axis=0)

    def weigh(r, tops, more, part_ref):
        cols = chunk(r)
        top = jnp.max(tops, axis=0, keepdims=True)
        if not first:
            top = jnp.maximum(top, m_in[0:1, cols])
        w = jnp.exp2(scores_ref[...] - top).astype(BF16)
        if more:
            tops = score(r + 1)
        out = jnp.dot(vals_t[...], w, preferred_element_type=F32)
        if not first:
            out = out + acc_in[:, cols] * jnp.exp2(m_in[0:1, cols] - top)
        if not last:
            acc_ref[:, cols] = out
            m_ref[:, cols] = jnp.broadcast_to(top, (8, width))
            return tops
        total_w = out[HD : HD + 1]
        normal = (out[0:HD] * (1.0 / total_w)).astype(BF16)
        stats = three_terms(top + jnp.log2(total_w))
        for i in range(width // TOK):
            head = r % (PART // width) * (width // TOK) + i
            lanes = slice(i * TOK, (i + 1) * TOK)
            part_ref[head // 2, pl.ds(pl.multiple_of(head % 2 * HD, HD), HD), :] = normal[:, lanes]
            part_ref[head // 2, pl.ds(pl.multiple_of(2 * HD + head % 2 * 16, 16), 16), :] = stats[:, lanes]
        return tops

    tops = score(0)
    if last:
        half = PART // width
        tops = lax.fori_loop(0, half, lambda r, tops: weigh(r, tops, True, part_refs[0]), tops)
        tops = lax.fori_loop(half, 2 * half - 1, lambda r, tops: weigh(r, tops, True, part_refs[1]), tops)
        weigh(2 * half - 1, tops, False, part_refs[1])
    else:
        tops = lax.fori_loop(0, ROWS // width - 1, lambda r, tops: weigh(r, tops, True, None), tops)
        weigh(ROWS // width - 1, tops, False, None)


def three_terms(row):
    high = row.astype(BF16)
    rest = row - high.astype(F32)
    middle = rest.astype(BF16)
    low = (rest - middle.astype(F32)).astype(BF16)
    return jnp.concatenate([high, middle, low] + [high] * 13, axis=0)


def flash(held, cache_len, qt, state, fresh=None, width=512):
    first, last = state is None, fresh is not None
    slots, blocks = indexed(held)
    total = len(slots) * FILL + (fresh.shape[0] if last else 0)
    total = -(-total // 128) * 128
    operands = [cache_len, qt, *blocks]
    if last:
        operands.append(fresh)
    if not first:
        operands += list(state)
    if last:
        out_shape = [jax.ShapeDtypeStruct((NSEG, CHUNK, TOK), BF16)] * 2
    else:
        out_shape = [jax.ShapeDtypeStruct((8, ROWS), F32), jax.ShapeDtypeStruct((ACC, ROWS), F32)]
    return pl.pallas_call(
        functools.partial(flash_kernel, slots, len(blocks), first, last, width),
        in_specs=[SMEM] + [VMEM] * (len(operands) - 1),
        out_specs=[VMEM, VMEM],
        out_shape=out_shape,
        scratch_shapes=[
            pltpu.VMEM((total, 2 * HD), BF16),
            pltpu.VMEM((total, 2 * HD), BF16),
            pltpu.VMEM((ACC, total), BF16),
            pltpu.VMEM((total, width), F32),
        ],
        compiler_params=pltpu.CompilerParams(vmem_limit_bytes=24 << 20),
        cost_estimate=pl.CostEstimate(
            flops=4 * total * ROWS * 256, bytes_accessed=1 << 20, transcendentals=total * ROWS
        ),
        name=f"flash_{len(slots)}",
    )(*operands)


def indexed(held):
    arrays, slots = [], []
    for slot, pieces in held.items():
        places = []
        for array, start, stop in pieces:
            number = next((i for i, known in enumerate(arrays) if known is array), None)
            if number is None:
                number = len(arrays)
                arrays.append(array)
            places.append((number, start, stop))
        slots.append((slot, places))
    return slots, arrays


def fresh_kernel(slots, *refs):
    blocks, share_ref, rows_ref = refs[:-2], refs[-2], refs[-1]
    start = pl.multiple_of(FILL + lax.axis_index("seg") * SHARE, SHARE)
    for slot, pieces in slots:
        pair = origin(slot) % NBLK // 2
        block = blocks[pieces[0][0]]
        share_ref[pl.ds(pl.multiple_of(pair * SHARE, SHARE), SHARE), :] = block[pl.ds(start, SHARE), :]
        rows_ref[pl.ds(pl.multiple_of(pair * TOK, TOK), TOK), :] = block[FILL : FILL + TOK, :]


def fresh_rows(held):
    slots, blocks = indexed(held)
    return pl.pallas_call(
        functools.partial(fresh_kernel, slots),
        in_specs=[VMEM] * len(blocks),
        out_specs=[VMEM, VMEM],
        out_shape=[
            jax.ShapeDtypeStruct((NBLK // 2 * SHARE, 2 * HD), BF16),
            jax.ShapeDtypeStruct((NBLK // 2 * TOK, 2 * HD), BF16),
        ],
        compiler_params=pltpu.CompilerParams(vmem_limit_bytes=1 << 20),
        name="fresh_rows",
    )(*blocks)


def pages_kernel(len_ref, owner_ref, cache_ref, own_ref, twin_ref, out_ref):
    blk = lax.axis_index("blk")
    device = lax.axis_index("seg") * NBLK + blk
    filled = len_ref[device]
    pages = owner_ref.shape[1]
    owned = jnp.broadcast_to((owner_ref[...] == device).astype(F32), (16, pages)).astype(BF16)
    before = (
        lax.broadcasted_iota(jnp.int32, (pages, pages), 0) < lax.broadcasted_iota(jnp.int32, (pages, pages), 1)
    ).astype(BF16)
    rank = jnp.dot(owned, before, preferred_element_type=F32)
    rank = jnp.where(owned > 0, rank, -1.0).astype(BF16)
    half = SLOTS // 2
    written, count = None, None
    for rows_ref, core in ((own_ref, blk % 2), (twin_ref, 1 - blk % 2)):
        rows = rows_ref.shape[0]
        row = lax.broadcasted_iota(jnp.int32, (pages, rows), 1)
        page = (row // TOK * 2 + core) * (TOK // PAGE) + row % TOK // PAGE
        spread = (page == lax.broadcasted_iota(jnp.int32, (pages, rows), 0)).astype(BF16)
        row_rank = jnp.dot(rank, spread, preferred_element_type=F32)[0:1].astype(jnp.int32)
        target = filled + row_rank * PAGE + lax.broadcasted_iota(jnp.int32, (1, rows), 1) % PAGE
        target = jnp.where(row_rank >= 0, target, -1)
        pick = (lax.broadcasted_iota(jnp.int32, (half, rows), 0) + half == target).astype(BF16)
        term = jnp.dot(pick, rows_ref[...], preferred_element_type=F32)
        written = term if written is None else written + term
        most = jnp.max(row_rank) + 1
        count = most if count is None else jnp.maximum(count, most)
    slot_id = lax.broadcasted_iota(jnp.int32, (half, 2 * HD), 0) + half
    is_new = (slot_id >= filled) & (slot_id < filled + count * PAGE)
    out_ref[0:half, :] = cache_ref[0:half, :]
    out_ref[half:SLOTS, :] = jnp.where(is_new, written.astype(BF16), cache_ref[half:SLOTS, :])


def write_pages(cache_len, page_owner, cache_kv, own_rows, twin_rows):
    return pl.pallas_call(
        pages_kernel,
        in_specs=[SMEM] + [VMEM] * 4,
        out_specs=VMEM,
        out_shape=jax.ShapeDtypeStruct(cache_kv.shape, BF16),
        compiler_params=pltpu.CompilerParams(vmem_limit_bytes=16 << 20),
        cost_estimate=pl.CostEstimate(flops=10**9, bytes_accessed=2 << 20, transcendentals=0),
        name="write_pages",
    )(cache_len, page_owner.reshape(1, -1), cache_kv, own_rows, twin_rows)


def log_sum(ref, s, stat):
    three = [ref[s, stat + i : stat + i + 1, :].astype(F32) for i in range(3)]
    return three[0] + three[1] + three[2]


def pair_kernel(own_ref, twin_ref, out_ref):
    for s in range(NSEG):
        for head in range(2):
            stat = 2 * HD + head * 16
            rows = slice(head * HD, (head + 1) * HD)
            own, twin = log_sum(own_ref, s, stat), log_sum(twin_ref, s, stat)
            top = jnp.maximum(own, twin)
            own_w, twin_w = jnp.exp2(own - top), jnp.exp2(twin - top)
            total = own_w + twin_w
            scale = 1.0 / total
            out = own_ref[s, rows, :].astype(F32) * (own_w * scale) + twin_ref[s, rows, :].astype(F32) * (twin_w * scale)
            out_ref[s, rows, :] = out.astype(BF16)
            out_ref[s, stat : stat + 16, :] = three_terms(top + jnp.log2(total))


def merge_pair(own, twin):
    return pl.pallas_call(
        pair_kernel,
        in_specs=[VMEM, VMEM],
        out_specs=VMEM,
        out_shape=jax.ShapeDtypeStruct(own.shape, BF16),
        compiler_params=pltpu.CompilerParams(vmem_limit_bytes=4 << 20),
        name="merge_pair",
    )(own, twin)


def merge_kernel(parts_ref, out_ref):
    for head in range(2):
        stat = 2 * HD + head * 16
        logs = [log_sum(parts_ref, s, stat) for s in range(NSEG)]
        top = functools.reduce(jnp.maximum, logs)
        weights = [jnp.exp2(v - top) for v in logs]
        scale = 1.0 / functools.reduce(jnp.add, weights)
        out = None
        for s in range(NSEG):
            term = parts_ref[s, head * HD : (head + 1) * HD, :].astype(F32) * (weights[s] * scale)
            out = term if out is None else out + term
        out_ref[:, head * HD : (head + 1) * HD] = out.T.astype(BF16)


def merge(parts):
    return pl.pallas_call(
        merge_kernel,
        in_specs=[VMEM],
        out_specs=VMEM,
        out_shape=jax.ShapeDtypeStruct((TOK, 2 * HD), BF16),
        compiler_params=pltpu.CompilerParams(vmem_limit_bytes=4 << 20),
        name="merge",
    )(parts)


def shift(block, dx=0, flip_z=False, flip_core=False):
    return lax.ppermute(block, AXES, neighbours(-dx, flip_z, flip_core))


def after(values, other):
    return lax.optimization_barrier((values, other))


def scaled_queries(twin, own):
    return pl.pallas_call(
        queries_kernel,
        in_specs=[VMEM, VMEM],
        out_specs=VMEM,
        out_shape=jax.ShapeDtypeStruct((2 * HD, ROWS), BF16),
        compiler_params=pltpu.CompilerParams(vmem_limit_bytes=4 << 20),
        name="scaled_queries",
    )(twin, own)


def on_device(queries, new_kv, cache_kv, cache_len, page_owner):
    def placed(blocks):
        return {(*slot, False): [(block, 0, FILL + TOK)] for slot, block in blocks.items()}

    own = pack(cache_kv, new_kv)
    across = shift(own, flip_z=True)
    twin_queries = shift(queries, flip_core=True)
    beside = {(1, False): shift(own, 1), (-1, False): shift(own, -1), (2, False): shift(own, 2)}
    qt = scaled_queries(twin_queries, queries)
    held = placed({(0, False): own})
    everything = dict(held)
    state = flash(held, cache_len, qt, None)

    across, state = after(across, state)
    far = {(1, True): shift(across, 1), (-1, True): shift(across, -1)}
    beside, state = after(beside, state)
    far[2, True] = shift(beside[2, False], flip_z=True)
    held = placed({(0, True): across, **beside})
    everything.update(held)
    state = flash(held, cache_len, qt, state)

    far, state = after(far, state)
    held = placed(far)
    everything.update(held)
    fresh, rows = fresh_rows(everything)
    twin_rows = shift(rows, flip_core=True)
    twin_part, own_part = flash(held, cache_len, qt, state, fresh)
    part = merge_pair(own_part, shift(twin_part, flip_core=True))
    parts = lax.all_to_all(part, "seg", 0, 0)
    cache_out = write_pages(cache_len, page_owner, cache_kv, rows, twin_rows)
    return merge(parts), cache_out


def solution(mesh):
    placed = (P("blk", None), P("blk", None), P(("seg", "blk"), None), P(), P())
    return jax.shard_map(
        on_device,
        mesh=mesh,
        in_specs=placed,
        out_specs=(P("blk", "seg"), P(("seg", "blk"), None)),
        check_vma=False,
    )
```

time: 91.2 us -> 61.7 us (0.68)
  local copies, waits for them, and re-layouts: 13.5 us -> 1.06 us
  Pallas kernels: 37.6 us -> 28 us
  starting transfers between devices: 25.6 us -> 17.5 us
  waiting for transfers between devices: 11.9 us -> 14 us
    unnamed x83 -> x8, local copies, waits for them, and re-layouts: 12.5 us -> 1.06 us
    pallas_call x7 -> x8, Pallas kernels: 35.7 us -> 27.2 us  [the longest x3 22.3 us: flash(): pl.pallas_call(functools.partial(flash_kernel, slots, len(blocks), first,...]
    ppermute x15 -> x10, starting transfers between devices: 19.8 us -> 13.3 us  [shift(): return lax.ppermute(block, AXES, neighbours(-dx, flip_z, flip_core))]
    all_to_all x1, waiting for transfers between devices: 3.37 us -> 7.72 us  [on_device(): parts = lax.all_to_all(part, 'seg', 0, 0)]
    ppermute x15 -> x10, waiting for transfers between devices: 8.58 us -> 6.3 us  [shift(): return lax.ppermute(block, AXES, neighbours(-dx, flip_z, flip_core))]
    all_to_all x1, starting transfers between devices: 5.81 us -> 4.19 us  [on_device(): parts = lax.all_to_all(part, 'seg', 0, 0)]
    pallas_call x1, Pallas kernels: 1.89 us -> 0.84 us  [merge(): pl.pallas_call(merge_kernel, in_specs=[VMEM], out_specs=VMEM, out_shape=j...]
    slice x1 -> x0, local copies, waits for them, and re-layouts: 0.96 us -> none  [on_device(): own = jnp.concatenate([cache_kv[:FILL], new_kv], axis=0)]
  transfers between devices with their start and end apart: 16 -> 11, of which waited for: 5 -> 4; matrix products, arithmetic and copies ran while one was open for 1% -> 0% of each run, Pallas kernels for 20% -> 30%
where the time goes in v2:
time: 61.7 us; the launch traced here: 61.4 us
  Pallas kernels  28 us (45%)
  starting transfers between devices  17.5 us (28%)
  waiting for transfers between devices  14 us (23%)
  local copies, waits for them, and re-layouts  1.06 us (2%)
  between operations  0.75 us (1%)
    pallas_call x3, Pallas kernels, flash(): pl.pallas_call(functools.partial(flash_kernel, slots, len(blocks), first,...  22.3 us
    ppermute x10, starting transfers between devices, shift(): return lax.ppermute(block, AXES, neighbours(-dx, flip_z, flip_core))  13.3 us
    all_to_all x1, waiting for transfers between devices, on_device(): parts = lax.all_to_all(part, 'seg', 0, 0)  7.72 us
    ppermute x10, waiting for transfers between devices, shift(): return lax.ppermute(block, AXES, neighbours(-dx, flip_z, flip_core))  6.3 us
    all_to_all x1, starting transfers between devices, on_device(): parts = lax.all_to_all(part, 'seg', 0, 0)  4.19 us
    pallas_call x1, Pallas kernels, write_pages(): pl.pallas_call(pages_kernel, in_specs=[SMEM] + [VMEM] * 4, out_specs=VMEM...  2.04 us
  transfers between devices with their start and end apart: 11, of which 4 were waited for; matrix products, arithmetic and copies ran while one was open for 0% of the time, Pallas kernels for 30%

profile of v2, /device:TPU:1, one launch (start us, length us, event | category | flops | bytes accessed | tf_op | source)
XLA Modules:
  0.0 61.4 jit_solution(13549197689278520656)
XLA Ops:
  0.6 0.0 copy-start.3
  0.6 1.5 %collective-permute-start = (bf16[128,2048]{1,0:T(8,128)(2,1)}, bf16[128,2048]{1,0:T(8,128)(2,1)S(1)}, u32[]{:S(2)}, u32[]{:S(2)}) collective-permute-start(bf16[128,2048]{1,0:T(8,128)(2,1)} %own_ref.1), channel_id=1, source_target_pairs={{0,1},{1,0},{2,3},{3,2},{4,5},{5,4},{6,7},{7,6},{8,9},{9,8},{10,11... | collective-permute-start | bytes 1572872 | tf_op jit(solution)/shard_map/ppermute | solution.py:385
  2.1 1.0 %pack.1.refs_2_.refs_0_ = bf16[576,256]{1,0:T(8,128)(2,1)S(1)} custom-call(bf16[512,256]{1,0:T(8,128)(2,1)} %cache_ref.3, bf16[128,256]{1,0:T(8,128)(2,1)} %new_ref.1), custom_call_target="tpu_custom_call" | custom-call | tf_op jit(solution)/shard_map/pack/pallas_call | solution.py:82
  3.1 3.9 %collective-permute-start.1 = (bf16[576,256]{1,0:T(8,128)(2,1)S(1)}, bf16[576,256]{1,0:T(8,128)(2,1)S(1)}, u32[]{:S(2)}, u32[]{:S(2)}) collective-permute-start(bf16[576,256]{1,0:T(8,128)(2,1)S(1)} %pack.1.refs_2_.refs_0_), channel_id=1, source_target_pairs={{0,24},{1,25},{2,26},{3,27},{4,28},{5,29},{6,30},{7,31},{8,16},{9,... | collective-permute-start | bytes 884744 | tf_op jit(solution)/shard_map/ppermute | solution.py:385
  7.0 2.7 %collective-permute-start.6 = (bf16[576,256]{1,0:T(8,128)(2,1)S(1)}, bf16[576,256]{1,0:T(8,128)(2,1)S(1)}, u32[]{:S(2)}, u32[]{:S(2)}) collective-permute-start(bf16[576,256]{1,0:T(8,128)(2,1)S(1)} %pack.1.refs_2_.refs_0_), channel_id=1, source_target_pairs={{0,4},{1,5},{2,6},{3,7},{4,0},{5,1},{6,2},{7,3},{8,12},{9,13},{10,... | collective-permute-start | bytes 884744 | tf_op jit(solution)/shard_map/ppermute | solution.py:385
  9.8 0.9 %collective-permute-start.5 = (bf16[576,256]{1,0:T(8,128)(2,1)S(1)}, bf16[576,256]{1,0:T(8,128)(2,1)S(1)}, u32[]{:S(2)}, u32[]{:S(2)}) collective-permute-start(bf16[576,256]{1,0:T(8,128)(2,1)S(1)} %pack.1.refs_2_.refs_0_), channel_id=1, source_target_pairs={{0,6},{1,7},{2,0},{3,1},{4,2},{5,3},{6,4},{7,5},{8,14},{9,15},{10,... | collective-permute-start | bytes 884744 | tf_op jit(solution)/shard_map/ppermute | solution.py:385
  10.6 0.6 collective-permute-start.4
  11.2 0.0 collective-permute-done.twin_ref
  11.2 0.0 copy-start
  11.3 1.0 %copy-done = bf16[128,2048]{1,0:T(8,128)(2,1)S(1)} copy-done((bf16[128,2048]{1,0:T(8,128)(2,1)S(1)}, bf16[128,2048]{1,0:T(8,128)(2,1)}, u32[]{:S(2)}) %copy-start) | copy-done | bytes 524312
  12.3 0.6 scaled_queries.1.refs_1_
  12.9 0.0 copy-done.3
  12.9 4.0 %flash_1.1 = (f32[8,4096]{1,0:T(8,128)S(1)}, f32[144,4096]{1,0:T(8,128)S(1)}) custom-call(s32[128]{0:T(128)S(1)} %copy-done.3, bf16[256,4096]{1,0:T(8,128)(2,1)S(1)} %scaled_queries.1.refs_1_, bf16[576,256]{1,0:T(8,128)(2,1)S(1)} %pack.1.refs_2_.refs_0_), custom_call_target="tpu_custom_call" | custom-call | flops 2147483648 | bytes 1048576 | tf_op jit(solution)/shard_map/flash_1/pallas_call | solution.py:226
  16.9 0.0 collective-permute-done.1.refs_2_.refs_1_
  16.9 2.1 %collective-permute-start.3 = (bf16[576,256]{1,0:T(8,128)(2,1)S(1)}, bf16[576,256]{1,0:T(8,128)(2,1)S(1)}, u32[]{:S(2)}, u32[]{:S(2)}) collective-permute-start(bf16[576,256]{1,0:T(8,128)(2,1)S(1)} %collective-permute-done.1.refs_2_.refs_1_), channel_id=1, source_target_pairs={{0,6},{1,7},{2,0},{3,1},{4,2},{5,3},{6,4},{7,5},{8,14},{9,15},{10,... | collective-permute-start | bytes 884744 | tf_op jit(solution)/shard_map/ppermute | solution.py:385
  19.0 0.0 collective-permute-start.2
  19.0 0.0 collective-permute-done.6.refs_5_.refs_4_
  19.0 4.3 %collective-permute-done.5.refs_4_.refs_3_ = bf16[576,256]{1,0:T(8,128)(2,1)S(1)} collective-permute-done((bf16[576,256]{1,0:T(8,128)(2,1)S(1)}, bf16[576,256]{1,0:T(8,128)(2,1)S(1)}, u32[]{:S(2)}, u32[]{:S(2)}) %collective-permute-start.5) | collective-permute-done | bytes 294944 | tf_op jit(solution)/shard_map/ppermute | solution.py:385
  23.3 0.5 collective-permute-done.4.refs_3_.refs_2_
  23.8 0.1 collective-permute-start.7
  23.9 9.7 %flash_4.1 = (f32[8,4096]{1,0:T(8,128)S(1)}, f32[144,4096]{1,0:T(8,128)S(1)}) custom-call(s32[128]{0:T(128)S(1)} %copy-done.3, bf16[256,4096]{1,0:T(8,128)(2,1)S(1)} %scaled_queries.1.refs_1_, bf16[576,256]{1,0:T(8,128)(2,1)S(1)} %collective-permute-done.1.refs_2_.refs_1_, bf16[576,256]{1,0:T(8,128)(2,1)S(1)} %collective-permute-done.4.refs_3_.refs_2_, ...), custom_call_target="tpu_custom_call" | custom-call | flops 7516192768 | bytes 1048576 | tf_op jit(solution)/shard_map/flash_4/pallas_call | solution.py:226
  33.6 0.0 collective-permute-done.7.refs_7_.refs_4_
  33.6 0.0 collective-permute-done.3.refs_6_.refs_3_
  33.6 0.0 collective-permute-done.2.refs_5_.refs_2_
  33.6 0.1 fresh_rows.1
  33.8 8.6 %flash_3.1 = (bf16[8,288,128]{2,1,0:T(8,128)(2,1)S(1)}, bf16[8,288,128]{2,1,0:T(8,128)(2,1)S(1)}) custom-call(s32[128]{0:T(128)S(1)} %copy-done.3, bf16[256,4096]{1,0:T(8,128)(2,1)S(1)} %scaled_queries.1.refs_1_, bf16[576,256]{1,0:T(8,128)(2,1)S(1)} %collective-permute-done.2.refs_5_.refs_2_, bf16[576,256]{1,0:T(8,128)(2,1)S(1)} %collective-permute-done.3.refs_6_.refs_3_, ...), custom_call_target="tpu_custom_call" | custom-call | flops 6442450944 | bytes 1048576 | tf_op jit(solution)/shard_map/flash_3/pallas_call | solution.py:226
  42.3 0.0 copy-start.1
  42.3 0.0 copy-start.2
  42.4 1.4 %collective-permute-start.8 = (bf16[8,288,128]{2,1,0:T(8,128)(2,1)S(1)}, bf16[8,288,128]{2,1,0:T(8,128)(2,1)S(1)}, u32[]{:S(2)}, u32[]{:S(2)}) collective-permute-start(bf16[8,288,128]{2,1,0:T(8,128)(2,1)S(1)} %get-tuple-element.42), channel_id=1, source_target_pairs={{0,1},{1,0},{2,3},{3,2},{4,5},{5,4},{6,7},{7,6},{8,9},{9,8},{10,11... | collective-permute-start | bytes 1769480 | tf_op jit(solution)/shard_map/ppermute | solution.py:385
  43.7 0.1 collective-permute-start.9
  43.8 1.5 %collective-permute-done.8.twin_ref = bf16[8,288,128]{2,1,0:T(8,128)(2,1)S(1)} collective-permute-done((bf16[8,288,128]{2,1,0:T(8,128)(2,1)S(1)}, bf16[8,288,128]{2,1,0:T(8,128)(2,1)S(1)}, u32[]{:S(2)}, u32[]{:S(2)}) %collective-permute-start.8) | collective-permute-done | bytes 589856 | tf_op jit(solution)/shard_map/ppermute | solution.py:385
  45.4 1.2 %merge_pair.1 = bf16[8,288,128]{2,1,0:T(8,128)(2,1)} custom-call(bf16[8,288,128]{2,1,0:T(8,128)(2,1)S(1)} %get-tuple-element.41.own_ref, bf16[8,288,128]{2,1,0:T(8,128)(2,1)S(1)} %collective-permute-done.8.twin_ref), custom_call_target="tpu_custom_call" | custom-call | tf_op jit(solution)/shard_map/merge_pair/pallas_call | solution.py:349
  46.6 4.2 %all-to-all-start = ((bf16[8,288,128]{2,1,0:T(8,128)(2,1)}), bf16[8,288,128]{2,1,0:T(8,128)(2,1)S(1)}, u32[]{:S(2)}, u32[]{:S(2)}) async-start(bf16[8,288,128]{2,1,0:T(8,128)(2,1)} %merge_pair.1), calls=%async_computation | async-start | bytes 1179648 | tf_op jit(solution)/shard_map/all_to_all | solution.py:431
  50.8 0.0 collective-permute-done.9.twin_ref
  50.8 0.0 copy-done.1
  50.8 0.0 copy-done.2
  50.8 2.0 %write_pages.1 = bf16[512,256]{1,0:T(8,128)(2,1)} custom-call(s32[128]{0:T(128)S(1)} %copy-done.3, s32[1,256]{1,0:T(1,128)S(1)} %bitcast.1, bf16[512,256]{1,0:T(8,128)(2,1)S(1)} %copy-done.1, bf16[1024,256]{1,0:T(8,128)(2,1)S(1)} %get-tuple-element.43.own_ref, bf16[1024,256]{1,0:T(8,128)(2,1)S(1)} %collective-permute-done.9.twin_ref), custom_call_target="tpu_custom_call" | custom-call | flops 1000000000 | bytes 2097152 | tf_op jit(solution)/shard_map/write_pages/pallas_call | solution.py:317
  52.8 7.7 %all-to-all-done.parts_ref = bf16[8,288,128]{2,1,0:T(8,128)(2,1)S(1)} async-done(((bf16[8,288,128]{2,1,0:T(8,128)(2,1)}), bf16[8,288,128]{2,1,0:T(8,128)(2,1)S(1)}, u32[]{:S(2)}, u32[]{:S(2)}) %all-to-all-start) | async-done | bytes 589856 | tf_op jit(solution)/shard_map/all_to_all | solution.py:431
  60.5 0.8 %merge.1 = bf16[128,256]{1,0:T(8,128)(2,1)} custom-call(bf16[8,288,128]{2,1,0:T(8,128)(2,1)S(1)} %all-to-all-done.parts_ref), custom_call_target="tpu_custom_call" | custom-call | tf_op jit(solution)/shard_map/merge/pallas_call | solution.py:374
Async XLA Ops:
  0.6 12.2 %copy-start.3 = (s32[128]{0:T(128)S(1)}, s32[128]{0:T(128)}, u32[]{:S(2)}) copy-start(s32[128]{0:T(128)} %len_ref.1) | copy-start | bytes 1540
  0.6 10.6 %collective-permute-start = (bf16[128,2048]{1,0:T(8,128)(2,1)}, bf16[128,2048]{1,0:T(8,128)(2,1)S(1)}, u32[]{:S(2)}, u32[]{:S(2)}) collective-permute-start(bf16[128,2048]{1,0:T(8,128)(2,1)} %own_ref.1), channel_id=1, source_target_pairs={{0,1},{1,0},{2,3},{3,2},{4,5},{5,4},{6,7},{7,6},{8,9},{9,8},{10,11... | collective-permute-start | bytes 1572872 | tf_op jit(solution)/shard_map/ppermute | solution.py:385
  3.1 13.8 %collective-permute-start.1 = (bf16[576,256]{1,0:T(8,128)(2,1)S(1)}, bf16[576,256]{1,0:T(8,128)(2,1)S(1)}, u32[]{:S(2)}, u32[]{:S(2)}) collective-permute-start(bf16[576,256]{1,0:T(8,128)(2,1)S(1)} %pack.1.refs_2_.refs_0_), channel_id=1, source_target_pairs={{0,24},{1,25},{2,26},{3,27},{4,28},{5,29},{6,30},{7,31},{8,16},{9,... | collective-permute-start | bytes 884744 | tf_op jit(solution)/shard_map/ppermute | solution.py:385
  7.0 12.0 %collective-permute-start.6 = (bf16[576,256]{1,0:T(8,128)(2,1)S(1)}, bf16[576,256]{1,0:T(8,128)(2,1)S(1)}, u32[]{:S(2)}, u32[]{:S(2)}) collective-permute-start(bf16[576,256]{1,0:T(8,128)(2,1)S(1)} %pack.1.refs_2_.refs_0_), channel_id=1, source_target_pairs={{0,4},{1,5},{2,6},{3,7},{4,0},{5,1},{6,2},{7,3},{8,12},{9,13},{10,... | collective-permute-start | bytes 884744 | tf_op jit(solution)/shard_map/ppermute | solution.py:385
  9.8 13.5 %collective-permute-start.5 = (bf16[576,256]{1,0:T(8,128)(2,1)S(1)}, bf16[576,256]{1,0:T(8,128)(2,1)S(1)}, u32[]{:S(2)}, u32[]{:S(2)}) collective-permute-start(bf16[576,256]{1,0:T(8,128)(2,1)S(1)} %pack.1.refs_2_.refs_0_), channel_id=1, source_target_pairs={{0,6},{1,7},{2,0},{3,1},{4,2},{5,3},{6,4},{7,5},{8,14},{9,15},{10,... | collective-permute-start | bytes 884744 | tf_op jit(solution)/shard_map/ppermute | solution.py:385
  10.6 13.1 %collective-permute-start.4 = (bf16[576,256]{1,0:T(8,128)(2,1)S(1)}, bf16[576,256]{1,0:T(8,128)(2,1)S(1)}, u32[]{:S(2)}, u32[]{:S(2)}) collective-permute-start(bf16[576,256]{1,0:T(8,128)(2,1)S(1)} %pack.1.refs_2_.refs_0_), channel_id=1, source_target_pairs={{0,2},{1,3},{2,4},{3,5},{4,6},{5,7},{6,0},{7,1},{8,10},{9,11},{10,... | collective-permute-start | bytes 884744 | tf_op jit(solution)/shard_map/ppermute | solution.py:385
  11.2 1.0 %copy-start = (bf16[128,2048]{1,0:T(8,128)(2,1)S(1)}, bf16[128,2048]{1,0:T(8,128)(2,1)}, u32[]{:S(2)}) copy-start(bf16[128,2048]{1,0:T(8,128)(2,1)} %own_ref.1) | copy-start | bytes 1572868
  16.9 16.7 %collective-permute-start.3 = (bf16[576,256]{1,0:T(8,128)(2,1)S(1)}, bf16[576,256]{1,0:T(8,128)(2,1)S(1)}, u32[]{:S(2)}, u32[]{:S(2)}) collective-permute-start(bf16[576,256]{1,0:T(8,128)(2,1)S(1)} %collective-permute-done.1.refs_2_.refs_1_), channel_id=1, source_target_pairs={{0,6},{1,7},{2,0},{3,1},{4,2},{5,3},{6,4},{7,5},{8,14},{9,15},{10,... | collective-permute-start | bytes 884744 | tf_op jit(solution)/shard_map/ppermute | solution.py:385
  19.0 14.6 %collective-permute-start.2 = (bf16[576,256]{1,0:T(8,128)(2,1)S(1)}, bf16[576,256]{1,0:T(8,128)(2,1)S(1)}, u32[]{:S(2)}, u32[]{:S(2)}) collective-permute-start(bf16[576,256]{1,0:T(8,128)(2,1)S(1)} %collective-permute-done.1.refs_2_.refs_1_), channel_id=1, source_target_pairs={{0,2},{1,3},{2,4},{3,5},{4,6},{5,7},{6,0},{7,1},{8,10},{9,11},{10,... | collective-permute-start | bytes 884744 | tf_op jit(solution)/shard_map/ppermute | solution.py:385
  23.8 9.8 %collective-permute-start.7 = (bf16[576,256]{1,0:T(8,128)(2,1)S(1)}, bf16[576,256]{1,0:T(8,128)(2,1)S(1)}, u32[]{:S(2)}, u32[]{:S(2)}) collective-permute-start(bf16[576,256]{1,0:T(8,128)(2,1)S(1)} %collective-permute-done.6.refs_5_.refs_4_), channel_id=1, source_target_pairs={{0,24},{1,25},{2,26},{3,27},{4,28},{5,29},{6,30},{7,31},{8,16},{9,... | collective-permute-start | bytes 884744 | tf_op jit(solution)/shard_map/ppermute | solution.py:385
  42.3 8.4 %copy-start.1 = (bf16[512,256]{1,0:T(8,128)(2,1)S(1)}, bf16[512,256]{1,0:T(8,128)(2,1)}, u32[]{:S(2)}) copy-start(bf16[512,256]{1,0:T(8,128)(2,1)} %cache_ref.3) | copy-start | bytes 786436
  42.3 8.4 %copy-start.2 = (s32[256,1]{0,1:T(1,128)S(1)}, s32[256,1]{0,1:T(1,128)}, u32[]{:S(2)}) copy-start(s32[256,1]{0,1:T(1,128)} %param.9) | copy-start | bytes 3076
  42.4 3.0 %collective-permute-start.8 = (bf16[8,288,128]{2,1,0:T(8,128)(2,1)S(1)}, bf16[8,288,128]{2,1,0:T(8,128)(2,1)S(1)}, u32[]{:S(2)}, u32[]{:S(2)}) collective-permute-start(bf16[8,288,128]{2,1,0:T(8,128)(2,1)S(1)} %get-tuple-element.42), channel_id=1, source_target_pairs={{0,1},{1,0},{2,3},{3,2},{4,5},{5,4},{6,7},{7,6},{8,9},{9,8},{10,11... | collective-permute-start | bytes 1769480 | tf_op jit(solution)/shard_map/ppermute | solution.py:385
  43.7 7.0 %collective-permute-start.9 = (bf16[1024,256]{1,0:T(8,128)(2,1)S(1)}, bf16[1024,256]{1,0:T(8,128)(2,1)S(1)}, u32[]{:S(2)}, u32[]{:S(2)}) collective-permute-start(bf16[1024,256]{1,0:T(8,128)(2,1)S(1)} %get-tuple-element.43.own_ref), channel_id=1, source_target_pairs={{0,1},{1,0},{2,3},{3,2},{4,5},{5,4},{6,7},{7,6},{8,9},{9,8},{10,11... | collective-permute-start | bytes 1572872 | tf_op jit(solution)/shard_map/ppermute | solution.py:385
  46.6 14.0 %all-to-all-start = ((bf16[8,288,128]{2,1,0:T(8,128)(2,1)}), bf16[8,288,128]{2,1,0:T(8,128)(2,1)S(1)}, u32[]{:S(2)}, u32[]{:S(2)}) async-start(bf16[8,288,128]{2,1,0:T(8,128)(2,1)} %merge_pair.1), calls=%async_computation | async-start | bytes 1179648 | tf_op jit(solution)/shard_map/all_to_all | solution.py:431

commit v3 on v2

v3 whole, which is shorter than its diff:
```python
import functools

import jax
import jax.numpy as jnp
from jax import lax
from jax.experimental import pallas as pl
from jax.experimental.pallas import tpu as pltpu
from jax.sharding import PartitionSpec as P


F32 = jnp.float32
BF16 = jnp.bfloat16
HEADS = 16
HD = 128
TOK = 128
ROWS = 2 * HEADS * TOK
PART = HEADS * TOK
SLOTS = 512
FILL = 448
PAGE = 8
NSEG = 8
NBLK = 16
SHARE = TOK // NSEG
CHUNK = 2 * HD + 16
ACC = HD + 16
WIDTH = 512
NEG = -1e30
SCALE = 1.4426950408889634 / HD**0.5
VMEM = pl.BlockSpec(memory_space=pltpu.VMEM)
SMEM = pl.BlockSpec(memory_space=pltpu.SMEM)
AXES = ("seg", "blk")


def neighbours(dx=0, flip_z=False, flip_core=False):
    pairs = []
    for here in range(NSEG * NBLK):
        seg, blk = divmod(here, NBLK)
        pairs.append((here, device_at(seg, blk, dx, flip_z, flip_core)))
    return pairs


def device_at(seg, blk, dx, flip_z, flip_core):
    y, z_lo = seg // 2, seg % 2
    z_hi, x, core = blk // 8, (blk // 2) % 4, blk % 2
    if flip_z:
        z_lo, z_hi = 1 - z_lo, 1 - z_hi
    if flip_core:
        core = 1 - core
    x = (x + dx) % 4
    return (y * 2 + z_lo) * NBLK + z_hi * 8 + x * 2 + core


def origin(slot):
    return device_at(lax.axis_index("seg"), lax.axis_index("blk"), *slot)


def queries_kernel(twin_ref, own_ref, qt_ref):
    for number, q_ref in enumerate((twin_ref, own_ref)):
        for h in range(HEADS):
            scaled = q_ref[:, h * HD : (h + 1) * HD].astype(F32).T * SCALE
            high = scaled.astype(BF16)
            cols = slice(number * PART + h * TOK, number * PART + (h + 1) * TOK)
            qt_ref[0:HD, cols] = high
            qt_ref[HD : 2 * HD, cols] = (scaled - high.astype(F32)).astype(BF16)


def in_hbm(array):
    return pltpu.with_memory_space_constraint(array, pltpu.HBM)


def pack_kernel(cache_ref, new_ref, q_ref, out_ref, q_out, sems):
    copies = [
        pltpu.make_async_copy(cache_ref.at[0:FILL], out_ref.at[0:FILL], sems.at[0]),
        pltpu.make_async_copy(new_ref, out_ref.at[FILL : FILL + TOK], sems.at[1]),
        pltpu.make_async_copy(q_ref, q_out, sems.at[2]),
    ]
    for copy in copies:
        copy.start()
    for copy in copies:
        copy.wait()


def pack(cache_kv, new_kv, queries):
    return pl.pallas_call(
        pack_kernel,
        in_specs=[pl.BlockSpec(memory_space=pltpu.HBM)] * 3,
        out_specs=[VMEM, VMEM],
        out_shape=[
            jax.ShapeDtypeStruct((FILL + TOK, 2 * HD), BF16),
            jax.ShapeDtypeStruct(queries.shape, BF16),
        ],
        scratch_shapes=[pltpu.SemaphoreType.DMA((3,))],
        compiler_params=pltpu.CompilerParams(vmem_limit_bytes=1 << 20),
        name="pack",
    )(in_hbm(cache_kv), in_hbm(new_kv), in_hbm(queries))


def gather_keys(slots, blocks, fresh_ref, len_ref, keys, vals, vals_t):
    total = keys.shape[0]
    for j, (slot, which) in enumerate(slots):
        ok = lax.broadcasted_iota(jnp.int32, (FILL, HD), 0) < len_ref[origin(slot)]
        key = blocks[which][0:FILL, 0:HD]
        value = blocks[which][0:FILL, HD : 2 * HD]
        key = jnp.where(ok, key, jnp.broadcast_to(key[0:1], (FILL, HD)))
        rows = slice(j * FILL, (j + 1) * FILL)
        keys[rows, 0:HD] = key
        keys[rows, HD : 2 * HD] = key
        vals[rows, 0:HD] = jnp.where(ok, value, jnp.zeros_like(value))
        vals[rows, HD : 2 * HD] = ok.astype(BF16)
    old = used = len(slots) * FILL
    if fresh_ref is not None:
        used = old + fresh_ref.shape[0]
        keys[old:used, 0:HD] = fresh_ref[:, 0:HD]
        keys[old:used, HD : 2 * HD] = fresh_ref[:, 0:HD]
        vals[old:used, 0:HD] = fresh_ref[:, HD : 2 * HD]
        vals[old:used, HD : 2 * HD] = jnp.ones((used - old, HD), BF16)
    if total > used:
        keys[used:total, :] = jnp.broadcast_to(keys[0:1, :], (total - used, 2 * HD))
        vals[used:total, :] = jnp.zeros((total - used, 2 * HD), BF16)
    for c in range(total // 128):
        rows = slice(c * 128, (c + 1) * 128)
        vals_t[0:HD, rows] = vals[rows, 0:HD].T
        vals_t[HD:ACC, rows] = vals[rows, HD : 2 * HD].T[0 : ACC - HD]


def flash_columns(columns, old, keys, vals_t, qt_ref, state, even_ref, odd_ref, query_blk, emit):
    total, width = even_ref.shape
    first, last = columns[0] // width, columns[1] // width

    def column_max(s):
        return jnp.max(s.reshape(s.shape[0] // 8, 8, width), axis=0)

    def score(r, scores_ref):
        cols = pl.ds(pl.multiple_of(r * width, width), width)
        s = jnp.dot(keys[...], qt_ref[:, cols], preferred_element_type=F32)
        if query_blk is None:
            scores_ref[...] = s
            return column_max(s)
        shape = (total - old, width)
        key_id = lax.broadcasted_iota(jnp.int32, shape, 0)
        key_blk = key_id // SHARE * 2 + lax.axis_index("blk") % 2
        key_pos = key_blk * TOK + lax.axis_index("seg") * SHARE + key_id % SHARE
        token = query_blk * TOK + lax.broadcasted_iota(jnp.int32, shape, 1) % TOK
        fresh = jnp.where(key_pos <= token, s[old:total], NEG)
        scores_ref[0:old] = s[0:old]
        scores_ref[old:total] = fresh
        return jnp.maximum(column_max(s[0:old]), column_max(fresh))

    def weigh(r, tops, scores_ref, next_ref):
        cols = pl.ds(pl.multiple_of(r * width, width), width)
        top = jnp.max(tops, axis=0, keepdims=True)
        if state is not None:
            top = jnp.maximum(top, state[0][0:1, cols])
        if next_ref is not None:
            tops = score(r + 1, next_ref)
        w = jnp.exp2(scores_ref[...] - top).astype(BF16)
        out = jnp.dot(vals_t[...], w, preferred_element_type=F32)
        if state is not None:
            out = out + state[1][:, cols] * jnp.exp2(state[0][0:1, cols] - top)
        emit(r - first, cols, out, top)
        return tops

    def two(i, tops, more=True):
        tops = weigh(first + 2 * i, tops, even_ref, odd_ref)
        return weigh(first + 2 * i + 1, tops, odd_ref, even_ref if more else None)

    pairs = (last - first) // 2
    tops = lax.fori_loop(0, pairs - 1, two, score(first, even_ref))
    two(pairs - 1, tops, False)


def flash_kernel(slots, operand_count, *refs):
    len_ref, qt_ref = refs[0], refs[1]
    blocks, refs = refs[2 : 2 + operand_count], refs[2 + operand_count :]
    state, (m_ref, acc_ref, keys, vals, vals_t, even_ref, odd_ref) = refs[:-7] or None, refs[-7:]
    gather_keys(slots, blocks, None, len_ref, keys, vals, vals_t)

    def emit(r, cols, out, top):
        acc_ref[:, cols] = out
        m_ref[:, cols] = jnp.broadcast_to(top, m_ref.at[:, cols].shape)

    flash_columns((0, ROWS), keys.shape[0], keys, vals_t, qt_ref, state, even_ref, odd_ref, None, emit)


def emit_part(part_ref, width):
    def emit(r, cols, out, top):
        total = out[HD : HD + 1]
        normal = (out[0:HD] * (1.0 / total)).astype(BF16)
        stats = top + jnp.log2(total)
        for i in range(0, width // TOK, 2):
            pair = r * (width // TOK // 2) + i // 2
            for j in range(2):
                part_ref[pair, j * HD : (j + 1) * HD, :] = normal[:, (i + j) * TOK : (i + j + 1) * TOK]
            put_sums(part_ref, pair, [stats[:, (i + j) * TOK : (i + j + 1) * TOK] for j in range(2)])

    return emit


def put_sums(part_ref, pair, rows):
    terms = []
    for row in rows:
        high = row.astype(BF16)
        rest = row - high.astype(F32)
        middle = rest.astype(BF16)
        terms += [high, middle, (rest - middle.astype(F32)).astype(BF16)]
    part_ref[pair, 2 * HD : CHUNK, :] = jnp.concatenate(terms + [terms[0]] * 10, axis=0)


def get_sums(part_ref, pair, head):
    three = [part_ref[pair, 2 * HD + head * 3 + i : 2 * HD + head * 3 + i + 1, :].astype(F32) for i in range(3)]
    return three[0] + three[1] + three[2]


def twin_kernel(slots, operand_count, *refs):
    len_ref, qt_ref = refs[0], refs[1]
    blocks, refs = refs[2 : 2 + operand_count], refs[2 + operand_count :]
    fresh_ref, m_in, acc_in, part_ref, keys, vals_t, vals, even_ref, odd_ref = refs
    gather_keys(slots, blocks, fresh_ref, len_ref, keys, vals, vals_t)
    blk = lax.axis_index("blk")
    flash_columns(
        (0, PART),
        len(slots) * FILL,
        keys,
        vals_t,
        qt_ref,
        (m_in, acc_in),
        even_ref,
        odd_ref,
        blk + 1 - blk % 2 * 2,
        emit_part(part_ref, even_ref.shape[1]),
    )


def own_kernel(old, qt_ref, keys, vals_t, m_in, acc_in, part_ref, even_ref, odd_ref):
    flash_columns(
        (PART, ROWS),
        old,
        keys,
        vals_t,
        qt_ref,
        (m_in, acc_in),
        even_ref,
        odd_ref,
        lax.axis_index("blk"),
        emit_part(part_ref, even_ref.shape[1]),
    )


def flash_call(kernel, operands, first_spec, out_shape, scratch, total, rows, name, width=WIDTH):
    return pl.pallas_call(
        kernel,
        in_specs=[first_spec] + [VMEM] * (len(operands) - 1),
        out_specs=jax.tree.map(lambda _: VMEM, out_shape),
        out_shape=out_shape,
        scratch_shapes=scratch + [pltpu.VMEM((total, width), F32)] * 2,
        compiler_params=pltpu.CompilerParams(vmem_limit_bytes=24 << 20),
        cost_estimate=pl.CostEstimate(
            flops=4 * total * rows * 256, bytes_accessed=1 << 20, transcendentals=total * rows
        ),
        name=name,
    )(*operands)


def flash(held, cache_len, qt, state):
    slots, blocks = indexed(held)
    total = -(-len(slots) * FILL // 128) * 128
    return flash_call(
        functools.partial(flash_kernel, slots, len(blocks)),
        [cache_len, qt, *blocks, *(state or ())],
        SMEM,
        [jax.ShapeDtypeStruct((8, ROWS), F32), jax.ShapeDtypeStruct((ACC, ROWS), F32)],
        [
            pltpu.VMEM((total, 2 * HD), BF16),
            pltpu.VMEM((total, 2 * HD), BF16),
            pltpu.VMEM((ACC, total), BF16),
        ],
        total,
        ROWS,
        f"flash_{len(slots)}",
    )


def flash_last(held, cache_len, qt, state, fresh):
    slots, blocks = indexed(held)
    old = len(slots) * FILL
    total = -(-(old + fresh.shape[0]) // 128) * 128
    part = jax.ShapeDtypeStruct((NSEG, CHUNK, TOK), BF16)
    twin_part, keys, vals_t = flash_call(
        functools.partial(twin_kernel, slots, len(blocks)),
        [cache_len, qt, *blocks, fresh, *state],
        SMEM,
        [part, jax.ShapeDtypeStruct((total, 2 * HD), BF16), jax.ShapeDtypeStruct((ACC, total), BF16)],
        [pltpu.VMEM((total, 2 * HD), BF16)],
        total,
        PART,
        "flash_twin",
    )
    own_part = flash_call(
        functools.partial(own_kernel, old), [qt, keys, vals_t, *state], VMEM, part, [], total, PART, "flash_own"
    )
    return twin_part, own_part


def indexed(held):
    return [(slot, i) for i, slot in enumerate(held)], list(held.values())


def fresh_kernel(slots, *refs):
    blocks, share_ref, rows_ref = refs[:-2], refs[-2], refs[-1]
    start = pl.multiple_of(FILL + lax.axis_index("seg") * SHARE, SHARE)
    for slot, which in slots:
        pair = origin(slot) % NBLK // 2
        block = blocks[which]
        share_ref[pl.ds(pl.multiple_of(pair * SHARE, SHARE), SHARE), :] = block[pl.ds(start, SHARE), :]
        rows_ref[pl.ds(pl.multiple_of(pair * TOK, TOK), TOK), :] = block[FILL : FILL + TOK, :]


def fresh_rows(held):
    slots, blocks = indexed(held)
    return pl.pallas_call(
        functools.partial(fresh_kernel, slots),
        in_specs=[VMEM] * len(blocks),
        out_specs=[VMEM, VMEM],
        out_shape=[
            jax.ShapeDtypeStruct((NBLK // 2 * SHARE, 2 * HD), BF16),
            jax.ShapeDtypeStruct((NBLK // 2 * TOK, 2 * HD), BF16),
        ],
        compiler_params=pltpu.CompilerParams(vmem_limit_bytes=1 << 20),
        name="fresh_rows",
    )(*blocks)


def pages_kernel(len_ref, owner_ref, cache_ref, own_ref, twin_ref, out_ref):
    blk = lax.axis_index("blk")
    device = lax.axis_index("seg") * NBLK + blk
    filled = len_ref[device]
    pages = owner_ref.shape[1]
    owned = jnp.broadcast_to((owner_ref[...] == device).astype(F32), (16, pages)).astype(BF16)
    before = (
        lax.broadcasted_iota(jnp.int32, (pages, pages), 0) < lax.broadcasted_iota(jnp.int32, (pages, pages), 1)
    ).astype(BF16)
    rank = jnp.dot(owned, before, preferred_element_type=F32)
    rank = jnp.where(owned > 0, rank, -1.0).astype(BF16)
    half = SLOTS // 2
    written, count = None, None
    for rows_ref, core in ((own_ref, blk % 2), (twin_ref, 1 - blk % 2)):
        rows = rows_ref.shape[0]
        row = lax.broadcasted_iota(jnp.int32, (pages, rows), 1)
        page = (row // TOK * 2 + core) * (TOK // PAGE) + row % TOK // PAGE
        spread = (page == lax.broadcasted_iota(jnp.int32, (pages, rows), 0)).astype(BF16)
        row_rank = jnp.dot(rank, spread, preferred_element_type=F32)[0:1].astype(jnp.int32)
        target = filled + row_rank * PAGE + lax.broadcasted_iota(jnp.int32, (1, rows), 1) % PAGE
        target = jnp.where(row_rank >= 0, target, -1)
        pick = (lax.broadcasted_iota(jnp.int32, (half, rows), 0) + half == target).astype(BF16)
        term = jnp.dot(pick, rows_ref[...], preferred_element_type=F32)
        written = term if written is None else written + term
        most = jnp.max(row_rank) + 1
        count = most if count is None else jnp.maximum(count, most)
    slot_id = lax.broadcasted_iota(jnp.int32, (half, 2 * HD), 0) + half
    is_new = (slot_id >= filled) & (slot_id < filled + count * PAGE)
    out_ref[0:half, :] = cache_ref[0:half, :]
    out_ref[half:SLOTS, :] = jnp.where(is_new, written.astype(BF16), cache_ref[half:SLOTS, :])


def write_pages(cache_len, page_owner, cache_kv, own_rows, twin_rows):
    return pl.pallas_call(
        pages_kernel,
        in_specs=[SMEM] + [VMEM] * 4,
        out_specs=VMEM,
        out_shape=jax.ShapeDtypeStruct(cache_kv.shape, BF16),
        compiler_params=pltpu.CompilerParams(vmem_limit_bytes=16 << 20),
        cost_estimate=pl.CostEstimate(flops=10**9, bytes_accessed=2 << 20, transcendentals=0),
        name="write_pages",
    )(cache_len, page_owner.reshape(1, -1), cache_kv, own_rows, twin_rows)


def pair_kernel(own_ref, twin_ref, out_ref, held, sems):
    copies = []
    for s in range(NSEG):
        sums = []
        for head in range(2):
            rows = slice(head * HD, (head + 1) * HD)
            own, twin = get_sums(own_ref, s, head), get_sums(twin_ref, s, head)
            top = jnp.maximum(own, twin)
            own_w, twin_w = jnp.exp2(own - top), jnp.exp2(twin - top)
            total = own_w + twin_w
            scale = 1.0 / total
            out = own_ref[s, rows, :].astype(F32) * (own_w * scale) + twin_ref[s, rows, :].astype(F32) * (twin_w * scale)
            held[s, rows, :] = out.astype(BF16)
            sums.append(top + jnp.log2(total))
        put_sums(held, s, sums)
        copies.append(pltpu.make_async_copy(held.at[s], out_ref.at[s], sems.at[s]))
        copies[-1].start()
    for copy in copies:
        copy.wait()


def merge_pair(own, twin):
    return pl.pallas_call(
        pair_kernel,
        in_specs=[VMEM, VMEM],
        out_specs=pl.BlockSpec(memory_space=pltpu.HBM),
        out_shape=jax.ShapeDtypeStruct(own.shape, BF16),
        scratch_shapes=[pltpu.VMEM(own.shape, BF16), pltpu.SemaphoreType.DMA((NSEG,))],
        compiler_params=pltpu.CompilerParams(vmem_limit_bytes=4 << 20),
        name="merge_pair",
    )(own, twin)


def merge_kernel(parts_ref, out_ref):
    for head in range(2):
        logs = [get_sums(parts_ref, s, head) for s in range(NSEG)]
        top = functools.reduce(jnp.maximum, logs)
        weights = [jnp.exp2(v - top) for v in logs]
        scale = 1.0 / functools.reduce(jnp.add, weights)
        out = None
        for s in range(NSEG):
            term = parts_ref[s, head * HD : (head + 1) * HD, :].astype(F32) * (weights[s] * scale)
            out = term if out is None else out + term
        out_ref[:, head * HD : (head + 1) * HD] = out.T.astype(BF16)


def merge(parts):
    return pl.pallas_call(
        merge_kernel,
        in_specs=[VMEM],
        out_specs=VMEM,
        out_shape=jax.ShapeDtypeStruct((TOK, 2 * HD), BF16),
        compiler_params=pltpu.CompilerParams(vmem_limit_bytes=4 << 20),
        name="merge",
    )(parts)


def shift(block, dx=0, flip_z=False, flip_core=False):
    return lax.ppermute(block, AXES, neighbours(-dx, flip_z, flip_core))


def after(values, other):
    return lax.optimization_barrier((values, other))


def scaled_queries(twin, own):
    return pl.pallas_call(
        queries_kernel,
        in_specs=[VMEM, VMEM],
        out_specs=VMEM,
        out_shape=jax.ShapeDtypeStruct((2 * HD, ROWS), BF16),
        compiler_params=pltpu.CompilerParams(vmem_limit_bytes=4 << 20),
        name="scaled_queries",
    )(twin, own)


def on_device(queries, new_kv, cache_kv, cache_len, page_owner):
    own, own_queries = pack(cache_kv, new_kv, queries)
    across = shift(own, flip_z=True)
    opposite = shift(own, 2)
    beside = {(1, False, False): shift(own, 1), (-1, False, False): shift(own, -1)}
    qt = scaled_queries(shift(own_queries, flip_core=True), own_queries)
    held = {(0, False, False): own}
    everything = dict(held)
    state = flash(held, cache_len, qt, None)

    across, state = after(across, state)
    far = {(1, True, False): shift(across, 1), (-1, True, False): shift(across, -1)}
    opposite, state = after(opposite, state)
    far[2, True, False] = shift(opposite, flip_z=True)
    held = {(0, True, False): across, (2, False, False): opposite}
    everything.update(held)
    state = flash(held, cache_len, qt, state)

    beside, state = after(beside, state)
    everything.update(beside)
    state = flash(beside, cache_len, qt, state)

    far, state = after(far, state)
    everything.update(far)
    fresh, rows = fresh_rows(everything)
    twin_rows = shift(rows, flip_core=True)
    twin_part, own_part = flash_last(far, cache_len, qt, state, fresh)
    part = merge_pair(own_part, shift(twin_part, flip_core=True))
    parts = lax.all_to_all(part, "seg", 0, 0)
    cache_out = write_pages(cache_len, page_owner, cache_kv, rows, twin_rows)
    return merge(parts), cache_out


def solution(mesh):
    placed = (P("blk", None), P("blk", None), P(("seg", "blk"), None), P(), P())
    return jax.shard_map(
        on_device,
        mesh=mesh,
        in_specs=placed,
        out_specs=(P("blk", "seg"), P(("seg", "blk"), None)),
        check_vma=False,
    )
```

time: 61.7 us -> 56.7 us (0.919)
  waiting for transfers between devices: 14 us -> 8.26 us
  starting transfers between devices: 17.5 us -> 18.8 us
  local copies, waits for them, and re-layouts: 1.06 us -> 0.02 us
    ppermute x10, waiting for transfers between devices: 6.3 us -> 0.85 us  [shift(): return lax.ppermute(block, AXES, neighbours(-dx, flip_z, flip_core))]
    ppermute x10, starting transfers between devices: 13.3 us -> 14.6 us  [shift(): return lax.ppermute(block, AXES, neighbours(-dx, flip_z, flip_core))]
    unnamed x8 -> x6, local copies, waits for them, and re-layouts: 1.06 us -> 0.02 us
    pallas_call x4 -> x6, Pallas kernels: 23.5 us -> 23.5 us  [the longest x5 22.5 us: flash_call(): pl.pallas_call(kernel, in_specs=[first_spec] + [VMEM] * (len(operands) -...]
  transfers between devices with their start and end apart: 11 -> 11, of which waited for: 4 -> 3; matrix products, arithmetic and copies ran while one was open for 0% -> 0% of each run, Pallas kernels for 30% -> 38%
where the time goes in v3:
time: 56.7 us; the launch traced here: 56.2 us
  Pallas kernels  28.3 us (50%)
  starting transfers between devices  18.8 us (33%)
  waiting for transfers between devices  8.26 us (15%)
  between operations  0.8 us (1%)
    pallas_call x5, Pallas kernels, flash_call(): pl.pallas_call(kernel, in_specs=[first_spec] + [VMEM] * (len(operands) -...  22.5 us
    ppermute x10, starting transfers between devices, shift(): return lax.ppermute(block, AXES, neighbours(-dx, flip_z, flip_core))  14.6 us
    all_to_all x1, waiting for transfers between devices, on_device(): parts = lax.all_to_all(part, 'seg', 0, 0)  7.41 us
    all_to_all x1, starting transfers between devices, on_device(): parts = lax.all_to_all(part, 'seg', 0, 0)  4.2 us
    pallas_call x1, Pallas kernels, write_pages(): pl.pallas_call(pages_kernel, in_specs=[SMEM] + [VMEM] * 4, out_specs=VMEM...  2.04 us
    pallas_call x1, Pallas kernels, pack(): pl.pallas_call(pack_kernel, in_specs=[pl.BlockSpec(memory_space=pltpu.HBM...  1.23 us
  transfers between devices with their start and end apart: 11, of which 3 were waited for; matrix products, arithmetic and copies ran while one was open for 0% of the time, Pallas kernels for 38%

profile of v3, /device:TPU:1, one launch (start us, length us, event | category | flops | bytes accessed | tf_op | source)
XLA Modules:
  0.0 56.2 jit_solution(3019869988203436509)
XLA Ops:
  0.6 0.0 copy-start.2
  0.6 1.2 %pack.1 = (bf16[576,256]{1,0:T(8,128)(2,1)S(1)}, bf16[128,2048]{1,0:T(8,128)(2,1)S(1)}) custom-call(bf16[512,256]{1,0:T(8,128)(2,1)} %cache_ref.3, bf16[128,256]{1,0:T(8,128)(2,1)} %new_ref.1, bf16[128,2048]{1,0:T(8,128)(2,1)} %q_ref.1), custom_call_target="tpu_custom_call" | custom-call | tf_op jit(solution)/shard_map/pack/pallas_call | solution.py:84
  1.9 1.5 %collective-permute-start = (bf16[128,2048]{1,0:T(8,128)(2,1)S(1)}, bf16[128,2048]{1,0:T(8,128)(2,1)S(1)}, u32[]{:S(2)}, u32[]{:S(2)}) collective-permute-start(bf16[128,2048]{1,0:T(8,128)(2,1)S(1)} %get-tuple-element.30.own_ref), channel_id=1, source_target_pairs={{0,1},{1,0},{2,3},{3,2},{4,5},{5,4},{6,7},{7,6},{8,9},{9,8},{10,11... | collective-permute-start | bytes 1572872 | tf_op jit(solution)/shard_map/ppermute | solution.py:435
  3.4 3.9 %collective-permute-start.1 = (bf16[576,256]{1,0:T(8,128)(2,1)S(1)}, bf16[576,256]{1,0:T(8,128)(2,1)S(1)}, u32[]{:S(2)}, u32[]{:S(2)}) collective-permute-start(bf16[576,256]{1,0:T(8,128)(2,1)S(1)} %get-tuple-element.31.refs_2_.refs_0_), channel_id=1, source_target_pairs={{0,24},{1,25},{2,26},{3,27},{4,28},{5,29},{6,30},{7,31},{8,16},{9,... | collective-permute-start | bytes 884744 | tf_op jit(solution)/shard_map/ppermute | solution.py:435
  7.2 2.7 %collective-permute-start.4 = (bf16[576,256]{1,0:T(8,128)(2,1)S(1)}, bf16[576,256]{1,0:T(8,128)(2,1)S(1)}, u32[]{:S(2)}, u32[]{:S(2)}) collective-permute-start(bf16[576,256]{1,0:T(8,128)(2,1)S(1)} %get-tuple-element.31.refs_2_.refs_0_), channel_id=1, source_target_pairs={{0,4},{1,5},{2,6},{3,7},{4,0},{5,1},{6,2},{7,3},{8,12},{9,13},{10,... | collective-permute-start | bytes 884744 | tf_op jit(solution)/shard_map/ppermute | solution.py:435
  10.0 0.9 %collective-permute-start.7 = (bf16[576,256]{1,0:T(8,128)(2,1)S(1)}, bf16[576,256]{1,0:T(8,128)(2,1)S(1)}, u32[]{:S(2)}, u32[]{:S(2)}) collective-permute-start(bf16[576,256]{1,0:T(8,128)(2,1)S(1)} %get-tuple-element.31.refs_2_.refs_0_), channel_id=1, source_target_pairs={{0,6},{1,7},{2,0},{3,1},{4,2},{5,3},{6,4},{7,5},{8,14},{9,15},{10,... | collective-permute-start | bytes 884744 | tf_op jit(solution)/shard_map/ppermute | solution.py:435
  10.8 0.6 %collective-permute-start.6 = (bf16[576,256]{1,0:T(8,128)(2,1)S(1)}, bf16[576,256]{1,0:T(8,128)(2,1)S(1)}, u32[]{:S(2)}, u32[]{:S(2)}) collective-permute-start(bf16[576,256]{1,0:T(8,128)(2,1)S(1)} %get-tuple-element.31.refs_2_.refs_0_), channel_id=1, source_target_pairs={{0,2},{1,3},{2,4},{3,5},{4,6},{5,7},{6,0},{7,1},{8,10},{9,11},{10,... | collective-permute-start | bytes 884744 | tf_op jit(solution)/shard_map/ppermute | solution.py:435
  11.4 0.0 collective-permute-done.twin_ref
  11.4 0.6 %scaled_queries.1.refs_1_.qt_ref = bf16[256,4096]{1,0:T(8,128)(2,1)S(1)} custom-call(bf16[128,2048]{1,0:T(8,128)(2,1)S(1)} %collective-permute-done.twin_ref, bf16[128,2048]{1,0:T(8,128)(2,1)S(1)} %get-tuple-element.30.own_ref), custom_call_target="tpu_custom_call" | custom-call | tf_op jit(solution)/shard_map/scaled_queries/pallas_call | solution.py:443
  12.0 0.0 copy-done.2
  12.0 3.4 %flash_1.1 = (f32[8,4096]{1,0:T(8,128)S(1)}, f32[144,4096]{1,0:T(8,128)S(1)}) custom-call(s32[128]{0:T(128)S(1)} %copy-done.2, bf16[256,4096]{1,0:T(8,128)(2,1)S(1)} %scaled_queries.1.refs_1_.qt_ref, bf16[576,256]{1,0:T(8,128)(2,1)S(1)} %get-tuple-element.31.refs_2_.refs_0_), custom_call_target="tpu_custom_call" | custom-call | flops 2147483648 | bytes 1048576 | tf_op jit(solution)/shard_map/flash_1/pallas_call | solution.py:250
  15.5 0.0 collective-permute-done.1.refs_2_.refs_1_
  15.5 2.1 %collective-permute-start.3 = (bf16[576,256]{1,0:T(8,128)(2,1)S(1)}, bf16[576,256]{1,0:T(8,128)(2,1)S(1)}, u32[]{:S(2)}, u32[]{:S(2)}) collective-permute-start(bf16[576,256]{1,0:T(8,128)(2,1)S(1)} %collective-permute-done.1.refs_2_.refs_1_), channel_id=1, source_target_pairs={{0,6},{1,7},{2,0},{3,1},{4,2},{5,3},{6,4},{7,5},{8,14},{9,15},{10,... | collective-permute-start | bytes 884744 | tf_op jit(solution)/shard_map/ppermute | solution.py:435
  17.6 0.0 collective-permute-start.2
  17.6 0.0 collective-permute-done.4.refs_3_.refs_2_
  17.6 1.8 %collective-permute-start.5 = (bf16[576,256]{1,0:T(8,128)(2,1)S(1)}, bf16[576,256]{1,0:T(8,128)(2,1)S(1)}, u32[]{:S(2)}, u32[]{:S(2)}) collective-permute-start(bf16[576,256]{1,0:T(8,128)(2,1)S(1)} %collective-permute-done.4.refs_3_.refs_2_), channel_id=1, source_target_pairs={{0,24},{1,25},{2,26},{3,27},{4,28},{5,29},{6,30},{7,31},{8,16},{9,... | collective-permute-start | bytes 884744 | tf_op jit(solution)/shard_map/ppermute | solution.py:435
  19.5 5.0 %flash_2.2 = (f32[8,4096]{1,0:T(8,128)S(1)}, f32[144,4096]{1,0:T(8,128)S(1)}) custom-call(s32[128]{0:T(128)S(1)} %copy-done.2, bf16[256,4096]{1,0:T(8,128)(2,1)S(1)} %scaled_queries.1.refs_1_.qt_ref, bf16[576,256]{1,0:T(8,128)(2,1)S(1)} %collective-permute-done.1.refs_2_.refs_1_, bf16[576,256]{1,0:T(8,128)(2,1)S(1)} %collective-permute-done.4.refs_3_.refs_2_, ...), custom_call_target="tpu_custom_call" | custom-call | flops 3758096384 | bytes 1048576 | tf_op jit(solution)/shard_map/flash_2/pallas_call | solution.py:250
  24.5 0.0 collective-permute-done.7.refs_3_.refs_4_
  24.5 0.0 collective-permute-done.6.refs_2_.refs_3_
  24.5 5.0 %flash_2.3 = (f32[8,4096]{1,0:T(8,128)S(1)}, f32[144,4096]{1,0:T(8,128)S(1)}) custom-call(s32[128]{0:T(128)S(1)} %copy-done.2, bf16[256,4096]{1,0:T(8,128)(2,1)S(1)} %scaled_queries.1.refs_1_.qt_ref, bf16[576,256]{1,0:T(8,128)(2,1)S(1)} %collective-permute-done.6.refs_2_.refs_3_, bf16[576,256]{1,0:T(8,128)(2,1)S(1)} %collective-permute-done.7.refs_3_.refs_4_, ...), custom_call_target="tpu_custom_call" | custom-call | flops 3758096384 | bytes 1048576 | tf_op jit(solution)/shard_map/flash_2/pallas_call | solution.py:250
  29.5 0.0 collective-permute-done.5.refs_7_.refs_4_
  29.5 0.3 collective-permute-done.3.refs_6_.refs_3_
  29.7 0.6 %collective-permute-done.2.refs_5_.refs_2_ = bf16[576,256]{1,0:T(8,128)(2,1)S(1)} collective-permute-done((bf16[576,256]{1,0:T(8,128)(2,1)S(1)}, bf16[576,256]{1,0:T(8,128)(2,1)S(1)}, u32[]{:S(2)}, u32[]{:S(2)}) %collective-permute-start.2) | collective-permute-done | bytes 294944 | tf_op jit(solution)/shard_map/ppermute | solution.py:435
  30.3 0.1 fresh_rows.1
  30.4 4.9 %flash_twin.1 = (bf16[8,272,128]{2,1,0:T(8,128)(2,1)S(1)}, bf16[1536,256]{1,0:T(8,128)(2,1)S(1)}, bf16[144,1536]{1,0:T(8,128)(2,1)S(1)}) custom-call(s32[128]{0:T(128)S(1)} %copy-done.2, bf16[256,4096]{1,0:T(8,128)(2,1)S(1)} %scaled_queries.1.refs_1_.qt_ref, bf16[576,256]{1,0:T(8,128)(2,1)S(1)} %collective-permute-done.2.refs_5_.refs_2_, ...), custom_call_target="tpu_custom_call" | custom-call | flops 3221225472 | bytes 1048576 | tf_op jit(solution)/shard_map/flash_twin/pallas_call | solution.py:250
  35.3 0.7 %collective-permute-start.8 = (bf16[8,272,128]{2,1,0:T(8,128)(2,1)S(1)}, bf16[8,272,128]{2,1,0:T(8,128)(2,1)S(1)}, u32[]{:S(2)}, u32[]{:S(2)}) collective-permute-start(bf16[8,272,128]{2,1,0:T(8,128)(2,1)S(1)} %get-tuple-element.56), channel_id=1, source_target_pairs={{0,1},{1,0},{2,3},{3,2},{4,5},{5,4},{6,7},{7,6},{8,9},{9,8},{10,11... | collective-permute-start | bytes 1671176 | tf_op jit(solution)/shard_map/ppermute | solution.py:435
  36.1 0.3 collective-permute-start.9
  36.4 4.2 %flash_own.1.own_ref = bf16[8,272,128]{2,1,0:T(8,128)(2,1)S(1)} custom-call(bf16[256,4096]{1,0:T(8,128)(2,1)S(1)} %scaled_queries.1.refs_1_.qt_ref, bf16[1536,256]{1,0:T(8,128)(2,1)S(1)} %get-tuple-element.54.keys, bf16[144,1536]{1,0:T(8,128)(2,1)S(1)} %get-tuple-element.55.vals_t, f32[8,4096]{1,0:T(8,128)S(1)} %get-tuple-element.52.refs_6_.m_in, ...), custom_call_target="tpu_custom_call" | custom-call | flops 3221225472 | bytes 1048576 | tf_op jit(solution)/shard_map/flash_own/pallas_call | solution.py:250
  40.6 0.0 copy-start
  40.6 0.0 copy-start.1
  40.6 0.0 collective-permute-done.8.twin_ref
  40.6 1.0 %merge_pair.1 = bf16[8,272,128]{2,1,0:T(8,128)(2,1)} custom-call(bf16[8,272,128]{2,1,0:T(8,128)(2,1)S(1)} %flash_own.1.own_ref, bf16[8,272,128]{2,1,0:T(8,128)(2,1)S(1)} %collective-permute-done.8.twin_ref), custom_call_target="tpu_custom_call" | custom-call | tf_op jit(solution)/shard_map/merge_pair/pallas_call | solution.py:399
  41.7 4.2 %all-to-all-start = ((bf16[8,272,128]{2,1,0:T(8,128)(2,1)}), bf16[8,272,128]{2,1,0:T(8,128)(2,1)S(1)}, u32[]{:S(2)}, u32[]{:S(2)}) async-start(bf16[8,272,128]{2,1,0:T(8,128)(2,1)} %merge_pair.1), calls=%async_computation | async-start | bytes 1114112 | tf_op jit(solution)/shard_map/all_to_all | solution.py:481
  45.9 0.0 collective-permute-done.9.twin_ref
  45.9 0.0 copy-done
  45.9 0.0 copy-done.1
  45.9 2.0 %write_pages.1 = bf16[512,256]{1,0:T(8,128)(2,1)} custom-call(s32[128]{0:T(128)S(1)} %copy-done.2, s32[1,256]{1,0:T(1,128)S(1)} %bitcast.1, bf16[512,256]{1,0:T(8,128)(2,1)S(1)} %copy-done, bf16[1024,256]{1,0:T(8,128)(2,1)S(1)} %get-tuple-element.57.own_ref, bf16[1024,256]{1,0:T(8,128)(2,1)S(1)} %collective-permute-done.9.twin_ref), custom_call_target="tpu_custom_call" | custom-call | flops 1000000000 | bytes 2097152 | tf_op jit(solution)/shard_map/write_pages/pallas_call | solution.py:366
  47.9 7.4 %all-to-all-done.parts_ref = bf16[8,272,128]{2,1,0:T(8,128)(2,1)S(1)} async-done(((bf16[8,272,128]{2,1,0:T(8,128)(2,1)}), bf16[8,272,128]{2,1,0:T(8,128)(2,1)S(1)}, u32[]{:S(2)}, u32[]{:S(2)}) %all-to-all-start) | async-done | bytes 557088 | tf_op jit(solution)/shard_map/all_to_all | solution.py:481
  55.3 0.8 %merge.1 = bf16[128,256]{1,0:T(8,128)(2,1)} custom-call(bf16[8,272,128]{2,1,0:T(8,128)(2,1)S(1)} %all-to-all-done.parts_ref), custom_call_target="tpu_custom_call" | custom-call | tf_op jit(solution)/shard_map/merge/pallas_call | solution.py:424
Async XLA Ops:
  0.6 11.4 %copy-start.2 = (s32[128]{0:T(128)S(1)}, s32[128]{0:T(128)}, u32[]{:S(2)}) copy-start(s32[128]{0:T(128)} %len_ref.1) | copy-start | bytes 1540
  1.9 9.6 %collective-permute-start = (bf16[128,2048]{1,0:T(8,128)(2,1)S(1)}, bf16[128,2048]{1,0:T(8,128)(2,1)S(1)}, u32[]{:S(2)}, u32[]{:S(2)}) collective-permute-start(bf16[128,2048]{1,0:T(8,128)(2,1)S(1)} %get-tuple-element.30.own_ref), channel_id=1, source_target_pairs={{0,1},{1,0},{2,3},{3,2},{4,5},{5,4},{6,7},{7,6},{8,9},{9,8},{10,11... | collective-permute-start | bytes 1572872 | tf_op jit(solution)/shard_map/ppermute | solution.py:435
  3.4 12.1 %collective-permute-start.1 = (bf16[576,256]{1,0:T(8,128)(2,1)S(1)}, bf16[576,256]{1,0:T(8,128)(2,1)S(1)}, u32[]{:S(2)}, u32[]{:S(2)}) collective-permute-start(bf16[576,256]{1,0:T(8,128)(2,1)S(1)} %get-tuple-element.31.refs_2_.refs_0_), channel_id=1, source_target_pairs={{0,24},{1,25},{2,26},{3,27},{4,28},{5,29},{6,30},{7,31},{8,16},{9,... | collective-permute-start | bytes 884744 | tf_op jit(solution)/shard_map/ppermute | solution.py:435
  7.2 10.4 %collective-permute-start.4 = (bf16[576,256]{1,0:T(8,128)(2,1)S(1)}, bf16[576,256]{1,0:T(8,128)(2,1)S(1)}, u32[]{:S(2)}, u32[]{:S(2)}) collective-permute-start(bf16[576,256]{1,0:T(8,128)(2,1)S(1)} %get-tuple-element.31.refs_2_.refs_0_), channel_id=1, source_target_pairs={{0,4},{1,5},{2,6},{3,7},{4,0},{5,1},{6,2},{7,3},{8,12},{9,13},{10,... | collective-permute-start | bytes 884744 | tf_op jit(solution)/shard_map/ppermute | solution.py:435
  10.0 14.5 %collective-permute-start.7 = (bf16[576,256]{1,0:T(8,128)(2,1)S(1)}, bf16[576,256]{1,0:T(8,128)(2,1)S(1)}, u32[]{:S(2)}, u32[]{:S(2)}) collective-permute-start(bf16[576,256]{1,0:T(8,128)(2,1)S(1)} %get-tuple-element.31.refs_2_.refs_0_), channel_id=1, source_target_pairs={{0,6},{1,7},{2,0},{3,1},{4,2},{5,3},{6,4},{7,5},{8,14},{9,15},{10,... | collective-permute-start | bytes 884744 | tf_op jit(solution)/shard_map/ppermute | solution.py:435
  10.8 13.7 %collective-permute-start.6 = (bf16[576,256]{1,0:T(8,128)(2,1)S(1)}, bf16[576,256]{1,0:T(8,128)(2,1)S(1)}, u32[]{:S(2)}, u32[]{:S(2)}) collective-permute-start(bf16[576,256]{1,0:T(8,128)(2,1)S(1)} %get-tuple-element.31.refs_2_.refs_0_), channel_id=1, source_target_pairs={{0,2},{1,3},{2,4},{3,5},{4,6},{5,7},{6,0},{7,1},{8,10},{9,11},{10,... | collective-permute-start | bytes 884744 | tf_op jit(solution)/shard_map/ppermute | solution.py:435
  15.5 14.2 %collective-permute-start.3 = (bf16[576,256]{1,0:T(8,128)(2,1)S(1)}, bf16[576,256]{1,0:T(8,128)(2,1)S(1)}, u32[]{:S(2)}, u32[]{:S(2)}) collective-permute-start(bf16[576,256]{1,0:T(8,128)(2,1)S(1)} %collective-permute-done.1.refs_2_.refs_1_), channel_id=1, source_target_pairs={{0,6},{1,7},{2,0},{3,1},{4,2},{5,3},{6,4},{7,5},{8,14},{9,15},{10,... | collective-permute-start | bytes 884744 | tf_op jit(solution)/shard_map/ppermute | solution.py:435
  17.6 12.7 %collective-permute-start.2 = (bf16[576,256]{1,0:T(8,128)(2,1)S(1)}, bf16[576,256]{1,0:T(8,128)(2,1)S(1)}, u32[]{:S(2)}, u32[]{:S(2)}) collective-permute-start(bf16[576,256]{1,0:T(8,128)(2,1)S(1)} %collective-permute-done.1.refs_2_.refs_1_), channel_id=1, source_target_pairs={{0,2},{1,3},{2,4},{3,5},{4,6},{5,7},{6,0},{7,1},{8,10},{9,11},{10,... | collective-permute-start | bytes 884744 | tf_op jit(solution)/shard_map/ppermute | solution.py:435
  17.6 11.8 %collective-permute-start.5 = (bf16[576,256]{1,0:T(8,128)(2,1)S(1)}, bf16[576,256]{1,0:T(8,128)(2,1)S(1)}, u32[]{:S(2)}, u32[]{:S(2)}) collective-permute-start(bf16[576,256]{1,0:T(8,128)(2,1)S(1)} %collective-permute-done.4.refs_3_.refs_2_), channel_id=1, source_target_pairs={{0,24},{1,25},{2,26},{3,27},{4,28},{5,29},{6,30},{7,31},{8,16},{9,... | collective-permute-start | bytes 884744 | tf_op jit(solution)/shard_map/ppermute | solution.py:435
  35.3 5.3 %collective-permute-start.8 = (bf16[8,272,128]{2,1,0:T(8,128)(2,1)S(1)}, bf16[8,272,128]{2,1,0:T(8,128)(2,1)S(1)}, u32[]{:S(2)}, u32[]{:S(2)}) collective-permute-start(bf16[8,272,128]{2,1,0:T(8,128)(2,1)S(1)} %get-tuple-element.56), channel_id=1, source_target_pairs={{0,1},{1,0},{2,3},{3,2},{4,5},{5,4},{6,7},{7,6},{8,9},{9,8},{10,11... | collective-permute-start | bytes 1671176 | tf_op jit(solution)/shard_map/ppermute | solution.py:435
  36.1 9.8 %collective-permute-start.9 = (bf16[1024,256]{1,0:T(8,128)(2,1)S(1)}, bf16[1024,256]{1,0:T(8,128)(2,1)S(1)}, u32[]{:S(2)}, u32[]{:S(2)}) collective-permute-start(bf16[1024,256]{1,0:T(8,128)(2,1)S(1)} %get-tuple-element.57.own_ref), channel_id=1, source_target_pairs={{0,1},{1,0},{2,3},{3,2},{4,5},{5,4},{6,7},{7,6},{8,9},{9,8},{10,11... | collective-permute-start | bytes 1572872 | tf_op jit(solution)/shard_map/ppermute | solution.py:435
  40.6 5.3 %copy-start = (bf16[512,256]{1,0:T(8,128)(2,1)S(1)}, bf16[512,256]{1,0:T(8,128)(2,1)}, u32[]{:S(2)}) copy-start(bf16[512,256]{1,0:T(8,128)(2,1)} %cache_ref.3) | copy-start | bytes 786436
  40.6 5.3 %copy-start.1 = (s32[256,1]{0,1:T(1,128)S(1)}, s32[256,1]{0,1:T(1,128)}, u32[]{:S(2)}) copy-start(s32[256,1]{0,1:T(1,128)} %param.9) | copy-start | bytes 3076
  41.7 13.7 %all-to-all-start = ((bf16[8,272,128]{2,1,0:T(8,128)(2,1)}), bf16[8,272,128]{2,1,0:T(8,128)(2,1)S(1)}, u32[]{:S(2)}, u32[]{:S(2)}) async-start(bf16[8,272,128]{2,1,0:T(8,128)(2,1)} %merge_pair.1), calls=%async_computation | async-start | bytes 1114112 | tf_op jit(solution)/shard_map/all_to_all | solution.py:481

commit v4 on v3

--- a/solution.py
+++ b/solution.py
@@ -16,6 +16,7 @@
 ROWS = 2 * HEADS * TOK
 PART = HEADS * TOK
 SLOTS = 512
+LEAST = 256
 FILL = 448
 PAGE = 8
 NSEG = 8
@@ -29,6 +30,7 @@
 VMEM = pl.BlockSpec(memory_space=pltpu.VMEM)
 SMEM = pl.BlockSpec(memory_space=pltpu.SMEM)
 AXES = ("seg", "blk")
+SLOT_ORDER = [(dx, flip_z, False) for flip_z in (False, True) for dx in (0, 1, -1, 2)]
 
 
 def neighbours(dx=0, flip_z=False, flip_core=False):
@@ -68,59 +70,77 @@
     return pltpu.with_memory_space_constraint(array, pltpu.HBM)
 
 
-def pack_kernel(cache_ref, new_ref, q_ref, out_ref, q_out, sems):
+def pack_kernel(cache_ref, new_ref, q_ref, len_ref, out_ref, q_out, filled_ref, len_copy, sems):
     copies = [
         pltpu.make_async_copy(cache_ref.at[0:FILL], out_ref.at[0:FILL], sems.at[0]),
         pltpu.make_async_copy(new_ref, out_ref.at[FILL : FILL + TOK], sems.at[1]),
         pltpu.make_async_copy(q_ref, q_out, sems.at[2]),
+        pltpu.make_async_copy(len_ref, len_copy, sems.at[3]),
     ]
     for copy in copies:
         copy.start()
-    for copy in copies:
+    for copy in reversed(copies):
         copy.wait()
-
-
-def pack(cache_kv, new_kv, queries):
+    for j, slot in enumerate(SLOT_ORDER):
+        filled_ref[j : j + 1, :] = jnp.full((1, 128), len_copy[origin(slot)], jnp.int32)
+
+
+def pack(cache_kv, new_kv, queries, cache_len):
     return pl.pallas_call(
         pack_kernel,
-        in_specs=[pl.BlockSpec(memory_space=pltpu.HBM)] * 3,
-        out_specs=[VMEM, VMEM],
+        in_specs=[pl.BlockSpec(memory_space=pltpu.HBM)] * 4,
+        out_specs=[VMEM] * 3,
         out_shape=[
             jax.ShapeDtypeStruct((FILL + TOK, 2 * HD), BF16),
             jax.ShapeDtypeStruct(queries.shape, BF16),
+            jax.ShapeDtypeStruct((len(SLOT_ORDER), 128), jnp.int32),
         ],
-        scratch_shapes=[pltpu.SemaphoreType.DMA((3,))],
+        scratch_shapes=[pltpu.SMEM(cache_len.shape, jnp.int32), pltpu.SemaphoreType.DMA((4,))],
         compiler_params=pltpu.CompilerParams(vmem_limit_bytes=1 << 20),
         name="pack",
-    )(in_hbm(cache_kv), in_hbm(new_kv), in_hbm(queries))
-
-
-def gather_keys(slots, blocks, fresh_ref, len_ref, keys, vals, vals_t):
+    )(*map(in_hbm, (cache_kv, new_kv, queries, cache_len)))
+
+
+def gather_keys(slots, blocks, fresh_ref, filled_ref, keys, vals, vals_t):
     total = keys.shape[0]
+    spans = []
     for j, (slot, which) in enumerate(slots):
-        ok = lax.broadcasted_iota(jnp.int32, (FILL, HD), 0) < len_ref[origin(slot)]
-        key = blocks[which][0:FILL, 0:HD]
-        value = blocks[which][0:FILL, HD : 2 * HD]
-        key = jnp.where(ok, key, jnp.broadcast_to(key[0:1], (FILL, HD)))
-        rows = slice(j * FILL, (j + 1) * FILL)
-        keys[rows, 0:HD] = key
-        keys[rows, HD : 2 * HD] = key
-        vals[rows, 0:HD] = jnp.where(ok, value, jnp.zeros_like(value))
-        vals[rows, HD : 2 * HD] = ok.astype(BF16)
+        filled = filled_ref[SLOT_ORDER.index(slot) : SLOT_ORDER.index(slot) + 1, :]
+        block, start = blocks[which], j * FILL
+        ok = lax.broadcasted_iota(jnp.int32, (FILL - LEAST, HD), 0) < filled - LEAST
+        head = block[0:LEAST, 0:HD]
+        tail = block[LEAST:FILL, 0:HD]
+        tail = jnp.where(ok, tail, jnp.broadcast_to(head[0:1], tail.shape))
+        value = block[LEAST:FILL, HD : 2 * HD]
+        for lanes in (slice(0, HD), slice(HD, 2 * HD)):
+            keys[start : start + LEAST, lanes] = head
+            keys[start + LEAST : start + FILL, lanes] = tail
+        vals[start : start + LEAST, :] = block[0:LEAST, HD : 2 * HD]
+        vals[start + LEAST : start + FILL, :] = jnp.where(ok, value, jnp.zeros_like(value))
+        spans.append((start, start + LEAST, start + FILL, start + filled))
     old = used = len(slots) * FILL
     if fresh_ref is not None:
         used = old + fresh_ref.shape[0]
         keys[old:used, 0:HD] = fresh_ref[:, 0:HD]
         keys[old:used, HD : 2 * HD] = fresh_ref[:, 0:HD]
-        vals[old:used, 0:HD] = fresh_ref[:, HD : 2 * HD]
-        vals[old:used, HD : 2 * HD] = jnp.ones((used - old, HD), BF16)
+        vals[old:used, :] = fresh_ref[:, HD : 2 * HD]
+        spans.append((old, used, used, used))
     if total > used:
         keys[used:total, :] = jnp.broadcast_to(keys[0:1, :], (total - used, 2 * HD))
-        vals[used:total, :] = jnp.zeros((total - used, 2 * HD), BF16)
+        vals[used:total, :] = jnp.zeros((total - used, HD), BF16)
     for c in range(total // 128):
-        rows = slice(c * 128, (c + 1) * 128)
-        vals_t[0:HD, rows] = vals[rows, 0:HD].T
-        vals_t[HD:ACC, rows] = vals[rows, HD : 2 * HD].T[0 : ACC - HD]
+        low, high = c * 128, (c + 1) * 128
+        vals_t[0:HD, low:high] = vals[low:high, :].T
+        if any(start <= low and high <= sure for start, sure, _, _ in spans):
+            vals_t[HD:ACC, low:high] = jnp.ones((ACC - HD, 128), BF16)
+            continue
+        lane = lax.broadcasted_iota(jnp.int32, (ACC - HD, 128), 1) + low
+        one = None
+        for start, _, stop, filled in spans:
+            if start < high and stop > low:
+                inside = (lane >= start) & (lane < filled)
+                one = inside if one is None else one | inside
+        vals_t[HD:ACC, low:high] = one.astype(F32).astype(BF16)
 
 
 def flash_columns(columns, old, keys, vals_t, qt_ref, state, even_ref, odd_ref, query_blk, emit):
@@ -165,15 +185,16 @@
         return weigh(first + 2 * i + 1, tops, odd_ref, even_ref if more else None)
 
     pairs = (last - first) // 2
-    tops = lax.fori_loop(0, pairs - 1, two, score(first, even_ref))
+    trips = jnp.minimum(lax.axis_index("seg") + pairs - 1, pairs - 1)
+    tops = lax.fori_loop(0, trips, two, score(first, even_ref))
     two(pairs - 1, tops, False)
 
 
 def flash_kernel(slots, operand_count, *refs):
-    len_ref, qt_ref = refs[0], refs[1]
+    filled_ref, qt_ref = refs[0], refs[1]
     blocks, refs = refs[2 : 2 + operand_count], refs[2 + operand_count :]
     state, (m_ref, acc_ref, keys, vals, vals_t, even_ref, odd_ref) = refs[:-7] or None, refs[-7:]
-    gather_keys(slots, blocks, None, len_ref, keys, vals, vals_t)
+    gather_keys(slots, blocks, None, filled_ref, keys, vals, vals_t)
 
     def emit(r, cols, out, top):
         acc_ref[:, cols] = out
@@ -212,10 +233,10 @@
 
 
 def twin_kernel(slots, operand_count, *refs):
-    len_ref, qt_ref = refs[0], refs[1]
+    filled_ref, qt_ref = refs[0], refs[1]
     blocks, refs = refs[2 : 2 + operand_count], refs[2 + operand_count :]
     fresh_ref, m_in, acc_in, part_ref, keys, vals_t, vals, even_ref, odd_ref = refs
-    gather_keys(slots, blocks, fresh_ref, len_ref, keys, vals, vals_t)
+    gather_keys(slots, blocks, fresh_ref, filled_ref, keys, vals, vals_t)
     blk = lax.axis_index("blk")
     flash_columns(
         (0, PART),
@@ -246,10 +267,10 @@
     )
 
 
-def flash_call(kernel, operands, first_spec, out_shape, scratch, total, rows, name, width=WIDTH):
+def flash_call(kernel, operands, out_shape, scratch, total, rows, name, width=WIDTH):
     return pl.pallas_call(
         kernel,
-        in_specs=[first_spec] + [VMEM] * (len(operands) - 1),
+        in_specs=[VMEM] * len(operands),
         out_specs=jax.tree.map(lambda _: VMEM, out_shape),
         out_shape=out_shape,
         scratch_shapes=scratch + [pltpu.VMEM((total, width), F32)] * 2,
@@ -261,17 +282,16 @@
     )(*operands)
 
 
-def flash(held, cache_len, qt, state):
+def flash(held, filled, qt, state):
     slots, blocks = indexed(held)
     total = -(-len(slots) * FILL // 128) * 128
     return flash_call(
         functools.partial(flash_kernel, slots, len(blocks)),
-        [cache_len, qt, *blocks, *(state or ())],
-        SMEM,
+        [filled, qt, *blocks, *(state or ())],
         [jax.ShapeDtypeStruct((8, ROWS), F32), jax.ShapeDtypeStruct((ACC, ROWS), F32)],
         [
             pltpu.VMEM((total, 2 * HD), BF16),
-            pltpu.VMEM((total, 2 * HD), BF16),
+            pltpu.VMEM((total, HD), BF16),
             pltpu.VMEM((ACC, total), BF16),
         ],
         total,
@@ -280,23 +300,22 @@
     )
 
 
-def flash_last(held, cache_len, qt, state, fresh):
+def flash_last(held, filled, qt, state, fresh):
     slots, blocks = indexed(held)
     old = len(slots) * FILL
     total = -(-(old + fresh.shape[0]) // 128) * 128
     part = jax.ShapeDtypeStruct((NSEG, CHUNK, TOK), BF16)
     twin_part, keys, vals_t = flash_call(
         functools.partial(twin_kernel, slots, len(blocks)),
-        [cache_len, qt, *blocks, fresh, *state],
-        SMEM,
+        [filled, qt, *blocks, fresh, *state],
         [part, jax.ShapeDtypeStruct((total, 2 * HD), BF16), jax.ShapeDtypeStruct((ACC, total), BF16)],
-        [pltpu.VMEM((total, 2 * HD), BF16)],
+        [pltpu.VMEM((total, HD), BF16)],
         total,
         PART,
         "flash_twin",
     )
     own_part = flash_call(
-        functools.partial(own_kernel, old), [qt, keys, vals_t, *state], VMEM, part, [], total, PART, "flash_own"
+        functools.partial(own_kernel, old), [qt, keys, vals_t, *state], part, [], total, PART, "flash_own"
     )
     return twin_part, own_part
 
@@ -451,14 +470,14 @@
 
 
 def on_device(queries, new_kv, cache_kv, cache_len, page_owner):
-    own, own_queries = pack(cache_kv, new_kv, queries)
+    own, own_queries, filled = pack(cache_kv, new_kv, queries, cache_len)
     across = shift(own, flip_z=True)
     opposite = shift(own, 2)
     beside = {(1, False, False): shift(own, 1), (-1, False, False): shift(own, -1)}
     qt = scaled_queries(shift(own_queries, flip_core=True), own_queries)
     held = {(0, False, False): own}
     everything = dict(held)
-    state = flash(held, cache_len, qt, None)
+    state = flash(held, filled, qt, None)
 
     across, state = after(across, state)
     far = {(1, True, False): shift(across, 1), (-1, True, False): shift(across, -1)}
@@ -466,17 +485,17 @@
     far[2, True, False] = shift(opposite, flip_z=True)
     held = {(0, True, False): across, (2, False, False): opposite}
     everything.update(held)
-    state = flash(held, cache_len, qt, state)
+    state = flash(held, filled, qt, state)
 
     beside, state = after(beside, state)
     everything.update(beside)
-    state = flash(beside, cache_len, qt, state)
+    state = flash(beside, filled, qt, state)
 
     far, state = after(far, state)
     everything.update(far)
     fresh, rows = fresh_rows(everything)
     twin_rows = shift(rows, flip_core=True)
-    twin_part, own_part = flash_last(far, cache_len, qt, state, fresh)
+    twin_part, own_part = flash_last(far, filled, qt, state, fresh)
     part = merge_pair(own_part, shift(twin_part, flip_core=True))
     parts = lax.all_to_all(part, "seg", 0, 0)
     cache_out = write_pages(cache_len, page_owner, cache_kv, rows, twin_rows)

time: 56.7 us -> 55.2 us (0.974)
  Pallas kernels: 28.3 us -> 25.6 us
  waiting for transfers between devices: 8.26 us -> 9.46 us
    pallas_call x5, Pallas kernels: 22.5 us -> 19.8 us  [flash_call(): pl.pallas_call(kernel, in_specs=[VMEM] * len(operands), out_specs=jax.tre...]
    ppermute x10, waiting for transfers between devices: 0.85 us -> 2.04 us  [shift(): return lax.ppermute(block, AXES, neighbours(-dx, flip_z, flip_core))]
  transfers between devices with their start and end apart: 11 -> 11, of which waited for: 3 -> 4; matrix products, arithmetic and copies ran while one was open for 0% -> 0% of each run, Pallas kernels for 38% -> 35%
where the time goes in v4:
time: 55.2 us; the launch traced here: 55 us
  Pallas kernels  25.6 us (46%)
  starting transfers between devices  19.1 us (35%)
  waiting for transfers between devices  9.46 us (17%)
  between operations  0.78 us (1%)
    pallas_call x5, Pallas kernels, flash_call(): pl.pallas_call(kernel, in_specs=[VMEM] * len(operands), out_specs=jax.tre...  19.8 us
    ppermute x10, starting transfers between devices, shift(): return lax.ppermute(block, AXES, neighbours(-dx, flip_z, flip_core))  14.9 us
    all_to_all x1, waiting for transfers between devices, on_device(): parts = lax.all_to_all(part, 'seg', 0, 0)  7.42 us
    all_to_all x1, starting transfers between devices, on_device(): parts = lax.all_to_all(part, 'seg', 0, 0)  4.2 us
    pallas_call x1, Pallas kernels, write_pages(): pl.pallas_call(pages_kernel, in_specs=[SMEM] + [VMEM] * 4, out_specs=VMEM...  2.04 us
    ppermute x10, waiting for transfers between devices, shift(): return lax.ppermute(block, AXES, neighbours(-dx, flip_z, flip_core))  2.04 us
    pallas_call x1, Pallas kernels, pack(): pl.pallas_call(pack_kernel, in_specs=[pl.BlockSpec(memory_space=pltpu.HBM...  1.24 us
  transfers between devices with their start and end apart: 11, of which 4 were waited for; matrix products, arithmetic and copies ran while one was open for 0% of the time, Pallas kernels for 35%

profile of v4, /device:TPU:1, one launch (start us, length us, event | category | flops | bytes accessed | tf_op | source)
XLA Modules:
  0.0 55.0 jit_solution(14096098259311041533)
XLA Ops:
  0.6 1.2 %pack.1 = (bf16[576,256]{1,0:T(8,128)(2,1)S(1)}, bf16[128,2048]{1,0:T(8,128)(2,1)S(1)}, s32[8,128]{1,0:T(8,128)S(1)}) custom-call(bf16[512,256]{1,0:T(8,128)(2,1)} %cache_ref.3, bf16[128,256]{1,0:T(8,128)(2,1)} %new_ref.1, bf16[128,2048]{1,0:T(8,128)(2,1)} %q_ref.1, s32[128]{0:T(128)} %len_ref.3), custom_call_target="tpu_custom_call" | custom-call | tf_op jit(solution)/shard_map/pack/pallas_call | solution.py:89
  1.9 1.5 %collective-permute-start = (bf16[128,2048]{1,0:T(8,128)(2,1)S(1)}, bf16[128,2048]{1,0:T(8,128)(2,1)S(1)}, u32[]{:S(2)}, u32[]{:S(2)}) collective-permute-start(bf16[128,2048]{1,0:T(8,128)(2,1)S(1)} %get-tuple-element.31.own_ref), channel_id=1, source_target_pairs={{0,1},{1,0},{2,3},{3,2},{4,5},{5,4},{6,7},{7,6},{8,9},{9,8},{10,11... | collective-permute-start | bytes 1572872 | tf_op jit(solution)/shard_map/ppermute | solution.py:454
  3.4 3.9 %collective-permute-start.1 = (bf16[576,256]{1,0:T(8,128)(2,1)S(1)}, bf16[576,256]{1,0:T(8,128)(2,1)S(1)}, u32[]{:S(2)}, u32[]{:S(2)}) collective-permute-start(bf16[576,256]{1,0:T(8,128)(2,1)S(1)} %get-tuple-element.33.refs_2_.refs_0_), channel_id=1, source_target_pairs={{0,24},{1,25},{2,26},{3,27},{4,28},{5,29},{6,30},{7,31},{8,16},{9,... | collective-permute-start | bytes 884744 | tf_op jit(solution)/shard_map/ppermute | solution.py:454
  7.2 2.7 %collective-permute-start.4 = (bf16[576,256]{1,0:T(8,128)(2,1)S(1)}, bf16[576,256]{1,0:T(8,128)(2,1)S(1)}, u32[]{:S(2)}, u32[]{:S(2)}) collective-permute-start(bf16[576,256]{1,0:T(8,128)(2,1)S(1)} %get-tuple-element.33.refs_2_.refs_0_), channel_id=1, source_target_pairs={{0,4},{1,5},{2,6},{3,7},{4,0},{5,1},{6,2},{7,3},{8,12},{9,13},{10,... | collective-permute-start | bytes 884744 | tf_op jit(solution)/shard_map/ppermute | solution.py:454
  10.0 0.9 %collective-permute-start.7 = (bf16[576,256]{1,0:T(8,128)(2,1)S(1)}, bf16[576,256]{1,0:T(8,128)(2,1)S(1)}, u32[]{:S(2)}, u32[]{:S(2)}) collective-permute-start(bf16[576,256]{1,0:T(8,128)(2,1)S(1)} %get-tuple-element.33.refs_2_.refs_0_), channel_id=1, source_target_pairs={{0,6},{1,7},{2,0},{3,1},{4,2},{5,3},{6,4},{7,5},{8,14},{9,15},{10,... | collective-permute-start | bytes 884744 | tf_op jit(solution)/shard_map/ppermute | solution.py:454
  10.8 0.6 %collective-permute-start.6 = (bf16[576,256]{1,0:T(8,128)(2,1)S(1)}, bf16[576,256]{1,0:T(8,128)(2,1)S(1)}, u32[]{:S(2)}, u32[]{:S(2)}) collective-permute-start(bf16[576,256]{1,0:T(8,128)(2,1)S(1)} %get-tuple-element.33.refs_2_.refs_0_), channel_id=1, source_target_pairs={{0,2},{1,3},{2,4},{3,5},{4,6},{5,7},{6,0},{7,1},{8,10},{9,11},{10,... | collective-permute-start | bytes 884744 | tf_op jit(solution)/shard_map/ppermute | solution.py:454
  11.4 0.0 collective-permute-done.twin_ref
  11.5 0.6 %scaled_queries.1.refs_1_.qt_ref = bf16[256,4096]{1,0:T(8,128)(2,1)S(1)} custom-call(bf16[128,2048]{1,0:T(8,128)(2,1)S(1)} %collective-permute-done.twin_ref, bf16[128,2048]{1,0:T(8,128)(2,1)S(1)} %get-tuple-element.31.own_ref), custom_call_target="tpu_custom_call" | custom-call | tf_op jit(solution)/shard_map/scaled_queries/pallas_call | solution.py:462
  12.0 2.9 %flash_1.1 = (f32[8,4096]{1,0:T(8,128)S(1)}, f32[144,4096]{1,0:T(8,128)S(1)}) custom-call(s32[8,128]{1,0:T(8,128)S(1)} %get-tuple-element.32.refs_0_, bf16[256,4096]{1,0:T(8,128)(2,1)S(1)} %scaled_queries.1.refs_1_.qt_ref, bf16[576,256]{1,0:T(8,128)(2,1)S(1)} %get-tuple-element.33.refs_2_.refs_0_), custom_call_target="tpu_custom_call" | custom-call | flops 2147483648 | bytes 1048576 | tf_op jit(solution)/shard_map/flash_1/pallas_call | solution.py:271
  14.9 0.0 collective-permute-done.1.refs_2_.refs_1_
  14.9 2.1 %collective-permute-start.3 = (bf16[576,256]{1,0:T(8,128)(2,1)S(1)}, bf16[576,256]{1,0:T(8,128)(2,1)S(1)}, u32[]{:S(2)}, u32[]{:S(2)}) collective-permute-start(bf16[576,256]{1,0:T(8,128)(2,1)S(1)} %collective-permute-done.1.refs_2_.refs_1_), channel_id=1, source_target_pairs={{0,6},{1,7},{2,0},{3,1},{4,2},{5,3},{6,4},{7,5},{8,14},{9,15},{10,... | collective-permute-start | bytes 884744 | tf_op jit(solution)/shard_map/ppermute | solution.py:454
  17.1 0.0 collective-permute-start.2
  17.1 0.0 collective-permute-done.4.refs_3_.refs_2_
  17.1 2.4 %collective-permute-start.5 = (bf16[576,256]{1,0:T(8,128)(2,1)S(1)}, bf16[576,256]{1,0:T(8,128)(2,1)S(1)}, u32[]{:S(2)}, u32[]{:S(2)}) collective-permute-start(bf16[576,256]{1,0:T(8,128)(2,1)S(1)} %collective-permute-done.4.refs_3_.refs_2_), channel_id=1, source_target_pairs={{0,24},{1,25},{2,26},{3,27},{4,28},{5,29},{6,30},{7,31},{8,16},{9,... | collective-permute-start | bytes 884744 | tf_op jit(solution)/shard_map/ppermute | solution.py:454
  19.5 4.4 %flash_2.2 = (f32[8,4096]{1,0:T(8,128)S(1)}, f32[144,4096]{1,0:T(8,128)S(1)}) custom-call(s32[8,128]{1,0:T(8,128)S(1)} %get-tuple-element.32.refs_0_, bf16[256,4096]{1,0:T(8,128)(2,1)S(1)} %scaled_queries.1.refs_1_.qt_ref, bf16[576,256]{1,0:T(8,128)(2,1)S(1)} %collective-permute-done.1.refs_2_.refs_1_, ...), custom_call_target="tpu_custom_call" | custom-call | flops 3758096384 | bytes 1048576 | tf_op jit(solution)/shard_map/flash_2/pallas_call | solution.py:271
  23.9 0.0 collective-permute-done.7.refs_3_.refs_4_
  23.9 0.1 collective-permute-done.6.refs_2_.refs_3_
  24.0 4.4 %flash_2.3 = (f32[8,4096]{1,0:T(8,128)S(1)}, f32[144,4096]{1,0:T(8,128)S(1)}) custom-call(s32[8,128]{1,0:T(8,128)S(1)} %get-tuple-element.32.refs_0_, bf16[256,4096]{1,0:T(8,128)(2,1)S(1)} %scaled_queries.1.refs_1_.qt_ref, bf16[576,256]{1,0:T(8,128)(2,1)S(1)} %collective-permute-done.6.refs_2_.refs_3_, ...), custom_call_target="tpu_custom_call" | custom-call | flops 3758096384 | bytes 1048576 | tf_op jit(solution)/shard_map/flash_2/pallas_call | solution.py:271
  28.4 0.0 collective-permute-done.5.refs_7_.refs_4_
  28.4 1.4 %collective-permute-done.3.refs_6_.refs_3_ = bf16[576,256]{1,0:T(8,128)(2,1)S(1)} collective-permute-done((bf16[576,256]{1,0:T(8,128)(2,1)S(1)}, bf16[576,256]{1,0:T(8,128)(2,1)S(1)}, u32[]{:S(2)}, u32[]{:S(2)}) %collective-permute-start.3) | collective-permute-done | bytes 294944 | tf_op jit(solution)/shard_map/ppermute | solution.py:454
  29.7 0.6 %collective-permute-done.2.refs_5_.refs_2_ = bf16[576,256]{1,0:T(8,128)(2,1)S(1)} collective-permute-done((bf16[576,256]{1,0:T(8,128)(2,1)S(1)}, bf16[576,256]{1,0:T(8,128)(2,1)S(1)}, u32[]{:S(2)}, u32[]{:S(2)}) %collective-permute-start.2) | collective-permute-done | bytes 294944 | tf_op jit(solution)/shard_map/ppermute | solution.py:454
  30.3 0.1 fresh_rows.1
  30.4 4.2 %flash_twin.1 = (bf16[8,272,128]{2,1,0:T(8,128)(2,1)S(1)}, bf16[1536,256]{1,0:T(8,128)(2,1)S(1)}, bf16[144,1536]{1,0:T(8,128)(2,1)S(1)}) custom-call(s32[8,128]{1,0:T(8,128)S(1)} %get-tuple-element.32.refs_0_, bf16[256,4096]{1,0:T(8,128)(2,1)S(1)} %scaled_queries.1.refs_1_.qt_ref, bf16[576,256]{1,0:T(8,128)(2,1)S(1)} %collective-permute-done.2.refs_5_.refs_2_, ...), custom_call_target="tpu_custom_call" | custom-call | flops 3221225472 | bytes 1048576 | tf_op jit(solution)/shard_map/flash_twin/pallas_call | solution.py:271
  34.6 0.7 %collective-permute-start.8 = (bf16[8,272,128]{2,1,0:T(8,128)(2,1)S(1)}, bf16[8,272,128]{2,1,0:T(8,128)(2,1)S(1)}, u32[]{:S(2)}, u32[]{:S(2)}) collective-permute-start(bf16[8,272,128]{2,1,0:T(8,128)(2,1)S(1)} %get-tuple-element.58), channel_id=1, source_target_pairs={{0,1},{1,0},{2,3},{3,2},{4,5},{5,4},{6,7},{7,6},{8,9},{9,8},{10,11... | collective-permute-start | bytes 1671176 | tf_op jit(solution)/shard_map/ppermute | solution.py:454
  35.3 0.1 collective-permute-start.9
  35.4 3.9 %flash_own.1.own_ref = bf16[8,272,128]{2,1,0:T(8,128)(2,1)S(1)} custom-call(bf16[256,4096]{1,0:T(8,128)(2,1)S(1)} %scaled_queries.1.refs_1_.qt_ref, bf16[1536,256]{1,0:T(8,128)(2,1)S(1)} %get-tuple-element.56.keys, bf16[144,1536]{1,0:T(8,128)(2,1)S(1)} %get-tuple-element.57.vals_t, f32[8,4096]{1,0:T(8,128)S(1)} %get-tuple-element.54.refs_6_.m_in, ...), custom_call_target="tpu_custom_call" | custom-call | flops 3221225472 | bytes 1048576 | tf_op jit(solution)/shard_map/flash_own/pallas_call | solution.py:271
  39.3 0.0 copy-start
  39.3 0.0 copy-start.1
  39.4 0.0 copy-start.2
  39.4 0.0 collective-permute-done.8.twin_ref
  39.4 1.0 %merge_pair.1 = bf16[8,272,128]{2,1,0:T(8,128)(2,1)} custom-call(bf16[8,272,128]{2,1,0:T(8,128)(2,1)S(1)} %flash_own.1.own_ref, bf16[8,272,128]{2,1,0:T(8,128)(2,1)S(1)} %collective-permute-done.8.twin_ref), custom_call_target="tpu_custom_call" | custom-call | tf_op jit(solution)/shard_map/merge_pair/pallas_call | solution.py:418
  40.4 4.2 %all-to-all-start = ((bf16[8,272,128]{2,1,0:T(8,128)(2,1)}), bf16[8,272,128]{2,1,0:T(8,128)(2,1)S(1)}, u32[]{:S(2)}, u32[]{:S(2)}) async-start(bf16[8,272,128]{2,1,0:T(8,128)(2,1)} %merge_pair.1), calls=%async_computation | async-start | bytes 1114112 | tf_op jit(solution)/shard_map/all_to_all | solution.py:500
  44.6 0.0 collective-permute-done.9.twin_ref
  44.6 0.0 copy-done
  44.6 0.0 copy-done.1
  44.7 0.0 copy-done.2
  44.7 2.0 %write_pages.1 = bf16[512,256]{1,0:T(8,128)(2,1)} custom-call(s32[128]{0:T(128)S(1)} %copy-done.1, s32[1,256]{1,0:T(1,128)S(1)} %bitcast.1, bf16[512,256]{1,0:T(8,128)(2,1)S(1)} %copy-done, bf16[1024,256]{1,0:T(8,128)(2,1)S(1)} %get-tuple-element.59.own_ref, bf16[1024,256]{1,0:T(8,128)(2,1)S(1)} %collective-permute-done.9.twin_ref), custom_call_target="tpu_custom_call" | custom-call | flops 1000000000 | bytes 2097152 | tf_op jit(solution)/shard_map/write_pages/pallas_call | solution.py:385
  46.7 7.4 %all-to-all-done.parts_ref = bf16[8,272,128]{2,1,0:T(8,128)(2,1)S(1)} async-done(((bf16[8,272,128]{2,1,0:T(8,128)(2,1)}), bf16[8,272,128]{2,1,0:T(8,128)(2,1)S(1)}, u32[]{:S(2)}, u32[]{:S(2)}) %all-to-all-start) | async-done | bytes 557088 | tf_op jit(solution)/shard_map/all_to_all | solution.py:500
  54.1 0.8 %merge.1 = bf16[128,256]{1,0:T(8,128)(2,1)} custom-call(bf16[8,272,128]{2,1,0:T(8,128)(2,1)S(1)} %all-to-all-done.parts_ref), custom_call_target="tpu_custom_call" | custom-call | tf_op jit(solution)/shard_map/merge/pallas_call | solution.py:443
Async XLA Ops:
  1.9 9.6 %collective-permute-start = (bf16[128,2048]{1,0:T(8,128)(2,1)S(1)}, bf16[128,2048]{1,0:T(8,128)(2,1)S(1)}, u32[]{:S(2)}, u32[]{:S(2)}) collective-permute-start(bf16[128,2048]{1,0:T(8,128)(2,1)S(1)} %get-tuple-element.31.own_ref), channel_id=1, source_target_pairs={{0,1},{1,0},{2,3},{3,2},{4,5},{5,4},{6,7},{7,6},{8,9},{9,8},{10,11... | collective-permute-start | bytes 1572872 | tf_op jit(solution)/shard_map/ppermute | solution.py:454
  3.4 11.6 %collective-permute-start.1 = (bf16[576,256]{1,0:T(8,128)(2,1)S(1)}, bf16[576,256]{1,0:T(8,128)(2,1)S(1)}, u32[]{:S(2)}, u32[]{:S(2)}) collective-permute-start(bf16[576,256]{1,0:T(8,128)(2,1)S(1)} %get-tuple-element.33.refs_2_.refs_0_), channel_id=1, source_target_pairs={{0,24},{1,25},{2,26},{3,27},{4,28},{5,29},{6,30},{7,31},{8,16},{9,... | collective-permute-start | bytes 884744 | tf_op jit(solution)/shard_map/ppermute | solution.py:454
  7.2 9.9 %collective-permute-start.4 = (bf16[576,256]{1,0:T(8,128)(2,1)S(1)}, bf16[576,256]{1,0:T(8,128)(2,1)S(1)}, u32[]{:S(2)}, u32[]{:S(2)}) collective-permute-start(bf16[576,256]{1,0:T(8,128)(2,1)S(1)} %get-tuple-element.33.refs_2_.refs_0_), channel_id=1, source_target_pairs={{0,4},{1,5},{2,6},{3,7},{4,0},{5,1},{6,2},{7,3},{8,12},{9,13},{10,... | collective-permute-start | bytes 884744 | tf_op jit(solution)/shard_map/ppermute | solution.py:454
  10.0 13.9 %collective-permute-start.7 = (bf16[576,256]{1,0:T(8,128)(2,1)S(1)}, bf16[576,256]{1,0:T(8,128)(2,1)S(1)}, u32[]{:S(2)}, u32[]{:S(2)}) collective-permute-start(bf16[576,256]{1,0:T(8,128)(2,1)S(1)} %get-tuple-element.33.refs_2_.refs_0_), channel_id=1, source_target_pairs={{0,6},{1,7},{2,0},{3,1},{4,2},{5,3},{6,4},{7,5},{8,14},{9,15},{10,... | collective-permute-start | bytes 884744 | tf_op jit(solution)/shard_map/ppermute | solution.py:454
  10.8 13.1 %collective-permute-start.6 = (bf16[576,256]{1,0:T(8,128)(2,1)S(1)}, bf16[576,256]{1,0:T(8,128)(2,1)S(1)}, u32[]{:S(2)}, u32[]{:S(2)}) collective-permute-start(bf16[576,256]{1,0:T(8,128)(2,1)S(1)} %get-tuple-element.33.refs_2_.refs_0_), channel_id=1, source_target_pairs={{0,2},{1,3},{2,4},{3,5},{4,6},{5,7},{6,0},{7,1},{8,10},{9,11},{10,... | collective-permute-start | bytes 884744 | tf_op jit(solution)/shard_map/ppermute | solution.py:454
  14.9 14.8 %collective-permute-start.3 = (bf16[576,256]{1,0:T(8,128)(2,1)S(1)}, bf16[576,256]{1,0:T(8,128)(2,1)S(1)}, u32[]{:S(2)}, u32[]{:S(2)}) collective-permute-start(bf16[576,256]{1,0:T(8,128)(2,1)S(1)} %collective-permute-done.1.refs_2_.refs_1_), channel_id=1, source_target_pairs={{0,6},{1,7},{2,0},{3,1},{4,2},{5,3},{6,4},{7,5},{8,14},{9,15},{10,... | collective-permute-start | bytes 884744 | tf_op jit(solution)/shard_map/ppermute | solution.py:454
  17.1 13.2 %collective-permute-start.2 = (bf16[576,256]{1,0:T(8,128)(2,1)S(1)}, bf16[576,256]{1,0:T(8,128)(2,1)S(1)}, u32[]{:S(2)}, u32[]{:S(2)}) collective-permute-start(bf16[576,256]{1,0:T(8,128)(2,1)S(1)} %collective-permute-done.1.refs_2_.refs_1_), channel_id=1, source_target_pairs={{0,2},{1,3},{2,4},{3,5},{4,6},{5,7},{6,0},{7,1},{8,10},{9,11},{10,... | collective-permute-start | bytes 884744 | tf_op jit(solution)/shard_map/ppermute | solution.py:454
  17.1 11.3 %collective-permute-start.5 = (bf16[576,256]{1,0:T(8,128)(2,1)S(1)}, bf16[576,256]{1,0:T(8,128)(2,1)S(1)}, u32[]{:S(2)}, u32[]{:S(2)}) collective-permute-start(bf16[576,256]{1,0:T(8,128)(2,1)S(1)} %collective-permute-done.4.refs_3_.refs_2_), channel_id=1, source_target_pairs={{0,24},{1,25},{2,26},{3,27},{4,28},{5,29},{6,30},{7,31},{8,16},{9,... | collective-permute-start | bytes 884744 | tf_op jit(solution)/shard_map/ppermute | solution.py:454
  34.6 4.8 %collective-permute-start.8 = (bf16[8,272,128]{2,1,0:T(8,128)(2,1)S(1)}, bf16[8,272,128]{2,1,0:T(8,128)(2,1)S(1)}, u32[]{:S(2)}, u32[]{:S(2)}) collective-permute-start(bf16[8,272,128]{2,1,0:T(8,128)(2,1)S(1)} %get-tuple-element.58), channel_id=1, source_target_pairs={{0,1},{1,0},{2,3},{3,2},{4,5},{5,4},{6,7},{7,6},{8,9},{9,8},{10,11... | collective-permute-start | bytes 1671176 | tf_op jit(solution)/shard_map/ppermute | solution.py:454
  35.3 9.3 %collective-permute-start.9 = (bf16[1024,256]{1,0:T(8,128)(2,1)S(1)}, bf16[1024,256]{1,0:T(8,128)(2,1)S(1)}, u32[]{:S(2)}, u32[]{:S(2)}) collective-permute-start(bf16[1024,256]{1,0:T(8,128)(2,1)S(1)} %get-tuple-element.59.own_ref), channel_id=1, source_target_pairs={{0,1},{1,0},{2,3},{3,2},{4,5},{5,4},{6,7},{7,6},{8,9},{9,8},{10,11... | collective-permute-start | bytes 1572872 | tf_op jit(solution)/shard_map/ppermute | solution.py:454
  39.3 5.3 %copy-start = (bf16[512,256]{1,0:T(8,128)(2,1)S(1)}, bf16[512,256]{1,0:T(8,128)(2,1)}, u32[]{:S(2)}) copy-start(bf16[512,256]{1,0:T(8,128)(2,1)} %cache_ref.3) | copy-start | bytes 786436
  39.3 5.3 %copy-start.1 = (s32[128]{0:T(128)S(1)}, s32[128]{0:T(128)}, u32[]{:S(2)}) copy-start(s32[128]{0:T(128)} %len_ref.3) | copy-start | bytes 1540
  39.4 5.3 %copy-start.2 = (s32[256,1]{0,1:T(1,128)S(1)}, s32[256,1]{0,1:T(1,128)}, u32[]{:S(2)}) copy-start(s32[256,1]{0,1:T(1,128)} %param.9) | copy-start | bytes 3076
  40.4 13.7 %all-to-all-start = ((bf16[8,272,128]{2,1,0:T(8,128)(2,1)}), bf16[8,272,128]{2,1,0:T(8,128)(2,1)S(1)}, u32[]{:S(2)}, u32[]{:S(2)}) async-start(bf16[8,272,128]{2,1,0:T(8,128)(2,1)} %merge_pair.1), calls=%async_computation | async-start | bytes 1114112 | tf_op jit(solution)/shard_map/all_to_all | solution.py:500

commit v5 on v4

--- a/solution.py
+++ b/solution.py
@@ -104,9 +104,9 @@
 def gather_keys(slots, blocks, fresh_ref, filled_ref, keys, vals, vals_t):
     total = keys.shape[0]
     spans = []
-    for j, (slot, which) in enumerate(slots):
+    for j, (slot, block) in enumerate(zip(slots, blocks)):
         filled = filled_ref[SLOT_ORDER.index(slot) : SLOT_ORDER.index(slot) + 1, :]
-        block, start = blocks[which], j * FILL
+        start = j * FILL
         ok = lax.broadcasted_iota(jnp.int32, (FILL - LEAST, HD), 0) < filled - LEAST
         head = block[0:LEAST, 0:HD]
         tail = block[LEAST:FILL, 0:HD]
@@ -118,16 +118,15 @@
         vals[start : start + LEAST, :] = block[0:LEAST, HD : 2 * HD]
         vals[start + LEAST : start + FILL, :] = jnp.where(ok, value, jnp.zeros_like(value))
         spans.append((start, start + LEAST, start + FILL, start + filled))
-    old = used = len(slots) * FILL
+    old = len(slots) * FILL
     if fresh_ref is not None:
-        used = old + fresh_ref.shape[0]
-        keys[old:used, 0:HD] = fresh_ref[:, 0:HD]
-        keys[old:used, HD : 2 * HD] = fresh_ref[:, 0:HD]
-        vals[old:used, :] = fresh_ref[:, HD : 2 * HD]
-        spans.append((old, used, used, used))
-    if total > used:
-        keys[used:total, :] = jnp.broadcast_to(keys[0:1, :], (total - used, 2 * HD))
-        vals[used:total, :] = jnp.zeros((total - used, HD), BF16)
+        keys[old:total, 0:HD] = fresh_ref[:, 0:HD]
+        keys[old:total, HD : 2 * HD] = fresh_ref[:, 0:HD]
+        vals[old:total, :] = fresh_ref[:, HD : 2 * HD]
+        spans.append((old, total, total, total))
+    elif total > old:
+        keys[old:total, :] = jnp.broadcast_to(keys[0:1, :], (total - old, 2 * HD))
+        vals[old:total, :] = jnp.zeros((total - old, HD), BF16)
     for c in range(total // 128):
         low, high = c * 128, (c + 1) * 128
         vals_t[0:HD, low:high] = vals[low:high, :].T
@@ -143,7 +142,7 @@
         vals_t[HD:ACC, low:high] = one.astype(F32).astype(BF16)
 
 
-def flash_columns(columns, old, keys, vals_t, qt_ref, state, even_ref, odd_ref, query_blk, emit):
+def flash_columns(columns, old, keys, vals_t, qt_ref, state, even_ref, odd_ref, place_ref, emit):
     total, width = even_ref.shape
     first, last = columns[0] // width, columns[1] // width
 
@@ -153,15 +152,16 @@
     def score(r, scores_ref):
         cols = pl.ds(pl.multiple_of(r * width, width), width)
         s = jnp.dot(keys[...], qt_ref[:, cols], preferred_element_type=F32)
-        if query_blk is None:
+        if place_ref is None:
             scores_ref[...] = s
             return column_max(s)
-        shape = (total - old, width)
-        key_id = lax.broadcasted_iota(jnp.int32, shape, 0)
-        key_blk = key_id // SHARE * 2 + lax.axis_index("blk") % 2
-        key_pos = key_blk * TOK + lax.axis_index("seg") * SHARE + key_id % SHARE
-        token = query_blk * TOK + lax.broadcasted_iota(jnp.int32, shape, 1) % TOK
-        fresh = jnp.where(key_pos <= token, s[old:total], NEG)
+        blk = lax.axis_index("blk")
+        query_blk = jnp.where(r < PART // width, blk + 1 - blk % 2 * 2, blk)
+        token = lax.broadcasted_iota(jnp.int32, place_ref.shape, 1)
+        seen = place_ref[...] - query_blk * TOK <= token
+        fresh = jnp.concatenate(
+            [jnp.where(seen, s[old:total, i : i + TOK], NEG) for i in range(0, width, TOK)], axis=1
+        )
         scores_ref[0:old] = s[0:old]
         scores_ref[old:total] = fresh
         return jnp.maximum(column_max(s[0:old]), column_max(fresh))
@@ -190,17 +190,21 @@
     two(pairs - 1, tops, False)
 
 
-def flash_kernel(slots, operand_count, *refs):
+def flash_kernel(slots, has_fresh, *refs):
     filled_ref, qt_ref = refs[0], refs[1]
-    blocks, refs = refs[2 : 2 + operand_count], refs[2 + operand_count :]
+    blocks, refs = refs[2 : 2 + len(slots)], refs[2 + len(slots) :]
+    fresh_ref = place_ref = None
+    if has_fresh:
+        fresh_ref, place_ref, refs = refs[0], refs[1], refs[2:]
     state, (m_ref, acc_ref, keys, vals, vals_t, even_ref, odd_ref) = refs[:-7] or None, refs[-7:]
-    gather_keys(slots, blocks, None, filled_ref, keys, vals, vals_t)
+    gather_keys(slots, blocks, fresh_ref, filled_ref, keys, vals, vals_t)
 
     def emit(r, cols, out, top):
         acc_ref[:, cols] = out
         m_ref[:, cols] = jnp.broadcast_to(top, m_ref.at[:, cols].shape)
 
-    flash_columns((0, ROWS), keys.shape[0], keys, vals_t, qt_ref, state, even_ref, odd_ref, None, emit)
+    old = len(slots) * FILL
+    flash_columns((0, ROWS), old, keys, vals_t, qt_ref, state, even_ref, odd_ref, place_ref, emit)
 
 
 def emit_part(part_ref, width):
@@ -232,39 +236,19 @@
     return three[0] + three[1] + three[2]
 
 
-def twin_kernel(slots, operand_count, *refs):
+def twin_kernel(slots, *refs):
     filled_ref, qt_ref = refs[0], refs[1]
-    blocks, refs = refs[2 : 2 + operand_count], refs[2 + operand_count :]
-    fresh_ref, m_in, acc_in, part_ref, keys, vals_t, vals, even_ref, odd_ref = refs
+    blocks, refs = refs[2 : 2 + len(slots)], refs[2 + len(slots) :]
+    fresh_ref, place_ref, m_in, acc_in, part_ref, keys, vals_t, vals, even_ref, odd_ref = refs
     gather_keys(slots, blocks, fresh_ref, filled_ref, keys, vals, vals_t)
-    blk = lax.axis_index("blk")
-    flash_columns(
-        (0, PART),
-        len(slots) * FILL,
-        keys,
-        vals_t,
-        qt_ref,
-        (m_in, acc_in),
-        even_ref,
-        odd_ref,
-        blk + 1 - blk % 2 * 2,
-        emit_part(part_ref, even_ref.shape[1]),
-    )
-
-
-def own_kernel(old, qt_ref, keys, vals_t, m_in, acc_in, part_ref, even_ref, odd_ref):
-    flash_columns(
-        (PART, ROWS),
-        old,
-        keys,
-        vals_t,
-        qt_ref,
-        (m_in, acc_in),
-        even_ref,
-        odd_ref,
-        lax.axis_index("blk"),
-        emit_part(part_ref, even_ref.shape[1]),
-    )
+    emit = emit_part(part_ref, even_ref.shape[1])
+    state, old = (m_in, acc_in), len(slots) * FILL
+    flash_columns((0, PART), old, keys, vals_t, qt_ref, state, even_ref, odd_ref, place_ref, emit)
+
+
+def own_kernel(old, qt_ref, keys, vals_t, place_ref, m_in, acc_in, part_ref, even_ref, odd_ref):
+    emit = emit_part(part_ref, even_ref.shape[1])
+    flash_columns((PART, ROWS), old, keys, vals_t, qt_ref, (m_in, acc_in), even_ref, odd_ref, place_ref, emit)
 
 
 def flash_call(kernel, operands, out_shape, scratch, total, rows, name, width=WIDTH):
@@ -282,12 +266,13 @@
     )(*operands)
 
 
-def flash(held, filled, qt, state):
-    slots, blocks = indexed(held)
-    total = -(-len(slots) * FILL // 128) * 128
+def flash(held, filled, qt, state, fresh=()):
+    total = -(-len(held) * FILL // 128) * 128
+    if fresh:
+        total = len(held) * FILL + fresh[0].shape[0]
     return flash_call(
-        functools.partial(flash_kernel, slots, len(blocks)),
-        [filled, qt, *blocks, *(state or ())],
+        functools.partial(flash_kernel, list(held), bool(fresh)),
+        [filled, qt, *held.values(), *fresh, *(state or ())],
         [jax.ShapeDtypeStruct((8, ROWS), F32), jax.ShapeDtypeStruct((ACC, ROWS), F32)],
         [
             pltpu.VMEM((total, 2 * HD), BF16),
@@ -296,18 +281,17 @@
         ],
         total,
         ROWS,
-        f"flash_{len(slots)}",
+        f"flash_{len(held)}",
     )
 
 
 def flash_last(held, filled, qt, state, fresh):
-    slots, blocks = indexed(held)
-    old = len(slots) * FILL
-    total = -(-(old + fresh.shape[0]) // 128) * 128
+    old = len(held) * FILL
+    total = old + fresh[0].shape[0]
     part = jax.ShapeDtypeStruct((NSEG, CHUNK, TOK), BF16)
     twin_part, keys, vals_t = flash_call(
-        functools.partial(twin_kernel, slots, len(blocks)),
-        [filled, qt, *blocks, fresh, *state],
+        functools.partial(twin_kernel, list(held)),
+        [filled, qt, *held.values(), *fresh, *state],
         [part, jax.ShapeDtypeStruct((total, 2 * HD), BF16), jax.ShapeDtypeStruct((ACC, total), BF16)],
         [pltpu.VMEM((total, HD), BF16)],
         total,
@@ -315,38 +299,52 @@
         "flash_twin",
     )
     own_part = flash_call(
-        functools.partial(own_kernel, old), [qt, keys, vals_t, *state], part, [], total, PART, "flash_own"
+        functools.partial(own_kernel, old), [qt, keys, vals_t, fresh[1], *state], part, [], total, PART, "flash_own"
     )
     return twin_part, own_part
 
 
-def indexed(held):
-    return [(slot, i) for i, slot in enumerate(held)], list(held.values())
-
-
 def fresh_kernel(slots, *refs):
-    blocks, share_ref, rows_ref = refs[:-2], refs[-2], refs[-1]
-    start = pl.multiple_of(FILL + lax.axis_index("seg") * SHARE, SHARE)
-    for slot, which in slots:
-        pair = origin(slot) % NBLK // 2
-        block = blocks[which]
-        share_ref[pl.ds(pl.multiple_of(pair * SHARE, SHARE), SHARE), :] = block[pl.ds(start, SHARE), :]
-        rows_ref[pl.ds(pl.multiple_of(pair * TOK, TOK), TOK), :] = block[FILL : FILL + TOK, :]
-
-
-def fresh_rows(held):
-    slots, blocks = indexed(held)
-    return pl.pallas_call(
-        functools.partial(fresh_kernel, slots),
-        in_specs=[VMEM] * len(blocks),
+    blocks, share_ref, place_ref = refs[: len(slots)], refs[-2], refs[-1]
+    first = lax.axis_index("seg") * SHARE
+    for j, (slot, block) in enumerate(zip(slots, blocks)):
+        rows = slice(j * SHARE, (j + 1) * SHARE)
+        share_ref[rows, :] = block[pl.ds(pl.multiple_of(FILL + first, SHARE), SHARE), :]
+        place = origin(slot) % NBLK * TOK + first
+        place_ref[rows, :] = lax.broadcasted_iota(jnp.int32, (SHARE, TOK), 0) + place
+    rest = share_ref.shape[0] - len(slots) * SHARE
+    share_ref[len(slots) * SHARE :, :] = jnp.zeros((rest, 2 * HD), BF16)
+    place_ref[len(slots) * SHARE :, :] = jnp.full((rest, TOK), NBLK * TOK, jnp.int32)
+
+
+def fresh_rows(held, after_slots):
+    old = after_slots * FILL
+    size = -(-(old + len(held) * SHARE) // 128) * 128 - old
+    return pl.pallas_call(
+        functools.partial(fresh_kernel, list(held)),
+        in_specs=[VMEM] * len(held),
         out_specs=[VMEM, VMEM],
-        out_shape=[
-            jax.ShapeDtypeStruct((NBLK // 2 * SHARE, 2 * HD), BF16),
-            jax.ShapeDtypeStruct((NBLK // 2 * TOK, 2 * HD), BF16),
-        ],
+        out_shape=[jax.ShapeDtypeStruct((size, 2 * HD), BF16), jax.ShapeDtypeStruct((size, TOK), jnp.int32)],
         compiler_params=pltpu.CompilerParams(vmem_limit_bytes=1 << 20),
         name="fresh_rows",
-    )(*blocks)
+    )(*held.values())
+
+
+def rows_kernel(slots, *refs):
+    for slot, block in zip(slots, refs):
+        pair = origin(slot) % NBLK // 2
+        refs[-1][pl.ds(pl.multiple_of(pair * TOK, TOK), TOK), :] = block[FILL : FILL + TOK, :]
+
+
+def new_rows(held):
+    return pl.pallas_call(
+        functools.partial(rows_kernel, list(held)),
+        in_specs=[VMEM] * len(held),
+        out_specs=VMEM,
+        out_shape=jax.ShapeDtypeStruct((NBLK // 2 * TOK, 2 * HD), BF16),
+        compiler_params=pltpu.CompilerParams(vmem_limit_bytes=1 << 20),
+        name="new_rows",
+    )(*held.values())
 
 
 def pages_kernel(len_ref, owner_ref, cache_ref, own_ref, twin_ref, out_ref):
@@ -489,13 +487,13 @@
 
     beside, state = after(beside, state)
     everything.update(beside)
-    state = flash(beside, filled, qt, state)
+    state = flash(beside, filled, qt, state, fresh_rows(everything, len(beside)))
 
     far, state = after(far, state)
     everything.update(far)
-    fresh, rows = fresh_rows(everything)
+    rows = new_rows(everything)
     twin_rows = shift(rows, flip_core=True)
-    twin_part, own_part = flash_last(far, filled, qt, state, fresh)
+    twin_part, own_part = flash_last(far, filled, qt, state, fresh_rows(far, len(far)))
     part = merge_pair(own_part, shift(twin_part, flip_core=True))
     parts = lax.all_to_all(part, "seg", 0, 0)
     cache_out = write_pages(cache_len, page_owner, cache_kv, rows, twin_rows)

time: 55.2 us -> 54.7 us (level)
  waiting for transfers between devices: 9.46 us -> 8.55 us
    ppermute x10, waiting for transfers between devices: 2.04 us -> 1.19 us  [shift(): return lax.ppermute(block, AXES, neighbours(-dx, flip_z, flip_core))]
  transfers between devices with their start and end apart: 11 -> 11, of which waited for: 4 -> 4; matrix products, arithmetic and copies ran while one was open for 0% -> 0% of each run, Pallas kernels for 35% -> 37%
where the time goes in v5:
time: 54.7 us; the launch traced here: 54.4 us
  Pallas kernels  25.9 us (47%)
  starting transfers between devices  19.1 us (35%)
  waiting for transfers between devices  8.55 us (16%)
  between operations  0.79 us (1%)
    pallas_call x5, Pallas kernels, flash_call(): pl.pallas_call(kernel, in_specs=[VMEM] * len(operands), out_specs=jax.tre...  20 us
    ppermute x10, starting transfers between devices, shift(): return lax.ppermute(block, AXES, neighbours(-dx, flip_z, flip_core))  14.9 us
    all_to_all x1, waiting for transfers between devices, on_device(): parts = lax.all_to_all(part, 'seg', 0, 0)  7.36 us
    all_to_all x1, starting transfers between devices, on_device(): parts = lax.all_to_all(part, 'seg', 0, 0)  4.2 us
    pallas_call x1, Pallas kernels, write_pages(): pl.pallas_call(pages_kernel, in_specs=[SMEM] + [VMEM] * 4, out_specs=VMEM...  2.04 us
    pallas_call x1, Pallas kernels, pack(): pl.pallas_call(pack_kernel, in_specs=[pl.BlockSpec(memory_space=pltpu.HBM...  1.24 us
    ppermute x10, waiting for transfers between devices, shift(): return lax.ppermute(block, AXES, neighbours(-dx, flip_z, flip_core))  1.19 us
  transfers between devices with their start and end apart: 11, of which 4 were waited for; matrix products, arithmetic and copies ran while one was open for 0% of the time, Pallas kernels for 37%

profile of v5, /device:TPU:1, one launch (start us, length us, event | category | flops | bytes accessed | tf_op | source)
XLA Modules:
  0.0 54.4 jit_solution(42067385983349161)
XLA Ops:
  0.6 1.2 %pack.1 = (bf16[576,256]{1,0:T(8,128)(2,1)S(1)}, bf16[128,2048]{1,0:T(8,128)(2,1)S(1)}, s32[8,128]{1,0:T(8,128)S(1)}) custom-call(bf16[512,256]{1,0:T(8,128)(2,1)} %cache_ref.3, bf16[128,256]{1,0:T(8,128)(2,1)} %new_ref.1, bf16[128,2048]{1,0:T(8,128)(2,1)} %q_ref.1, s32[128]{0:T(128)} %len_ref.3), custom_call_target="tpu_custom_call" | custom-call | tf_op jit(solution)/shard_map/pack/pallas_call | solution.py:89
  1.9 1.5 %collective-permute-start = (bf16[128,2048]{1,0:T(8,128)(2,1)S(1)}, bf16[128,2048]{1,0:T(8,128)(2,1)S(1)}, u32[]{:S(2)}, u32[]{:S(2)}) collective-permute-start(bf16[128,2048]{1,0:T(8,128)(2,1)S(1)} %get-tuple-element.33.own_ref), channel_id=1, source_target_pairs={{0,1},{1,0},{2,3},{3,2},{4,5},{5,4},{6,7},{7,6},{8,9},{9,8},{10,11... | collective-permute-start | bytes 1572872 | tf_op jit(solution)/shard_map/ppermute | solution.py:452
  3.4 3.9 %collective-permute-start.1 = (bf16[576,256]{1,0:T(8,128)(2,1)S(1)}, bf16[576,256]{1,0:T(8,128)(2,1)S(1)}, u32[]{:S(2)}, u32[]{:S(2)}) collective-permute-start(bf16[576,256]{1,0:T(8,128)(2,1)S(1)} %get-tuple-element.35.refs_2_.refs_0_), channel_id=1, source_target_pairs={{0,24},{1,25},{2,26},{3,27},{4,28},{5,29},{6,30},{7,31},{8,16},{9,... | collective-permute-start | bytes 884744 | tf_op jit(solution)/shard_map/ppermute | solution.py:452
  7.2 2.7 %collective-permute-start.4 = (bf16[576,256]{1,0:T(8,128)(2,1)S(1)}, bf16[576,256]{1,0:T(8,128)(2,1)S(1)}, u32[]{:S(2)}, u32[]{:S(2)}) collective-permute-start(bf16[576,256]{1,0:T(8,128)(2,1)S(1)} %get-tuple-element.35.refs_2_.refs_0_), channel_id=1, source_target_pairs={{0,4},{1,5},{2,6},{3,7},{4,0},{5,1},{6,2},{7,3},{8,12},{9,13},{10,... | collective-permute-start | bytes 884744 | tf_op jit(solution)/shard_map/ppermute | solution.py:452
  10.0 0.9 %collective-permute-start.7 = (bf16[576,256]{1,0:T(8,128)(2,1)S(1)}, bf16[576,256]{1,0:T(8,128)(2,1)S(1)}, u32[]{:S(2)}, u32[]{:S(2)}) collective-permute-start(bf16[576,256]{1,0:T(8,128)(2,1)S(1)} %get-tuple-element.35.refs_2_.refs_0_), channel_id=1, source_target_pairs={{0,6},{1,7},{2,0},{3,1},{4,2},{5,3},{6,4},{7,5},{8,14},{9,15},{10,... | collective-permute-start | bytes 884744 | tf_op jit(solution)/shard_map/ppermute | solution.py:452
  10.8 0.6 %collective-permute-start.6 = (bf16[576,256]{1,0:T(8,128)(2,1)S(1)}, bf16[576,256]{1,0:T(8,128)(2,1)S(1)}, u32[]{:S(2)}, u32[]{:S(2)}) collective-permute-start(bf16[576,256]{1,0:T(8,128)(2,1)S(1)} %get-tuple-element.35.refs_2_.refs_0_), channel_id=1, source_target_pairs={{0,2},{1,3},{2,4},{3,5},{4,6},{5,7},{6,0},{7,1},{8,10},{9,11},{10,... | collective-permute-start | bytes 884744 | tf_op jit(solution)/shard_map/ppermute | solution.py:452
  11.4 0.0 collective-permute-done.twin_ref
  11.5 0.6 %scaled_queries.1.refs_1_.qt_ref = bf16[256,4096]{1,0:T(8,128)(2,1)S(1)} custom-call(bf16[128,2048]{1,0:T(8,128)(2,1)S(1)} %collective-permute-done.twin_ref, bf16[128,2048]{1,0:T(8,128)(2,1)S(1)} %get-tuple-element.33.own_ref), custom_call_target="tpu_custom_call" | custom-call | tf_op jit(solution)/shard_map/scaled_queries/pallas_call | solution.py:460
  12.0 2.9 %flash_1.1 = (f32[8,4096]{1,0:T(8,128)S(1)}, f32[144,4096]{1,0:T(8,128)S(1)}) custom-call(s32[8,128]{1,0:T(8,128)S(1)} %get-tuple-element.34.refs_0_, bf16[256,4096]{1,0:T(8,128)(2,1)S(1)} %scaled_queries.1.refs_1_.qt_ref, bf16[576,256]{1,0:T(8,128)(2,1)S(1)} %get-tuple-element.35.refs_2_.refs_0_), custom_call_target="tpu_custom_call" | custom-call | flops 2147483648 | bytes 1048576 | tf_op jit(solution)/shard_map/flash_1/pallas_call | solution.py:255
  14.9 0.0 collective-permute-done.1.refs_2_.refs_1_
  14.9 2.1 %collective-permute-start.3 = (bf16[576,256]{1,0:T(8,128)(2,1)S(1)}, bf16[576,256]{1,0:T(8,128)(2,1)S(1)}, u32[]{:S(2)}, u32[]{:S(2)}) collective-permute-start(bf16[576,256]{1,0:T(8,128)(2,1)S(1)} %collective-permute-done.1.refs_2_.refs_1_), channel_id=1, source_target_pairs={{0,6},{1,7},{2,0},{3,1},{4,2},{5,3},{6,4},{7,5},{8,14},{9,15},{10,... | collective-permute-start | bytes 884744 | tf_op jit(solution)/shard_map/ppermute | solution.py:452
  17.1 0.0 collective-permute-start.2
  17.1 0.0 collective-permute-done.4.refs_3_.refs_2_
  17.1 2.4 %collective-permute-start.5 = (bf16[576,256]{1,0:T(8,128)(2,1)S(1)}, bf16[576,256]{1,0:T(8,128)(2,1)S(1)}, u32[]{:S(2)}, u32[]{:S(2)}) collective-permute-start(bf16[576,256]{1,0:T(8,128)(2,1)S(1)} %collective-permute-done.4.refs_3_.refs_2_), channel_id=1, source_target_pairs={{0,24},{1,25},{2,26},{3,27},{4,28},{5,29},{6,30},{7,31},{8,16},{9,... | collective-permute-start | bytes 884744 | tf_op jit(solution)/shard_map/ppermute | solution.py:452
  19.5 4.4 %flash_2.2 = (f32[8,4096]{1,0:T(8,128)S(1)}, f32[144,4096]{1,0:T(8,128)S(1)}) custom-call(s32[8,128]{1,0:T(8,128)S(1)} %get-tuple-element.34.refs_0_, bf16[256,4096]{1,0:T(8,128)(2,1)S(1)} %scaled_queries.1.refs_1_.qt_ref, bf16[576,256]{1,0:T(8,128)(2,1)S(1)} %collective-permute-done.1.refs_2_.refs_1_, ...), custom_call_target="tpu_custom_call" | custom-call | flops 3758096384 | bytes 1048576 | tf_op jit(solution)/shard_map/flash_2/pallas_call | solution.py:255
  23.9 0.0 collective-permute-done.7.refs_4_.refs_3_
  23.9 0.1 collective-permute-done.6.refs_3_.refs_2_
  24.0 5.2 %flash_2.3 = (f32[8,4096]{1,0:T(8,128)S(1)}, f32[144,4096]{1,0:T(8,128)S(1)}) custom-call(s32[8,128]{1,0:T(8,128)S(1)} %get-tuple-element.34.refs_0_, bf16[256,4096]{1,0:T(8,128)(2,1)S(1)} %scaled_queries.1.refs_1_.qt_ref, bf16[576,256]{1,0:T(8,128)(2,1)S(1)} %collective-permute-done.6.refs_3_.refs_2_, ...), custom_call_target="tpu_custom_call" | custom-call | flops 4294967296 | bytes 1048576 | tf_op jit(solution)/shard_map/flash_2/pallas_call | solution.py:255
  29.2 0.0 collective-permute-done.5.refs_2_.refs_4_.refs_7_
  29.2 0.5 collective-permute-done.3.refs_1_.refs_3_.refs_6_
  29.7 0.6 %collective-permute-done.2.refs_0_.refs_2_.refs_5_ = bf16[576,256]{1,0:T(8,128)(2,1)S(1)} collective-permute-done((bf16[576,256]{1,0:T(8,128)(2,1)S(1)}, bf16[576,256]{1,0:T(8,128)(2,1)S(1)}, u32[]{:S(2)}, u32[]{:S(2)}) %collective-permute-start.2) | collective-permute-done | bytes 294944 | tf_op jit(solution)/shard_map/ppermute | solution.py:452
  30.3 3.9 %flash_twin.1 = (bf16[8,272,128]{2,1,0:T(8,128)(2,1)S(1)}, bf16[1408,256]{1,0:T(8,128)(2,1)S(1)}, bf16[144,1408]{1,0:T(8,128)(2,1)S(1)}) custom-call(s32[8,128]{1,0:T(8,128)S(1)} %get-tuple-element.34.refs_0_, bf16[256,4096]{1,0:T(8,128)(2,1)S(1)} %scaled_queries.1.refs_1_.qt_ref, bf16[576,256]{1,0:T(8,128)(2,1)S(1)} %collective-permute-done.2.refs_0_.refs_2_.refs_5_, ...), custom_call_target="tpu_custom_call" | custom-call | flops 2952790016 | bytes 1048576 | tf_op jit(solution)/shard_map/flash_twin/pallas_call | solution.py:255
  34.3 0.7 %collective-permute-start.8 = (bf16[8,272,128]{2,1,0:T(8,128)(2,1)S(1)}, bf16[8,272,128]{2,1,0:T(8,128)(2,1)S(1)}, u32[]{:S(2)}, u32[]{:S(2)}) collective-permute-start(bf16[8,272,128]{2,1,0:T(8,128)(2,1)S(1)} %get-tuple-element.63), channel_id=1, source_target_pairs={{0,1},{1,0},{2,3},{3,2},{4,5},{5,4},{6,7},{7,6},{8,9},{9,8},{10,11... | collective-permute-start | bytes 1671176 | tf_op jit(solution)/shard_map/ppermute | solution.py:452
  35.0 0.1 new_rows.1.own_ref
  35.1 0.1 collective-permute-start.9
  35.2 3.6 %flash_own.1.own_ref = bf16[8,272,128]{2,1,0:T(8,128)(2,1)S(1)} custom-call(bf16[256,4096]{1,0:T(8,128)(2,1)S(1)} %scaled_queries.1.refs_1_.qt_ref, bf16[1408,256]{1,0:T(8,128)(2,1)S(1)} %get-tuple-element.61.keys, bf16[144,1408]{1,0:T(8,128)(2,1)S(1)} %get-tuple-element.62.vals_t, s32[64,128]{1,0:T(8,128)S(1)} %get-tuple-element.58.refs_6_.place_ref, ...), custom_call_target="tpu_custom_call" | custom-call | flops 2952790016 | bytes 1048576 | tf_op jit(solution)/shard_map/flash_own/pallas_call | solution.py:255
  38.9 0.0 copy-start
  38.9 0.0 copy-start.1
  38.9 0.0 copy-start.2
  38.9 0.0 collective-permute-done.8.twin_ref
  38.9 1.0 %merge_pair.1 = bf16[8,272,128]{2,1,0:T(8,128)(2,1)} custom-call(bf16[8,272,128]{2,1,0:T(8,128)(2,1)S(1)} %flash_own.1.own_ref, bf16[8,272,128]{2,1,0:T(8,128)(2,1)S(1)} %collective-permute-done.8.twin_ref), custom_call_target="tpu_custom_call" | custom-call | tf_op jit(solution)/shard_map/merge_pair/pallas_call | solution.py:416
  40.0 4.2 %all-to-all-start = ((bf16[8,272,128]{2,1,0:T(8,128)(2,1)}), bf16[8,272,128]{2,1,0:T(8,128)(2,1)S(1)}, u32[]{:S(2)}, u32[]{:S(2)}) async-start(bf16[8,272,128]{2,1,0:T(8,128)(2,1)} %merge_pair.1), calls=%async_computation | async-start | bytes 1114112 | tf_op jit(solution)/shard_map/all_to_all | solution.py:498
  44.2 0.0 collective-permute-done.9.twin_ref
  44.2 0.0 copy-done
  44.2 0.0 copy-done.1
  44.2 0.0 copy-done.2
  44.2 2.0 %write_pages.1 = bf16[512,256]{1,0:T(8,128)(2,1)} custom-call(s32[128]{0:T(128)S(1)} %copy-done.1, s32[1,256]{1,0:T(1,128)S(1)} %bitcast.1, bf16[512,256]{1,0:T(8,128)(2,1)S(1)} %copy-done, bf16[1024,256]{1,0:T(8,128)(2,1)S(1)} %new_rows.1.own_ref, bf16[1024,256]{1,0:T(8,128)(2,1)S(1)} %collective-permute-done.9.twin_ref), custom_call_target="tpu_custom_call" | custom-call | flops 1000000000 | bytes 2097152 | tf_op jit(solution)/shard_map/write_pages/pallas_call | solution.py:383
  46.2 7.4 %all-to-all-done.parts_ref = bf16[8,272,128]{2,1,0:T(8,128)(2,1)S(1)} async-done(((bf16[8,272,128]{2,1,0:T(8,128)(2,1)}), bf16[8,272,128]{2,1,0:T(8,128)(2,1)S(1)}, u32[]{:S(2)}, u32[]{:S(2)}) %all-to-all-start) | async-done | bytes 557088 | tf_op jit(solution)/shard_map/all_to_all | solution.py:498
  53.6 0.8 %merge.1 = bf16[128,256]{1,0:T(8,128)(2,1)} custom-call(bf16[8,272,128]{2,1,0:T(8,128)(2,1)S(1)} %all-to-all-done.parts_ref), custom_call_target="tpu_custom_call" | custom-call | tf_op jit(solution)/shard_map/merge/pallas_call | solution.py:441
  (2 shorter events, 0.0 us)
Async XLA Ops:
  1.9 9.6 %collective-permute-start = (bf16[128,2048]{1,0:T(8,128)(2,1)S(1)}, bf16[128,2048]{1,0:T(8,128)(2,1)S(1)}, u32[]{:S(2)}, u32[]{:S(2)}) collective-permute-start(bf16[128,2048]{1,0:T(8,128)(2,1)S(1)} %get-tuple-element.33.own_ref), channel_id=1, source_target_pairs={{0,1},{1,0},{2,3},{3,2},{4,5},{5,4},{6,7},{7,6},{8,9},{9,8},{10,11... | collective-permute-start | bytes 1572872 | tf_op jit(solution)/shard_map/ppermute | solution.py:452
  3.4 11.6 %collective-permute-start.1 = (bf16[576,256]{1,0:T(8,128)(2,1)S(1)}, bf16[576,256]{1,0:T(8,128)(2,1)S(1)}, u32[]{:S(2)}, u32[]{:S(2)}) collective-permute-start(bf16[576,256]{1,0:T(8,128)(2,1)S(1)} %get-tuple-element.35.refs_2_.refs_0_), channel_id=1, source_target_pairs={{0,24},{1,25},{2,26},{3,27},{4,28},{5,29},{6,30},{7,31},{8,16},{9,... | collective-permute-start | bytes 884744 | tf_op jit(solution)/shard_map/ppermute | solution.py:452
  7.2 9.9 %collective-permute-start.4 = (bf16[576,256]{1,0:T(8,128)(2,1)S(1)}, bf16[576,256]{1,0:T(8,128)(2,1)S(1)}, u32[]{:S(2)}, u32[]{:S(2)}) collective-permute-start(bf16[576,256]{1,0:T(8,128)(2,1)S(1)} %get-tuple-element.35.refs_2_.refs_0_), channel_id=1, source_target_pairs={{0,4},{1,5},{2,6},{3,7},{4,0},{5,1},{6,2},{7,3},{8,12},{9,13},{10,... | collective-permute-start | bytes 884744 | tf_op jit(solution)/shard_map/ppermute | solution.py:452
  10.0 13.9 %collective-permute-start.7 = (bf16[576,256]{1,0:T(8,128)(2,1)S(1)}, bf16[576,256]{1,0:T(8,128)(2,1)S(1)}, u32[]{:S(2)}, u32[]{:S(2)}) collective-permute-start(bf16[576,256]{1,0:T(8,128)(2,1)S(1)} %get-tuple-element.35.refs_2_.refs_0_), channel_id=1, source_target_pairs={{0,6},{1,7},{2,0},{3,1},{4,2},{5,3},{6,4},{7,5},{8,14},{9,15},{10,... | collective-permute-start | bytes 884744 | tf_op jit(solution)/shard_map/ppermute | solution.py:452
  10.8 13.1 %collective-permute-start.6 = (bf16[576,256]{1,0:T(8,128)(2,1)S(1)}, bf16[576,256]{1,0:T(8,128)(2,1)S(1)}, u32[]{:S(2)}, u32[]{:S(2)}) collective-permute-start(bf16[576,256]{1,0:T(8,128)(2,1)S(1)} %get-tuple-element.35.refs_2_.refs_0_), channel_id=1, source_target_pairs={{0,2},{1,3},{2,4},{3,5},{4,6},{5,7},{6,0},{7,1},{8,10},{9,11},{10,... | collective-permute-start | bytes 884744 | tf_op jit(solution)/shard_map/ppermute | solution.py:452
  14.9 14.8 %collective-permute-start.3 = (bf16[576,256]{1,0:T(8,128)(2,1)S(1)}, bf16[576,256]{1,0:T(8,128)(2,1)S(1)}, u32[]{:S(2)}, u32[]{:S(2)}) collective-permute-start(bf16[576,256]{1,0:T(8,128)(2,1)S(1)} %collective-permute-done.1.refs_2_.refs_1_), channel_id=1, source_target_pairs={{0,6},{1,7},{2,0},{3,1},{4,2},{5,3},{6,4},{7,5},{8,14},{9,15},{10,... | collective-permute-start | bytes 884744 | tf_op jit(solution)/shard_map/ppermute | solution.py:452
  17.1 13.2 %collective-permute-start.2 = (bf16[576,256]{1,0:T(8,128)(2,1)S(1)}, bf16[576,256]{1,0:T(8,128)(2,1)S(1)}, u32[]{:S(2)}, u32[]{:S(2)}) collective-permute-start(bf16[576,256]{1,0:T(8,128)(2,1)S(1)} %collective-permute-done.1.refs_2_.refs_1_), channel_id=1, source_target_pairs={{0,2},{1,3},{2,4},{3,5},{4,6},{5,7},{6,0},{7,1},{8,10},{9,11},{10,... | collective-permute-start | bytes 884744 | tf_op jit(solution)/shard_map/ppermute | solution.py:452
  17.1 12.1 %collective-permute-start.5 = (bf16[576,256]{1,0:T(8,128)(2,1)S(1)}, bf16[576,256]{1,0:T(8,128)(2,1)S(1)}, u32[]{:S(2)}, u32[]{:S(2)}) collective-permute-start(bf16[576,256]{1,0:T(8,128)(2,1)S(1)} %collective-permute-done.4.refs_3_.refs_2_), channel_id=1, source_target_pairs={{0,24},{1,25},{2,26},{3,27},{4,28},{5,29},{6,30},{7,31},{8,16},{9,... | collective-permute-start | bytes 884744 | tf_op jit(solution)/shard_map/ppermute | solution.py:452
  34.3 4.7 %collective-permute-start.8 = (bf16[8,272,128]{2,1,0:T(8,128)(2,1)S(1)}, bf16[8,272,128]{2,1,0:T(8,128)(2,1)S(1)}, u32[]{:S(2)}, u32[]{:S(2)}) collective-permute-start(bf16[8,272,128]{2,1,0:T(8,128)(2,1)S(1)} %get-tuple-element.63), channel_id=1, source_target_pairs={{0,1},{1,0},{2,3},{3,2},{4,5},{5,4},{6,7},{7,6},{8,9},{9,8},{10,11... | collective-permute-start | bytes 1671176 | tf_op jit(solution)/shard_map/ppermute | solution.py:452
  35.1 9.1 %collective-permute-start.9 = (bf16[1024,256]{1,0:T(8,128)(2,1)S(1)}, bf16[1024,256]{1,0:T(8,128)(2,1)S(1)}, u32[]{:S(2)}, u32[]{:S(2)}) collective-permute-start(bf16[1024,256]{1,0:T(8,128)(2,1)S(1)} %new_rows.1.own_ref), channel_id=1, source_target_pairs={{0,1},{1,0},{2,3},{3,2},{4,5},{5,4},{6,7},{7,6},{8,9},{9,8},{10,11... | collective-permute-start | bytes 1572872 | tf_op jit(solution)/shard_map/ppermute | solution.py:452
  38.9 5.3 %copy-start = (bf16[512,256]{1,0:T(8,128)(2,1)S(1)}, bf16[512,256]{1,0:T(8,128)(2,1)}, u32[]{:S(2)}) copy-start(bf16[512,256]{1,0:T(8,128)(2,1)} %cache_ref.3) | copy-start | bytes 786436
  38.9 5.3 %copy-start.1 = (s32[128]{0:T(128)S(1)}, s32[128]{0:T(128)}, u32[]{:S(2)}) copy-start(s32[128]{0:T(128)} %len_ref.3) | copy-start | bytes 1540
  38.9 5.3 %copy-start.2 = (s32[256,1]{0,1:T(1,128)S(1)}, s32[256,1]{0,1:T(1,128)}, u32[]{:S(2)}) copy-start(s32[256,1]{0,1:T(1,128)} %param.9) | copy-start | bytes 3076
  40.0 13.6 %all-to-all-start = ((bf16[8,272,128]{2,1,0:T(8,128)(2,1)}), bf16[8,272,128]{2,1,0:T(8,128)(2,1)S(1)}, u32[]{:S(2)}, u32[]{:S(2)}) async-start(bf16[8,272,128]{2,1,0:T(8,128)(2,1)} %merge_pair.1), calls=%async_computation | async-start | bytes 1114112 | tf_op jit(solution)/shard_map/all_to_all | solution.py:498

commit v6 on v5

--- a/solution.py
+++ b/solution.py
@@ -56,49 +56,50 @@
     return device_at(lax.axis_index("seg"), lax.axis_index("blk"), *slot)
 
 
-def queries_kernel(twin_ref, own_ref, qt_ref):
+def queries_kernel(twin_ref, own_hbm, len_hbm, qt_ref, filled_ref, own_ref, len_ref, sems):
+    own_copy = pltpu.make_async_copy(own_hbm, own_ref, sems.at[0])
+    len_copy = pltpu.make_async_copy(len_hbm, len_ref, sems.at[1])
+    own_copy.start()
+    len_copy.start()
     for number, q_ref in enumerate((twin_ref, own_ref)):
+        if number == 1:
+            own_copy.wait()
         for h in range(HEADS):
             scaled = q_ref[:, h * HD : (h + 1) * HD].astype(F32).T * SCALE
             high = scaled.astype(BF16)
             cols = slice(number * PART + h * TOK, number * PART + (h + 1) * TOK)
             qt_ref[0:HD, cols] = high
             qt_ref[HD : 2 * HD, cols] = (scaled - high.astype(F32)).astype(BF16)
+    len_copy.wait()
+    for j, slot in enumerate(SLOT_ORDER):
+        filled_ref[j : j + 1, :] = jnp.full((1, 128), len_ref[origin(slot)], jnp.int32)
 
 
 def in_hbm(array):
     return pltpu.with_memory_space_constraint(array, pltpu.HBM)
 
 
-def pack_kernel(cache_ref, new_ref, q_ref, len_ref, out_ref, q_out, filled_ref, len_copy, sems):
+def pack_kernel(cache_ref, new_ref, out_ref, sems):
     copies = [
         pltpu.make_async_copy(cache_ref.at[0:FILL], out_ref.at[0:FILL], sems.at[0]),
         pltpu.make_async_copy(new_ref, out_ref.at[FILL : FILL + TOK], sems.at[1]),
-        pltpu.make_async_copy(q_ref, q_out, sems.at[2]),
-        pltpu.make_async_copy(len_ref, len_copy, sems.at[3]),
     ]
     for copy in copies:
         copy.start()
-    for copy in reversed(copies):
+    for copy in copies:
         copy.wait()
-    for j, slot in enumerate(SLOT_ORDER):
-        filled_ref[j : j + 1, :] = jnp.full((1, 128), len_copy[origin(slot)], jnp.int32)
-
-
-def pack(cache_kv, new_kv, queries, cache_len):
+
+
+def pack(cache_kv, new_kv):
     return pl.pallas_call(
         pack_kernel,
-        in_specs=[pl.BlockSpec(memory_space=pltpu.HBM)] * 4,
-        out_specs=[VMEM] * 3,
-        out_shape=[
-            jax.ShapeDtypeStruct((FILL + TOK, 2 * HD), BF16),
-            jax.ShapeDtypeStruct(queries.shape, BF16),
-            jax.ShapeDtypeStruct((len(SLOT_ORDER), 128), jnp.int32),
-        ],
-        scratch_shapes=[pltpu.SMEM(cache_len.shape, jnp.int32), pltpu.SemaphoreType.DMA((4,))],
+        in_specs=[pl.BlockSpec(memory_space=pltpu.HBM)] * 2,
+        out_specs=VMEM,
+        out_shape=jax.ShapeDtypeStruct((FILL + TOK, 2 * HD), BF16),
+        scratch_shapes=[pltpu.SemaphoreType.DMA((2,))],
         compiler_params=pltpu.CompilerParams(vmem_limit_bytes=1 << 20),
         name="pack",
-    )(*map(in_hbm, (cache_kv, new_kv, queries, cache_len)))
+    )(in_hbm(cache_kv), in_hbm(new_kv))
 
 
 def gather_keys(slots, blocks, fresh_ref, filled_ref, keys, vals, vals_t):
@@ -456,23 +457,32 @@
     return lax.optimization_barrier((values, other))
 
 
-def scaled_queries(twin, own):
+def scaled_queries(twin, own, cache_len):
     return pl.pallas_call(
         queries_kernel,
-        in_specs=[VMEM, VMEM],
-        out_specs=VMEM,
-        out_shape=jax.ShapeDtypeStruct((2 * HD, ROWS), BF16),
+        in_specs=[VMEM] + [pl.BlockSpec(memory_space=pltpu.HBM)] * 2,
+        out_specs=[VMEM, VMEM],
+        out_shape=[
+            jax.ShapeDtypeStruct((2 * HD, ROWS), BF16),
+            jax.ShapeDtypeStruct((len(SLOT_ORDER), 128), jnp.int32),
+        ],
+        scratch_shapes=[
+            pltpu.VMEM(own.shape, BF16),
+            pltpu.SMEM(cache_len.shape, jnp.int32),
+            pltpu.SemaphoreType.DMA((2,)),
+        ],
         compiler_params=pltpu.CompilerParams(vmem_limit_bytes=4 << 20),
         name="scaled_queries",
-    )(twin, own)
+    )(twin, in_hbm(own), in_hbm(cache_len))
 
 
 def on_device(queries, new_kv, cache_kv, cache_len, page_owner):
-    own, own_queries, filled = pack(cache_kv, new_kv, queries, cache_len)
+    own = pack(cache_kv, new_kv)
     across = shift(own, flip_z=True)
     opposite = shift(own, 2)
     beside = {(1, False, False): shift(own, 1), (-1, False, False): shift(own, -1)}
-    qt = scaled_queries(shift(own_queries, flip_core=True), own_queries)
+    twin_queries = shift(after(queries, own)[0], flip_core=True)
+    qt, filled = scaled_queries(twin_queries, queries, cache_len)
     held = {(0, False, False): own}
     everything = dict(held)
     state = flash(held, filled, qt, None)

time: 54.7 us -> 54.3 us (level)
  starting transfers between devices: 19.1 us -> 18.3 us
    ppermute x10, starting transfers between devices: 14.9 us -> 14.1 us  [shift(): return lax.ppermute(block, AXES, neighbours(-dx, flip_z, flip_core))]
    pallas_call x1, Pallas kernels: 0.57 us -> 1.42 us  [scaled_queries(): pl.pallas_call(queries_kernel, in_specs=[VMEM] + [pl.BlockSpec(memory_spa...]
  transfers between devices with their start and end apart: 11 -> 11, of which waited for: 4 -> 4; matrix products, arithmetic and copies ran while one was open for 0% -> 0% of each run, Pallas kernels for 37% -> 38%
where the time goes in v6:
time: 54.3 us; the launch traced here: 54 us
  Pallas kernels  26.4 us (49%)
  starting transfers between devices  18.3 us (34%)
  waiting for transfers between devices  8.6 us (16%)
  between operations  0.79 us (1%)
    pallas_call x5, Pallas kernels, flash_call(): pl.pallas_call(kernel, in_specs=[VMEM] * len(operands), out_specs=jax.tre...  19.9 us
    ppermute x10, starting transfers between devices, shift(): return lax.ppermute(block, AXES, neighbours(-dx, flip_z, flip_core))  14.1 us
    all_to_all x1, waiting for transfers between devices, on_device(): parts = lax.all_to_all(part, 'seg', 0, 0)  7.37 us
    all_to_all x1, starting transfers between devices, on_device(): parts = lax.all_to_all(part, 'seg', 0, 0)  4.2 us
    pallas_call x1, Pallas kernels, write_pages(): pl.pallas_call(pages_kernel, in_specs=[SMEM] + [VMEM] * 4, out_specs=VMEM...  2.04 us
    pallas_call x1, Pallas kernels, scaled_queries(): pl.pallas_call(queries_kernel, in_specs=[VMEM] + [pl.BlockSpec(memory_spa...  1.42 us
    ppermute x10, waiting for transfers between devices, shift(): return lax.ppermute(block, AXES, neighbours(-dx, flip_z, flip_core))  1.23 us
  transfers between devices with their start and end apart: 11, of which 4 were waited for; matrix products, arithmetic and copies ran while one was open for 0% of the time, Pallas kernels for 38%

profile of v6, /device:TPU:1, one launch (start us, length us, event | category | flops | bytes accessed | tf_op | source)
XLA Modules:
  0.0 54.0 jit_solution(11861735492554980343)
XLA Ops:
  0.6 1.0 %pack.1.refs_2_.refs_0_ = bf16[576,256]{1,0:T(8,128)(2,1)S(1)} custom-call(bf16[512,256]{1,0:T(8,128)(2,1)} %cache_ref.3, bf16[128,256]{1,0:T(8,128)(2,1)} %new_ref.1), custom_call_target="tpu_custom_call" | custom-call | tf_op jit(solution)/shard_map/pack/pallas_call | solution.py:94
  1.6 1.5 %collective-permute-start = (bf16[128,2048]{1,0:T(8,128)(2,1)}, bf16[128,2048]{1,0:T(8,128)(2,1)S(1)}, u32[]{:S(2)}, u32[]{:S(2)}) collective-permute-start(bf16[128,2048]{1,0:T(8,128)(2,1)} %own_hbm.1), channel_id=1, source_target_pairs={{0,1},{1,0},{2,3},{3,2},{4,5},{5,4},{6,7},{7,6},{8,9},{9,8},{10,11... | collective-permute-start | bytes 1572872 | tf_op jit(solution)/shard_map/ppermute | solution.py:453
  3.1 3.9 %collective-permute-start.1 = (bf16[576,256]{1,0:T(8,128)(2,1)S(1)}, bf16[576,256]{1,0:T(8,128)(2,1)S(1)}, u32[]{:S(2)}, u32[]{:S(2)}) collective-permute-start(bf16[576,256]{1,0:T(8,128)(2,1)S(1)} %pack.1.refs_2_.refs_0_), channel_id=1, source_target_pairs={{0,24},{1,25},{2,26},{3,27},{4,28},{5,29},{6,30},{7,31},{8,16},{9,... | collective-permute-start | bytes 884744 | tf_op jit(solution)/shard_map/ppermute | solution.py:453
  7.0 2.7 %collective-permute-start.4 = (bf16[576,256]{1,0:T(8,128)(2,1)S(1)}, bf16[576,256]{1,0:T(8,128)(2,1)S(1)}, u32[]{:S(2)}, u32[]{:S(2)}) collective-permute-start(bf16[576,256]{1,0:T(8,128)(2,1)S(1)} %pack.1.refs_2_.refs_0_), channel_id=1, source_target_pairs={{0,4},{1,5},{2,6},{3,7},{4,0},{5,1},{6,2},{7,3},{8,12},{9,13},{10,... | collective-permute-start | bytes 884744 | tf_op jit(solution)/shard_map/ppermute | solution.py:453
  9.7 0.9 %collective-permute-start.7 = (bf16[576,256]{1,0:T(8,128)(2,1)S(1)}, bf16[576,256]{1,0:T(8,128)(2,1)S(1)}, u32[]{:S(2)}, u32[]{:S(2)}) collective-permute-start(bf16[576,256]{1,0:T(8,128)(2,1)S(1)} %pack.1.refs_2_.refs_0_), channel_id=1, source_target_pairs={{0,6},{1,7},{2,0},{3,1},{4,2},{5,3},{6,4},{7,5},{8,14},{9,15},{10,... | collective-permute-start | bytes 884744 | tf_op jit(solution)/shard_map/ppermute | solution.py:453
  10.6 0.6 %collective-permute-start.6 = (bf16[576,256]{1,0:T(8,128)(2,1)S(1)}, bf16[576,256]{1,0:T(8,128)(2,1)S(1)}, u32[]{:S(2)}, u32[]{:S(2)}) collective-permute-start(bf16[576,256]{1,0:T(8,128)(2,1)S(1)} %pack.1.refs_2_.refs_0_), channel_id=1, source_target_pairs={{0,2},{1,3},{2,4},{3,5},{4,6},{5,7},{6,0},{7,1},{8,10},{9,11},{10,... | collective-permute-start | bytes 884744 | tf_op jit(solution)/shard_map/ppermute | solution.py:453
  11.2 0.0 collective-permute-done.twin_ref
  11.2 1.4 %scaled_queries.1 = (bf16[256,4096]{1,0:T(8,128)(2,1)S(1)}, s32[8,128]{1,0:T(8,128)S(1)}) custom-call(bf16[128,2048]{1,0:T(8,128)(2,1)S(1)} %collective-permute-done.twin_ref, bf16[128,2048]{1,0:T(8,128)(2,1)} %own_hbm.1, s32[128]{0:T(128)} %len_ref.1), custom_call_target="tpu_custom_call" | custom-call | tf_op jit(solution)/shard_map/scaled_queries/pallas_call | solution.py:461
  12.6 2.9 %flash_1.1 = (f32[8,4096]{1,0:T(8,128)S(1)}, f32[144,4096]{1,0:T(8,128)S(1)}) custom-call(s32[8,128]{1,0:T(8,128)S(1)} %get-tuple-element.35.refs_0_, bf16[256,4096]{1,0:T(8,128)(2,1)S(1)} %get-tuple-element.34.refs_1_.qt_ref, bf16[576,256]{1,0:T(8,128)(2,1)S(1)} %pack.1.refs_2_.refs_0_), custom_call_target="tpu_custom_call" | custom-call | flops 2147483648 | bytes 1048576 | tf_op jit(solution)/shard_map/flash_1/pallas_call | solution.py:256
  15.5 0.0 collective-permute-done.1.refs_2_.refs_1_
  15.5 2.1 %collective-permute-start.3 = (bf16[576,256]{1,0:T(8,128)(2,1)S(1)}, bf16[576,256]{1,0:T(8,128)(2,1)S(1)}, u32[]{:S(2)}, u32[]{:S(2)}) collective-permute-start(bf16[576,256]{1,0:T(8,128)(2,1)S(1)} %collective-permute-done.1.refs_2_.refs_1_), channel_id=1, source_target_pairs={{0,6},{1,7},{2,0},{3,1},{4,2},{5,3},{6,4},{7,5},{8,14},{9,15},{10,... | collective-permute-start | bytes 884744 | tf_op jit(solution)/shard_map/ppermute | solution.py:453
  17.7 0.0 collective-permute-start.2
  17.7 0.0 collective-permute-done.4.refs_3_.refs_2_
  17.7 1.5 %collective-permute-start.5 = (bf16[576,256]{1,0:T(8,128)(2,1)S(1)}, bf16[576,256]{1,0:T(8,128)(2,1)S(1)}, u32[]{:S(2)}, u32[]{:S(2)}) collective-permute-start(bf16[576,256]{1,0:T(8,128)(2,1)S(1)} %collective-permute-done.4.refs_3_.refs_2_), channel_id=1, source_target_pairs={{0,24},{1,25},{2,26},{3,27},{4,28},{5,29},{6,30},{7,31},{8,16},{9,... | collective-permute-start | bytes 884744 | tf_op jit(solution)/shard_map/ppermute | solution.py:453
  19.2 4.4 %flash_2.2 = (f32[8,4096]{1,0:T(8,128)S(1)}, f32[144,4096]{1,0:T(8,128)S(1)}) custom-call(s32[8,128]{1,0:T(8,128)S(1)} %get-tuple-element.35.refs_0_, bf16[256,4096]{1,0:T(8,128)(2,1)S(1)} %get-tuple-element.34.refs_1_.qt_ref, bf16[576,256]{1,0:T(8,128)(2,1)S(1)} %collective-permute-done.1.refs_2_.refs_1_, ...), custom_call_target="tpu_custom_call" | custom-call | flops 3758096384 | bytes 1048576 | tf_op jit(solution)/shard_map/flash_2/pallas_call | solution.py:256
  23.6 0.0 collective-permute-done.7.refs_4_.refs_3_
  23.6 0.1 collective-permute-done.6.refs_3_.refs_2_
  23.8 5.1 %flash_2.3 = (f32[8,4096]{1,0:T(8,128)S(1)}, f32[144,4096]{1,0:T(8,128)S(1)}) custom-call(s32[8,128]{1,0:T(8,128)S(1)} %get-tuple-element.35.refs_0_, bf16[256,4096]{1,0:T(8,128)(2,1)S(1)} %get-tuple-element.34.refs_1_.qt_ref, bf16[576,256]{1,0:T(8,128)(2,1)S(1)} %collective-permute-done.6.refs_3_.refs_2_, ...), custom_call_target="tpu_custom_call" | custom-call | flops 4294967296 | bytes 1048576 | tf_op jit(solution)/shard_map/flash_2/pallas_call | solution.py:256
  28.9 0.0 collective-permute-done.5.refs_2_.refs_4_.refs_7_
  28.9 0.6 %collective-permute-done.3.refs_1_.refs_3_.refs_6_ = bf16[576,256]{1,0:T(8,128)(2,1)S(1)} collective-permute-done((bf16[576,256]{1,0:T(8,128)(2,1)S(1)}, bf16[576,256]{1,0:T(8,128)(2,1)S(1)}, u32[]{:S(2)}, u32[]{:S(2)}) %collective-permute-start.3) | collective-permute-done | bytes 294944 | tf_op jit(solution)/shard_map/ppermute | solution.py:453
  29.5 0.6 %collective-permute-done.2.refs_0_.refs_2_.refs_5_ = bf16[576,256]{1,0:T(8,128)(2,1)S(1)} collective-permute-done((bf16[576,256]{1,0:T(8,128)(2,1)S(1)}, bf16[576,256]{1,0:T(8,128)(2,1)S(1)}, u32[]{:S(2)}, u32[]{:S(2)}) %collective-permute-start.2) | collective-permute-done | bytes 294944 | tf_op jit(solution)/shard_map/ppermute | solution.py:453
  30.1 3.9 %flash_twin.1 = (bf16[8,272,128]{2,1,0:T(8,128)(2,1)S(1)}, bf16[1408,256]{1,0:T(8,128)(2,1)S(1)}, bf16[144,1408]{1,0:T(8,128)(2,1)S(1)}) custom-call(s32[8,128]{1,0:T(8,128)S(1)} %get-tuple-element.35.refs_0_, bf16[256,4096]{1,0:T(8,128)(2,1)S(1)} %get-tuple-element.34.refs_1_.qt_ref, bf16[576,256]{1,0:T(8,128)(2,1)S(1)} %collective-permute-done.2.refs_0_.refs_2_.refs_5_, ...), custom_call_target="tpu_custom_call" | custom-call | flops 2952790016 | bytes 1048576 | tf_op jit(solution)/shard_map/flash_twin/pallas_call | solution.py:256
  33.9 0.7 %collective-permute-start.8 = (bf16[8,272,128]{2,1,0:T(8,128)(2,1)S(1)}, bf16[8,272,128]{2,1,0:T(8,128)(2,1)S(1)}, u32[]{:S(2)}, u32[]{:S(2)}) collective-permute-start(bf16[8,272,128]{2,1,0:T(8,128)(2,1)S(1)} %get-tuple-element.63), channel_id=1, source_target_pairs={{0,1},{1,0},{2,3},{3,2},{4,5},{5,4},{6,7},{7,6},{8,9},{9,8},{10,11... | collective-permute-start | bytes 1671176 | tf_op jit(solution)/shard_map/ppermute | solution.py:453
  34.6 0.1 new_rows.1.own_ref
  34.8 0.1 collective-permute-start.9
  34.9 3.6 %flash_own.1.own_ref = bf16[8,272,128]{2,1,0:T(8,128)(2,1)S(1)} custom-call(bf16[256,4096]{1,0:T(8,128)(2,1)S(1)} %get-tuple-element.34.refs_1_.qt_ref, bf16[1408,256]{1,0:T(8,128)(2,1)S(1)} %get-tuple-element.61.keys, bf16[144,1408]{1,0:T(8,128)(2,1)S(1)} %get-tuple-element.62.vals_t, s32[64,128]{1,0:T(8,128)S(1)} %get-tuple-element.58.refs_6_.place_ref, ...), custom_call_target="tpu_custom_call" | custom-call | flops 2952790016 | bytes 1048576 | tf_op jit(solution)/shard_map/flash_own/pallas_call | solution.py:256
  38.5 0.0 copy-start
  38.5 0.0 copy-start.1
  38.5 0.0 copy-start.2
  38.5 0.0 collective-permute-done.8.twin_ref
  38.5 1.0 %merge_pair.1 = bf16[8,272,128]{2,1,0:T(8,128)(2,1)} custom-call(bf16[8,272,128]{2,1,0:T(8,128)(2,1)S(1)} %flash_own.1.own_ref, bf16[8,272,128]{2,1,0:T(8,128)(2,1)S(1)} %collective-permute-done.8.twin_ref), custom_call_target="tpu_custom_call" | custom-call | tf_op jit(solution)/shard_map/merge_pair/pallas_call | solution.py:417
  39.6 4.2 %all-to-all-start = ((bf16[8,272,128]{2,1,0:T(8,128)(2,1)}), bf16[8,272,128]{2,1,0:T(8,128)(2,1)S(1)}, u32[]{:S(2)}, u32[]{:S(2)}) async-start(bf16[8,272,128]{2,1,0:T(8,128)(2,1)} %merge_pair.1), calls=%async_computation | async-start | bytes 1114112 | tf_op jit(solution)/shard_map/all_to_all | solution.py:508
  43.8 0.0 collective-permute-done.9.twin_ref
  43.8 0.0 copy-done
  43.8 0.0 copy-done.1
  43.8 0.0 copy-done.2
  43.8 2.0 %write_pages.1 = bf16[512,256]{1,0:T(8,128)(2,1)} custom-call(s32[128]{0:T(128)S(1)} %copy-done.1, s32[1,256]{1,0:T(1,128)S(1)} %bitcast.1, bf16[512,256]{1,0:T(8,128)(2,1)S(1)} %copy-done, bf16[1024,256]{1,0:T(8,128)(2,1)S(1)} %new_rows.1.own_ref, bf16[1024,256]{1,0:T(8,128)(2,1)S(1)} %collective-permute-done.9.twin_ref), custom_call_target="tpu_custom_call" | custom-call | flops 1000000000 | bytes 2097152 | tf_op jit(solution)/shard_map/write_pages/pallas_call | solution.py:384
  45.8 7.4 %all-to-all-done.parts_ref = bf16[8,272,128]{2,1,0:T(8,128)(2,1)S(1)} async-done(((bf16[8,272,128]{2,1,0:T(8,128)(2,1)}), bf16[8,272,128]{2,1,0:T(8,128)(2,1)S(1)}, u32[]{:S(2)}, u32[]{:S(2)}) %all-to-all-start) | async-done | bytes 557088 | tf_op jit(solution)/shard_map/all_to_all | solution.py:508
  53.2 0.8 %merge.1 = bf16[128,256]{1,0:T(8,128)(2,1)} custom-call(bf16[8,272,128]{2,1,0:T(8,128)(2,1)S(1)} %all-to-all-done.parts_ref), custom_call_target="tpu_custom_call" | custom-call | tf_op jit(solution)/shard_map/merge/pallas_call | solution.py:442
  (2 shorter events, 0.0 us)
Async XLA Ops:
  1.6 9.6 %collective-permute-start = (bf16[128,2048]{1,0:T(8,128)(2,1)}, bf16[128,2048]{1,0:T(8,128)(2,1)S(1)}, u32[]{:S(2)}, u32[]{:S(2)}) collective-permute-start(bf16[128,2048]{1,0:T(8,128)(2,1)} %own_hbm.1), channel_id=1, source_target_pairs={{0,1},{1,0},{2,3},{3,2},{4,5},{5,4},{6,7},{7,6},{8,9},{9,8},{10,11... | collective-permute-start | bytes 1572872 | tf_op jit(solution)/shard_map/ppermute | solution.py:453
  3.1 12.4 %collective-permute-start.1 = (bf16[576,256]{1,0:T(8,128)(2,1)S(1)}, bf16[576,256]{1,0:T(8,128)(2,1)S(1)}, u32[]{:S(2)}, u32[]{:S(2)}) collective-permute-start(bf16[576,256]{1,0:T(8,128)(2,1)S(1)} %pack.1.refs_2_.refs_0_), channel_id=1, source_target_pairs={{0,24},{1,25},{2,26},{3,27},{4,28},{5,29},{6,30},{7,31},{8,16},{9,... | collective-permute-start | bytes 884744 | tf_op jit(solution)/shard_map/ppermute | solution.py:453
  7.0 10.7 %collective-permute-start.4 = (bf16[576,256]{1,0:T(8,128)(2,1)S(1)}, bf16[576,256]{1,0:T(8,128)(2,1)S(1)}, u32[]{:S(2)}, u32[]{:S(2)}) collective-permute-start(bf16[576,256]{1,0:T(8,128)(2,1)S(1)} %pack.1.refs_2_.refs_0_), channel_id=1, source_target_pairs={{0,4},{1,5},{2,6},{3,7},{4,0},{5,1},{6,2},{7,3},{8,12},{9,13},{10,... | collective-permute-start | bytes 884744 | tf_op jit(solution)/shard_map/ppermute | solution.py:453
  9.7 13.9 %collective-permute-start.7 = (bf16[576,256]{1,0:T(8,128)(2,1)S(1)}, bf16[576,256]{1,0:T(8,128)(2,1)S(1)}, u32[]{:S(2)}, u32[]{:S(2)}) collective-permute-start(bf16[576,256]{1,0:T(8,128)(2,1)S(1)} %pack.1.refs_2_.refs_0_), channel_id=1, source_target_pairs={{0,6},{1,7},{2,0},{3,1},{4,2},{5,3},{6,4},{7,5},{8,14},{9,15},{10,... | collective-permute-start | bytes 884744 | tf_op jit(solution)/shard_map/ppermute | solution.py:453
  10.6 13.1 %collective-permute-start.6 = (bf16[576,256]{1,0:T(8,128)(2,1)S(1)}, bf16[576,256]{1,0:T(8,128)(2,1)S(1)}, u32[]{:S(2)}, u32[]{:S(2)}) collective-permute-start(bf16[576,256]{1,0:T(8,128)(2,1)S(1)} %pack.1.refs_2_.refs_0_), channel_id=1, source_target_pairs={{0,2},{1,3},{2,4},{3,5},{4,6},{5,7},{6,0},{7,1},{8,10},{9,11},{10,... | collective-permute-start | bytes 884744 | tf_op jit(solution)/shard_map/ppermute | solution.py:453
  15.5 13.9 %collective-permute-start.3 = (bf16[576,256]{1,0:T(8,128)(2,1)S(1)}, bf16[576,256]{1,0:T(8,128)(2,1)S(1)}, u32[]{:S(2)}, u32[]{:S(2)}) collective-permute-start(bf16[576,256]{1,0:T(8,128)(2,1)S(1)} %collective-permute-done.1.refs_2_.refs_1_), channel_id=1, source_target_pairs={{0,6},{1,7},{2,0},{3,1},{4,2},{5,3},{6,4},{7,5},{8,14},{9,15},{10,... | collective-permute-start | bytes 884744 | tf_op jit(solution)/shard_map/ppermute | solution.py:453
  17.7 12.4 %collective-permute-start.2 = (bf16[576,256]{1,0:T(8,128)(2,1)S(1)}, bf16[576,256]{1,0:T(8,128)(2,1)S(1)}, u32[]{:S(2)}, u32[]{:S(2)}) collective-permute-start(bf16[576,256]{1,0:T(8,128)(2,1)S(1)} %collective-permute-done.1.refs_2_.refs_1_), channel_id=1, source_target_pairs={{0,2},{1,3},{2,4},{3,5},{4,6},{5,7},{6,0},{7,1},{8,10},{9,11},{10,... | collective-permute-start | bytes 884744 | tf_op jit(solution)/shard_map/ppermute | solution.py:453
  17.7 11.2 %collective-permute-start.5 = (bf16[576,256]{1,0:T(8,128)(2,1)S(1)}, bf16[576,256]{1,0:T(8,128)(2,1)S(1)}, u32[]{:S(2)}, u32[]{:S(2)}) collective-permute-start(bf16[576,256]{1,0:T(8,128)(2,1)S(1)} %collective-permute-done.4.refs_3_.refs_2_), channel_id=1, source_target_pairs={{0,24},{1,25},{2,26},{3,27},{4,28},{5,29},{6,30},{7,31},{8,16},{9,... | collective-permute-start | bytes 884744 | tf_op jit(solution)/shard_map/ppermute | solution.py:453
  33.9 4.6 %collective-permute-start.8 = (bf16[8,272,128]{2,1,0:T(8,128)(2,1)S(1)}, bf16[8,272,128]{2,1,0:T(8,128)(2,1)S(1)}, u32[]{:S(2)}, u32[]{:S(2)}) collective-permute-start(bf16[8,272,128]{2,1,0:T(8,128)(2,1)S(1)} %get-tuple-element.63), channel_id=1, source_target_pairs={{0,1},{1,0},{2,3},{3,2},{4,5},{5,4},{6,7},{7,6},{8,9},{9,8},{10,11... | collective-permute-start | bytes 1671176 | tf_op jit(solution)/shard_map/ppermute | solution.py:453
  34.8 9.0 %collective-permute-start.9 = (bf16[1024,256]{1,0:T(8,128)(2,1)S(1)}, bf16[1024,256]{1,0:T(8,128)(2,1)S(1)}, u32[]{:S(2)}, u32[]{:S(2)}) collective-permute-start(bf16[1024,256]{1,0:T(8,128)(2,1)S(1)} %new_rows.1.own_ref), channel_id=1, source_target_pairs={{0,1},{1,0},{2,3},{3,2},{4,5},{5,4},{6,7},{7,6},{8,9},{9,8},{10,11... | collective-permute-start | bytes 1572872 | tf_op jit(solution)/shard_map/ppermute | solution.py:453
  38.5 5.3 %copy-start = (bf16[512,256]{1,0:T(8,128)(2,1)S(1)}, bf16[512,256]{1,0:T(8,128)(2,1)}, u32[]{:S(2)}) copy-start(bf16[512,256]{1,0:T(8,128)(2,1)} %cache_ref.3) | copy-start | bytes 786436
  38.5 5.3 %copy-start.1 = (s32[128]{0:T(128)S(1)}, s32[128]{0:T(128)}, u32[]{:S(2)}) copy-start(s32[128]{0:T(128)} %len_ref.1) | copy-start | bytes 1540
  38.5 5.3 %copy-start.2 = (s32[256,1]{0,1:T(1,128)S(1)}, s32[256,1]{0,1:T(1,128)}, u32[]{:S(2)}) copy-start(s32[256,1]{0,1:T(1,128)} %param.9) | copy-start | bytes 3076
  39.6 13.6 %all-to-all-start = ((bf16[8,272,128]{2,1,0:T(8,128)(2,1)}), bf16[8,272,128]{2,1,0:T(8,128)(2,1)S(1)}, u32[]{:S(2)}, u32[]{:S(2)}) async-start(bf16[8,272,128]{2,1,0:T(8,128)(2,1)} %merge_pair.1), calls=%async_computation | async-start | bytes 1114112 | tf_op jit(solution)/shard_map/all_to_all | solution.py:508

commit v7 on v6

--- a/solution.py
+++ b/solution.py
@@ -30,7 +30,7 @@
 VMEM = pl.BlockSpec(memory_space=pltpu.VMEM)
 SMEM = pl.BlockSpec(memory_space=pltpu.SMEM)
 AXES = ("seg", "blk")
-SLOT_ORDER = [(dx, flip_z, False) for flip_z in (False, True) for dx in (0, 1, -1, 2)]
+SLOT_ORDER = [(dx, flip_z, False) for flip_z in (False, True) for dx in (0, 1, 3, 2)]
 
 
 def neighbours(dx=0, flip_z=False, flip_core=False):
@@ -48,7 +48,7 @@
         z_lo, z_hi = 1 - z_lo, 1 - z_hi
     if flip_core:
         core = 1 - core
-    x = (x + dx) % 4
+    x = x ^ dx
     return (y * 2 + z_lo) * NBLK + z_hi * 8 + x * 2 + core
 
 
@@ -143,7 +143,9 @@
         vals_t[HD:ACC, low:high] = one.astype(F32).astype(BF16)
 
 
-def flash_columns(columns, old, keys, vals_t, qt_ref, state, even_ref, odd_ref, place_ref, emit):
+def flash_columns(
+    columns, old, keys, vals_t, qt_ref, state, even_ref, odd_ref, place_ref, emit, given=None, handed=None
+):
     total, width = even_ref.shape
     first, last = columns[0] // width, columns[1] // width
 
@@ -181,14 +183,17 @@
         emit(r - first, cols, out, top)
         return tops
 
-    def two(i, tops, more=True):
-        tops = weigh(first + 2 * i, tops, even_ref, odd_ref)
-        return weigh(first + 2 * i + 1, tops, odd_ref, even_ref if more else None)
+    def two(i, tops, here_ref, next_ref):
+        tops = weigh(first + 2 * i, tops, here_ref, odd_ref)
+        return weigh(first + 2 * i + 1, tops, odd_ref, next_ref)
 
     pairs = (last - first) // 2
+    here_ref, tops = (even_ref, score(first, even_ref)) if given is None else (given[0], given[1][...])
     trips = jnp.minimum(lax.axis_index("seg") + pairs - 1, pairs - 1)
-    tops = lax.fori_loop(0, trips, two, score(first, even_ref))
-    two(pairs - 1, tops, False)
+    tops = lax.fori_loop(0, trips, lambda i, tops: two(i, tops, here_ref, even_ref), tops)
+    tops = two(pairs - 1, tops, even_ref, None if handed is None else handed[0])
+    if handed is not None:
+        handed[1][...] = tops
 
 
 def flash_kernel(slots, has_fresh, *refs):
@@ -240,16 +245,39 @@
 def twin_kernel(slots, *refs):
     filled_ref, qt_ref = refs[0], refs[1]
     blocks, refs = refs[2 : 2 + len(slots)], refs[2 + len(slots) :]
-    fresh_ref, place_ref, m_in, acc_in, part_ref, keys, vals_t, vals, even_ref, odd_ref = refs
+    fresh_ref, place_ref, m_in, acc_in, part_ref, keys, vals_t, scores_ref, tops_ref, vals, even_ref, odd_ref = refs
     gather_keys(slots, blocks, fresh_ref, filled_ref, keys, vals, vals_t)
     emit = emit_part(part_ref, even_ref.shape[1])
-    state, old = (m_in, acc_in), len(slots) * FILL
-    flash_columns((0, PART), old, keys, vals_t, qt_ref, state, even_ref, odd_ref, place_ref, emit)
-
-
-def own_kernel(old, qt_ref, keys, vals_t, place_ref, m_in, acc_in, part_ref, even_ref, odd_ref):
+    flash_columns(
+        (0, PART),
+        len(slots) * FILL,
+        keys,
+        vals_t,
+        qt_ref,
+        (m_in, acc_in),
+        even_ref,
+        odd_ref,
+        place_ref,
+        emit,
+        handed=(scores_ref, tops_ref),
+    )
+
+
+def own_kernel(old, qt_ref, keys, vals_t, scores_ref, tops_ref, place_ref, m_in, acc_in, part_ref, even_ref, odd_ref):
     emit = emit_part(part_ref, even_ref.shape[1])
-    flash_columns((PART, ROWS), old, keys, vals_t, qt_ref, (m_in, acc_in), even_ref, odd_ref, place_ref, emit)
+    flash_columns(
+        (PART, ROWS),
+        old,
+        keys,
+        vals_t,
+        qt_ref,
+        (m_in, acc_in),
+        even_ref,
+        odd_ref,
+        place_ref,
+        emit,
+        given=(scores_ref, tops_ref),
+    )
 
 
 def flash_call(kernel, operands, out_shape, scratch, total, rows, name, width=WIDTH):
@@ -290,17 +318,23 @@
     old = len(held) * FILL
     total = old + fresh[0].shape[0]
     part = jax.ShapeDtypeStruct((NSEG, CHUNK, TOK), BF16)
-    twin_part, keys, vals_t = flash_call(
+    twin_part, *handed = flash_call(
         functools.partial(twin_kernel, list(held)),
         [filled, qt, *held.values(), *fresh, *state],
-        [part, jax.ShapeDtypeStruct((total, 2 * HD), BF16), jax.ShapeDtypeStruct((ACC, total), BF16)],
+        [
+            part,
+            jax.ShapeDtypeStruct((total, 2 * HD), BF16),
+            jax.ShapeDtypeStruct((ACC, total), BF16),
+            jax.ShapeDtypeStruct((total, WIDTH), F32),
+            jax.ShapeDtypeStruct((8, WIDTH), F32),
+        ],
         [pltpu.VMEM((total, HD), BF16)],
         total,
         PART,
         "flash_twin",
     )
     own_part = flash_call(
-        functools.partial(own_kernel, old), [qt, keys, vals_t, fresh[1], *state], part, [], total, PART, "flash_own"
+        functools.partial(own_kernel, old), [qt, *handed, fresh[1], *state], part, [], total, PART, "flash_own"
     )
     return twin_part, own_part
 
@@ -450,7 +484,7 @@
 
 
 def shift(block, dx=0, flip_z=False, flip_core=False):
-    return lax.ppermute(block, AXES, neighbours(-dx, flip_z, flip_core))
+    return lax.ppermute(block, AXES, neighbours(dx, flip_z, flip_core))
 
 
 def after(values, other):
@@ -480,7 +514,7 @@
     own = pack(cache_kv, new_kv)
     across = shift(own, flip_z=True)
     opposite = shift(own, 2)
-    beside = {(1, False, False): shift(own, 1), (-1, False, False): shift(own, -1)}
+    beside = {(1, False, False): shift(own, 1), (3, False, False): shift(own, 3)}
     twin_queries = shift(after(queries, own)[0], flip_core=True)
     qt, filled = scaled_queries(twin_queries, queries, cache_len)
     held = {(0, False, False): own}
@@ -488,7 +522,7 @@
     state = flash(held, filled, qt, None)
 
     across, state = after(across, state)
-    far = {(1, True, False): shift(across, 1), (-1, True, False): shift(across, -1)}
+    far = {(1, True, False): shift(across, 1), (3, True, False): shift(across, 3)}
     opposite, state = after(opposite, state)
     far[2, True, False] = shift(opposite, flip_z=True)
     held = {(0, True, False): across, (2, False, False): opposite}

time: 54.3 us -> 53.8 us (level)
  Pallas kernels: 26.4 us -> 25.7 us
    pallas_call x5, Pallas kernels: 19.9 us -> 19.3 us  [flash_call(): pl.pallas_call(kernel, in_specs=[VMEM] * len(operands), out_specs=jax.tre...]
  transfers between devices with their start and end apart: 11 -> 11, of which waited for: 4 -> 3; matrix products, arithmetic and copies ran while one was open for 0% -> 0% of each run, Pallas kernels for 38% -> 37%
where the time goes in v7:
time: 53.8 us; the launch traced here: 53.6 us
  Pallas kernels  25.7 us (48%)
  starting transfers between devices  18.4 us (34%)
  waiting for transfers between devices  8.63 us (16%)
  between operations  0.79 us (1%)
    pallas_call x5, Pallas kernels, flash_call(): pl.pallas_call(kernel, in_specs=[VMEM] * len(operands), out_specs=jax.tre...  19.3 us
    ppermute x10, starting transfers between devices, shift(): return lax.ppermute(block, AXES, neighbours(dx, flip_z, flip_core))  14.2 us
    all_to_all x1, waiting for transfers between devices, on_device(): parts = lax.all_to_all(part, 'seg', 0, 0)  7.36 us
    all_to_all x1, starting transfers between devices, on_device(): parts = lax.all_to_all(part, 'seg', 0, 0)  4.21 us
    pallas_call x1, Pallas kernels, write_pages(): pl.pallas_call(pages_kernel, in_specs=[SMEM] + [VMEM] * 4, out_specs=VMEM...  2.04 us
    pallas_call x1, Pallas kernels, scaled_queries(): pl.pallas_call(queries_kernel, in_specs=[VMEM] + [pl.BlockSpec(memory_spa...  1.42 us
    ppermute x10, waiting for transfers between devices, shift(): return lax.ppermute(block, AXES, neighbours(dx, flip_z, flip_core))  1.27 us
  transfers between devices with their start and end apart: 11, of which 3 were waited for; matrix products, arithmetic and copies ran while one was open for 0% of the time, Pallas kernels for 37%

profile of v7, /device:TPU:1, one launch (start us, length us, event | category | flops | bytes accessed | tf_op | source)
XLA Modules:
  0.0 53.6 jit_solution(5579167278420501988)
XLA Ops:
  0.6 1.0 %pack.1.refs_2_.refs_0_ = bf16[576,256]{1,0:T(8,128)(2,1)S(1)} custom-call(bf16[512,256]{1,0:T(8,128)(2,1)} %cache_ref.3, bf16[128,256]{1,0:T(8,128)(2,1)} %new_ref.1), custom_call_target="tpu_custom_call" | custom-call | tf_op jit(solution)/shard_map/pack/pallas_call | solution.py:94
  1.6 1.5 %collective-permute-start = (bf16[128,2048]{1,0:T(8,128)(2,1)}, bf16[128,2048]{1,0:T(8,128)(2,1)S(1)}, u32[]{:S(2)}, u32[]{:S(2)}) collective-permute-start(bf16[128,2048]{1,0:T(8,128)(2,1)} %own_hbm.1), channel_id=1, source_target_pairs={{0,1},{1,0},{2,3},{3,2},{4,5},{5,4},{6,7},{7,6},{8,9},{9,8},{10,11... | collective-permute-start | bytes 1572872 | tf_op jit(solution)/shard_map/ppermute | solution.py:487
  3.1 3.9 %collective-permute-start.1 = (bf16[576,256]{1,0:T(8,128)(2,1)S(1)}, bf16[576,256]{1,0:T(8,128)(2,1)S(1)}, u32[]{:S(2)}, u32[]{:S(2)}) collective-permute-start(bf16[576,256]{1,0:T(8,128)(2,1)S(1)} %pack.1.refs_2_.refs_0_), channel_id=1, source_target_pairs={{0,24},{1,25},{2,26},{3,27},{4,28},{5,29},{6,30},{7,31},{8,16},{9,... | collective-permute-start | bytes 884744 | tf_op jit(solution)/shard_map/ppermute | solution.py:487
  7.0 2.7 %collective-permute-start.3 = (bf16[576,256]{1,0:T(8,128)(2,1)S(1)}, bf16[576,256]{1,0:T(8,128)(2,1)S(1)}, u32[]{:S(2)}, u32[]{:S(2)}) collective-permute-start(bf16[576,256]{1,0:T(8,128)(2,1)S(1)} %pack.1.refs_2_.refs_0_), channel_id=1, source_target_pairs={{0,4},{1,5},{2,6},{3,7},{4,0},{5,1},{6,2},{7,3},{8,12},{9,13},{10,... | collective-permute-start | bytes 884744 | tf_op jit(solution)/shard_map/ppermute | solution.py:487
  9.7 0.9 %collective-permute-start.7 = (bf16[576,256]{1,0:T(8,128)(2,1)S(1)}, bf16[576,256]{1,0:T(8,128)(2,1)S(1)}, u32[]{:S(2)}, u32[]{:S(2)}) collective-permute-start(bf16[576,256]{1,0:T(8,128)(2,1)S(1)} %pack.1.refs_2_.refs_0_), channel_id=1, source_target_pairs={{0,6},{1,7},{2,4},{3,5},{4,2},{5,3},{6,0},{7,1},{8,14},{9,15},{10,... | collective-permute-start | bytes 884744 | tf_op jit(solution)/shard_map/ppermute | solution.py:487
  10.6 0.0 collective-permute-start.6
  10.6 0.0 collective-permute-done.twin_ref
  10.6 1.4 %scaled_queries.1 = (bf16[256,4096]{1,0:T(8,128)(2,1)S(1)}, s32[8,128]{1,0:T(8,128)S(1)}) custom-call(bf16[128,2048]{1,0:T(8,128)(2,1)S(1)} %collective-permute-done.twin_ref, bf16[128,2048]{1,0:T(8,128)(2,1)} %own_hbm.1, s32[128]{0:T(128)} %len_ref.1), custom_call_target="tpu_custom_call" | custom-call | tf_op jit(solution)/shard_map/scaled_queries/pallas_call | solution.py:495
  12.0 2.9 %flash_1.1 = (f32[8,4096]{1,0:T(8,128)S(1)}, f32[144,4096]{1,0:T(8,128)S(1)}) custom-call(s32[8,128]{1,0:T(8,128)S(1)} %get-tuple-element.37.refs_0_, bf16[256,4096]{1,0:T(8,128)(2,1)S(1)} %get-tuple-element.36.refs_1_.qt_ref, bf16[576,256]{1,0:T(8,128)(2,1)S(1)} %pack.1.refs_2_.refs_0_), custom_call_target="tpu_custom_call" | custom-call | flops 2147483648 | bytes 1048576 | tf_op jit(solution)/shard_map/flash_1/pallas_call | solution.py:284
  14.9 0.0 collective-permute-done.1.refs_2_.refs_1_
  14.9 1.9 %collective-permute-start.5 = (bf16[576,256]{1,0:T(8,128)(2,1)S(1)}, bf16[576,256]{1,0:T(8,128)(2,1)S(1)}, u32[]{:S(2)}, u32[]{:S(2)}) collective-permute-start(bf16[576,256]{1,0:T(8,128)(2,1)S(1)} %collective-permute-done.1.refs_2_.refs_1_), channel_id=1, source_target_pairs={{0,6},{1,7},{2,4},{3,5},{4,2},{5,3},{6,0},{7,1},{8,14},{9,15},{10,... | collective-permute-start | bytes 884744 | tf_op jit(solution)/shard_map/ppermute | solution.py:487
  16.8 0.9 %collective-permute-start.2 = (bf16[576,256]{1,0:T(8,128)(2,1)S(1)}, bf16[576,256]{1,0:T(8,128)(2,1)S(1)}, u32[]{:S(2)}, u32[]{:S(2)}) collective-permute-start(bf16[576,256]{1,0:T(8,128)(2,1)S(1)} %collective-permute-done.1.refs_2_.refs_1_), channel_id=1, source_target_pairs={{0,2},{1,3},{2,0},{3,1},{4,6},{5,7},{6,4},{7,5},{8,10},{9,11},{10,... | collective-permute-start | bytes 884744 | tf_op jit(solution)/shard_map/ppermute | solution.py:487
  17.7 0.0 collective-permute-done.3.refs_3_.refs_2_
  17.7 1.6 %collective-permute-start.4 = (bf16[576,256]{1,0:T(8,128)(2,1)S(1)}, bf16[576,256]{1,0:T(8,128)(2,1)S(1)}, u32[]{:S(2)}, u32[]{:S(2)}) collective-permute-start(bf16[576,256]{1,0:T(8,128)(2,1)S(1)} %collective-permute-done.3.refs_3_.refs_2_), channel_id=1, source_target_pairs={{0,24},{1,25},{2,26},{3,27},{4,28},{5,29},{6,30},{7,31},{8,16},{9,... | collective-permute-start | bytes 884744 | tf_op jit(solution)/shard_map/ppermute | solution.py:487
  19.2 4.4 %flash_2.2 = (f32[8,4096]{1,0:T(8,128)S(1)}, f32[144,4096]{1,0:T(8,128)S(1)}) custom-call(s32[8,128]{1,0:T(8,128)S(1)} %get-tuple-element.37.refs_0_, bf16[256,4096]{1,0:T(8,128)(2,1)S(1)} %get-tuple-element.36.refs_1_.qt_ref, bf16[576,256]{1,0:T(8,128)(2,1)S(1)} %collective-permute-done.1.refs_2_.refs_1_, ...), custom_call_target="tpu_custom_call" | custom-call | flops 3758096384 | bytes 1048576 | tf_op jit(solution)/shard_map/flash_2/pallas_call | solution.py:284
  23.6 0.1 collective-permute-done.7.refs_4_.refs_3_
  23.7 0.0 collective-permute-done.6.refs_3_.refs_2_
  23.8 5.1 %flash_2.3 = (f32[8,4096]{1,0:T(8,128)S(1)}, f32[144,4096]{1,0:T(8,128)S(1)}) custom-call(s32[8,128]{1,0:T(8,128)S(1)} %get-tuple-element.37.refs_0_, bf16[256,4096]{1,0:T(8,128)(2,1)S(1)} %get-tuple-element.36.refs_1_.qt_ref, bf16[576,256]{1,0:T(8,128)(2,1)S(1)} %collective-permute-done.6.refs_3_.refs_2_, ...), custom_call_target="tpu_custom_call" | custom-call | flops 4294967296 | bytes 1048576 | tf_op jit(solution)/shard_map/flash_2/pallas_call | solution.py:284
  28.9 0.0 collective-permute-done.4.refs_1_.refs_3_.refs_6_
  28.9 1.1 %collective-permute-done.5.refs_2_.refs_4_.refs_7_ = bf16[576,256]{1,0:T(8,128)(2,1)S(1)} collective-permute-done((bf16[576,256]{1,0:T(8,128)(2,1)S(1)}, bf16[576,256]{1,0:T(8,128)(2,1)S(1)}, u32[]{:S(2)}, u32[]{:S(2)}) %collective-permute-start.5) | collective-permute-done | bytes 294944 | tf_op jit(solution)/shard_map/ppermute | solution.py:487
  30.0 0.0 collective-permute-done.2.refs_0_.refs_2_.refs_5_
  30.1 3.8 %flash_twin.1 = (bf16[8,272,128]{2,1,0:T(8,128)(2,1)S(1)}, bf16[1408,256]{1,0:T(8,128)(2,1)S(1)}, bf16[144,1408]{1,0:T(8,128)(2,1)S(1)}, f32[1408,512]{1,0:T(8,128)S(1)}, f32[8,512]{1,0:T(8,128)S(1)}) custom-call(s32[8,128]{1,0:T(8,128)S(1)} %get-tuple-element.37.refs_0_, bf16[256,4096]{1,0:T(8,128)(2,1)S(1)} %get-tuple-element.36.refs_1_.qt_ref, ...), custom_call_target="tpu_custom_call" | custom-call | flops 2952790016 | bytes 1048576 | tf_op jit(solution)/shard_map/flash_twin/pallas_call | solution.py:284
  33.9 0.9 %collective-permute-start.8 = (bf16[8,272,128]{2,1,0:T(8,128)(2,1)S(1)}, bf16[8,272,128]{2,1,0:T(8,128)(2,1)S(1)}, u32[]{:S(2)}, u32[]{:S(2)}) collective-permute-start(bf16[8,272,128]{2,1,0:T(8,128)(2,1)S(1)} %get-tuple-element.67), channel_id=1, source_target_pairs={{0,1},{1,0},{2,3},{3,2},{4,5},{5,4},{6,7},{7,6},{8,9},{9,8},{10,11... | collective-permute-start | bytes 1671176 | tf_op jit(solution)/shard_map/ppermute | solution.py:487
  34.7 0.1 new_rows.1.own_ref
  34.9 0.1 collective-permute-start.9
  35.0 3.0 %flash_own.1.own_ref = bf16[8,272,128]{2,1,0:T(8,128)(2,1)S(1)} custom-call(bf16[256,4096]{1,0:T(8,128)(2,1)S(1)} %get-tuple-element.36.refs_1_.qt_ref, bf16[1408,256]{1,0:T(8,128)(2,1)S(1)} %get-tuple-element.63.keys, bf16[144,1408]{1,0:T(8,128)(2,1)S(1)} %get-tuple-element.64.vals_t, f32[1408,512]{1,0:T(8,128)S(1)} %get-tuple-element.65.scores_ref, ...), custom_call_target="tpu_custom_call" | custom-call | flops 2952790016 | bytes 1048576 | tf_op jit(solution)/shard_map/flash_own/pallas_call | solution.py:284
  38.0 0.0 copy-start
  38.0 0.0 copy-start.1
  38.0 0.0 copy-start.2
  38.0 0.0 collective-permute-done.8.twin_ref
  38.1 1.0 %merge_pair.1 = bf16[8,272,128]{2,1,0:T(8,128)(2,1)} custom-call(bf16[8,272,128]{2,1,0:T(8,128)(2,1)S(1)} %flash_own.1.own_ref, bf16[8,272,128]{2,1,0:T(8,128)(2,1)S(1)} %collective-permute-done.8.twin_ref), custom_call_target="tpu_custom_call" | custom-call | tf_op jit(solution)/shard_map/merge_pair/pallas_call | solution.py:451
  39.1 4.2 %all-to-all-start = ((bf16[8,272,128]{2,1,0:T(8,128)(2,1)}), bf16[8,272,128]{2,1,0:T(8,128)(2,1)S(1)}, u32[]{:S(2)}, u32[]{:S(2)}) async-start(bf16[8,272,128]{2,1,0:T(8,128)(2,1)} %merge_pair.1), calls=%async_computation | async-start | bytes 1114112 | tf_op jit(solution)/shard_map/all_to_all | solution.py:542
  43.3 0.0 collective-permute-done.9.twin_ref
  43.3 0.0 copy-done
  43.3 0.0 copy-done.1
  43.3 0.0 copy-done.2
  43.3 2.0 %write_pages.1 = bf16[512,256]{1,0:T(8,128)(2,1)} custom-call(s32[128]{0:T(128)S(1)} %copy-done.1, s32[1,256]{1,0:T(1,128)S(1)} %bitcast.1, bf16[512,256]{1,0:T(8,128)(2,1)S(1)} %copy-done, bf16[1024,256]{1,0:T(8,128)(2,1)S(1)} %new_rows.1.own_ref, bf16[1024,256]{1,0:T(8,128)(2,1)S(1)} %collective-permute-done.9.twin_ref), custom_call_target="tpu_custom_call" | custom-call | flops 1000000000 | bytes 2097152 | tf_op jit(solution)/shard_map/write_pages/pallas_call | solution.py:418
  45.4 7.4 %all-to-all-done.parts_ref = bf16[8,272,128]{2,1,0:T(8,128)(2,1)S(1)} async-done(((bf16[8,272,128]{2,1,0:T(8,128)(2,1)}), bf16[8,272,128]{2,1,0:T(8,128)(2,1)S(1)}, u32[]{:S(2)}, u32[]{:S(2)}) %all-to-all-start) | async-done | bytes 557088 | tf_op jit(solution)/shard_map/all_to_all | solution.py:542
  52.8 0.8 %merge.1 = bf16[128,256]{1,0:T(8,128)(2,1)} custom-call(bf16[8,272,128]{2,1,0:T(8,128)(2,1)S(1)} %all-to-all-done.parts_ref), custom_call_target="tpu_custom_call" | custom-call | tf_op jit(solution)/shard_map/merge/pallas_call | solution.py:476
  (2 shorter events, 0.1 us)
Async XLA Ops:
  1.6 9.0 %collective-permute-start = (bf16[128,2048]{1,0:T(8,128)(2,1)}, bf16[128,2048]{1,0:T(8,128)(2,1)S(1)}, u32[]{:S(2)}, u32[]{:S(2)}) collective-permute-start(bf16[128,2048]{1,0:T(8,128)(2,1)} %own_hbm.1), channel_id=1, source_target_pairs={{0,1},{1,0},{2,3},{3,2},{4,5},{5,4},{6,7},{7,6},{8,9},{9,8},{10,11... | collective-permute-start | bytes 1572872 | tf_op jit(solution)/shard_map/ppermute | solution.py:487
  3.1 11.8 %collective-permute-start.1 = (bf16[576,256]{1,0:T(8,128)(2,1)S(1)}, bf16[576,256]{1,0:T(8,128)(2,1)S(1)}, u32[]{:S(2)}, u32[]{:S(2)}) collective-permute-start(bf16[576,256]{1,0:T(8,128)(2,1)S(1)} %pack.1.refs_2_.refs_0_), channel_id=1, source_target_pairs={{0,24},{1,25},{2,26},{3,27},{4,28},{5,29},{6,30},{7,31},{8,16},{9,... | collective-permute-start | bytes 884744 | tf_op jit(solution)/shard_map/ppermute | solution.py:487
  7.0 10.7 %collective-permute-start.3 = (bf16[576,256]{1,0:T(8,128)(2,1)S(1)}, bf16[576,256]{1,0:T(8,128)(2,1)S(1)}, u32[]{:S(2)}, u32[]{:S(2)}) collective-permute-start(bf16[576,256]{1,0:T(8,128)(2,1)S(1)} %pack.1.refs_2_.refs_0_), channel_id=1, source_target_pairs={{0,4},{1,5},{2,6},{3,7},{4,0},{5,1},{6,2},{7,3},{8,12},{9,13},{10,... | collective-permute-start | bytes 884744 | tf_op jit(solution)/shard_map/ppermute | solution.py:487
  9.7 14.0 %collective-permute-start.7 = (bf16[576,256]{1,0:T(8,128)(2,1)S(1)}, bf16[576,256]{1,0:T(8,128)(2,1)S(1)}, u32[]{:S(2)}, u32[]{:S(2)}) collective-permute-start(bf16[576,256]{1,0:T(8,128)(2,1)S(1)} %pack.1.refs_2_.refs_0_), channel_id=1, source_target_pairs={{0,6},{1,7},{2,4},{3,5},{4,2},{5,3},{6,0},{7,1},{8,14},{9,15},{10,... | collective-permute-start | bytes 884744 | tf_op jit(solution)/shard_map/ppermute | solution.py:487
  10.6 13.2 %collective-permute-start.6 = (bf16[576,256]{1,0:T(8,128)(2,1)S(1)}, bf16[576,256]{1,0:T(8,128)(2,1)S(1)}, u32[]{:S(2)}, u32[]{:S(2)}) collective-permute-start(bf16[576,256]{1,0:T(8,128)(2,1)S(1)} %pack.1.refs_2_.refs_0_), channel_id=1, source_target_pairs={{0,2},{1,3},{2,0},{3,1},{4,6},{5,7},{6,4},{7,5},{8,10},{9,11},{10,... | collective-permute-start | bytes 884744 | tf_op jit(solution)/shard_map/ppermute | solution.py:487
  14.9 15.1 %collective-permute-start.5 = (bf16[576,256]{1,0:T(8,128)(2,1)S(1)}, bf16[576,256]{1,0:T(8,128)(2,1)S(1)}, u32[]{:S(2)}, u32[]{:S(2)}) collective-permute-start(bf16[576,256]{1,0:T(8,128)(2,1)S(1)} %collective-permute-done.1.refs_2_.refs_1_), channel_id=1, source_target_pairs={{0,6},{1,7},{2,4},{3,5},{4,2},{5,3},{6,0},{7,1},{8,14},{9,15},{10,... | collective-permute-start | bytes 884744 | tf_op jit(solution)/shard_map/ppermute | solution.py:487
  16.8 13.2 %collective-permute-start.2 = (bf16[576,256]{1,0:T(8,128)(2,1)S(1)}, bf16[576,256]{1,0:T(8,128)(2,1)S(1)}, u32[]{:S(2)}, u32[]{:S(2)}) collective-permute-start(bf16[576,256]{1,0:T(8,128)(2,1)S(1)} %collective-permute-done.1.refs_2_.refs_1_), channel_id=1, source_target_pairs={{0,2},{1,3},{2,0},{3,1},{4,6},{5,7},{6,4},{7,5},{8,10},{9,11},{10,... | collective-permute-start | bytes 884744 | tf_op jit(solution)/shard_map/ppermute | solution.py:487
  17.7 11.3 %collective-permute-start.4 = (bf16[576,256]{1,0:T(8,128)(2,1)S(1)}, bf16[576,256]{1,0:T(8,128)(2,1)S(1)}, u32[]{:S(2)}, u32[]{:S(2)}) collective-permute-start(bf16[576,256]{1,0:T(8,128)(2,1)S(1)} %collective-permute-done.3.refs_3_.refs_2_), channel_id=1, source_target_pairs={{0,24},{1,25},{2,26},{3,27},{4,28},{5,29},{6,30},{7,31},{8,16},{9,... | collective-permute-start | bytes 884744 | tf_op jit(solution)/shard_map/ppermute | solution.py:487
  33.9 4.2 %collective-permute-start.8 = (bf16[8,272,128]{2,1,0:T(8,128)(2,1)S(1)}, bf16[8,272,128]{2,1,0:T(8,128)(2,1)S(1)}, u32[]{:S(2)}, u32[]{:S(2)}) collective-permute-start(bf16[8,272,128]{2,1,0:T(8,128)(2,1)S(1)} %get-tuple-element.67), channel_id=1, source_target_pairs={{0,1},{1,0},{2,3},{3,2},{4,5},{5,4},{6,7},{7,6},{8,9},{9,8},{10,11... | collective-permute-start | bytes 1671176 | tf_op jit(solution)/shard_map/ppermute | solution.py:487
  34.9 8.4 %collective-permute-start.9 = (bf16[1024,256]{1,0:T(8,128)(2,1)S(1)}, bf16[1024,256]{1,0:T(8,128)(2,1)S(1)}, u32[]{:S(2)}, u32[]{:S(2)}) collective-permute-start(bf16[1024,256]{1,0:T(8,128)(2,1)S(1)} %new_rows.1.own_ref), channel_id=1, source_target_pairs={{0,1},{1,0},{2,3},{3,2},{4,5},{5,4},{6,7},{7,6},{8,9},{9,8},{10,11... | collective-permute-start | bytes 1572872 | tf_op jit(solution)/shard_map/ppermute | solution.py:487
  38.0 5.3 %copy-start = (bf16[512,256]{1,0:T(8,128)(2,1)S(1)}, bf16[512,256]{1,0:T(8,128)(2,1)}, u32[]{:S(2)}) copy-start(bf16[512,256]{1,0:T(8,128)(2,1)} %cache_ref.3) | copy-start | bytes 786436
  38.0 5.3 %copy-start.1 = (s32[128]{0:T(128)S(1)}, s32[128]{0:T(128)}, u32[]{:S(2)}) copy-start(s32[128]{0:T(128)} %len_ref.1) | copy-start | bytes 1540
  38.0 5.3 %copy-start.2 = (s32[256,1]{0,1:T(1,128)S(1)}, s32[256,1]{0,1:T(1,128)}, u32[]{:S(2)}) copy-start(s32[256,1]{0,1:T(1,128)} %param.9) | copy-start | bytes 3076
  39.1 13.7 %all-to-all-start = ((bf16[8,272,128]{2,1,0:T(8,128)(2,1)}), bf16[8,272,128]{2,1,0:T(8,128)(2,1)S(1)}, u32[]{:S(2)}, u32[]{:S(2)}) async-start(bf16[8,272,128]{2,1,0:T(8,128)(2,1)} %merge_pair.1), calls=%async_computation | async-start | bytes 1114112 | tf_op jit(solution)/shard_map/all_to_all | solution.py:542

commit v8 on v7

--- a/solution.py
+++ b/solution.py
@@ -311,6 +311,7 @@
         total,
         ROWS,
         f"flash_{len(held)}",
+        WIDTH if state else 2 * WIDTH,
     )
 
 

time: 53.8 us -> 53.8 us (level)
  no operation moved by 1% of the time
where the time goes in v8:
time: 53.8 us; the launch traced here: 53.6 us
  Pallas kernels  25.6 us (48%)
  starting transfers between devices  18.6 us (35%)
  waiting for transfers between devices  8.63 us (16%)
  between operations  0.79 us (1%)
    pallas_call x5, Pallas kernels, flash_call(): pl.pallas_call(kernel, in_specs=[VMEM] * len(operands), out_specs=jax.tre...  19.1 us
    ppermute x10, starting transfers between devices, shift(): return lax.ppermute(block, AXES, neighbours(dx, flip_z, flip_core))  14.4 us
    all_to_all x1, waiting for transfers between devices, on_device(): parts = lax.all_to_all(part, 'seg', 0, 0)  7.36 us
    all_to_all x1, starting transfers between devices, on_device(): parts = lax.all_to_all(part, 'seg', 0, 0)  4.23 us
    pallas_call x1, Pallas kernels, write_pages(): pl.pallas_call(pages_kernel, in_specs=[SMEM] + [VMEM] * 4, out_specs=VMEM...  2.04 us
    pallas_call x1, Pallas kernels, scaled_queries(): pl.pallas_call(queries_kernel, in_specs=[VMEM] + [pl.BlockSpec(memory_spa...  1.42 us
    ppermute x10, waiting for transfers between devices, shift(): return lax.ppermute(block, AXES, neighbours(dx, flip_z, flip_core))  1.27 us
  transfers between devices with their start and end apart: 11, of which 3 were waited for; matrix products, arithmetic and copies ran while one was open for 0% of the time, Pallas kernels for 37%

profile of v8, /device:TPU:1, one launch (start us, length us, event | category | flops | bytes accessed | tf_op | source)
XLA Modules:
  0.0 53.6 jit_solution(10041751777166237241)
XLA Ops:
  0.6 1.0 %pack.1.refs_2_.refs_0_ = bf16[576,256]{1,0:T(8,128)(2,1)S(1)} custom-call(bf16[512,256]{1,0:T(8,128)(2,1)} %cache_ref.3, bf16[128,256]{1,0:T(8,128)(2,1)} %new_ref.1), custom_call_target="tpu_custom_call" | custom-call | tf_op jit(solution)/shard_map/pack/pallas_call | solution.py:94
  1.6 1.5 %collective-permute-start = (bf16[128,2048]{1,0:T(8,128)(2,1)}, bf16[128,2048]{1,0:T(8,128)(2,1)S(1)}, u32[]{:S(2)}, u32[]{:S(2)}) collective-permute-start(bf16[128,2048]{1,0:T(8,128)(2,1)} %own_hbm.1), channel_id=1, source_target_pairs={{0,1},{1,0},{2,3},{3,2},{4,5},{5,4},{6,7},{7,6},{8,9},{9,8},{10,11... | collective-permute-start | bytes 1572872 | tf_op jit(solution)/shard_map/ppermute | solution.py:488
  3.1 3.9 %collective-permute-start.1 = (bf16[576,256]{1,0:T(8,128)(2,1)S(1)}, bf16[576,256]{1,0:T(8,128)(2,1)S(1)}, u32[]{:S(2)}, u32[]{:S(2)}) collective-permute-start(bf16[576,256]{1,0:T(8,128)(2,1)S(1)} %pack.1.refs_2_.refs_0_), channel_id=1, source_target_pairs={{0,24},{1,25},{2,26},{3,27},{4,28},{5,29},{6,30},{7,31},{8,16},{9,... | collective-permute-start | bytes 884744 | tf_op jit(solution)/shard_map/ppermute | solution.py:488
  7.0 2.7 %collective-permute-start.3 = (bf16[576,256]{1,0:T(8,128)(2,1)S(1)}, bf16[576,256]{1,0:T(8,128)(2,1)S(1)}, u32[]{:S(2)}, u32[]{:S(2)}) collective-permute-start(bf16[576,256]{1,0:T(8,128)(2,1)S(1)} %pack.1.refs_2_.refs_0_), channel_id=1, source_target_pairs={{0,4},{1,5},{2,6},{3,7},{4,0},{5,1},{6,2},{7,3},{8,12},{9,13},{10,... | collective-permute-start | bytes 884744 | tf_op jit(solution)/shard_map/ppermute | solution.py:488
  9.7 0.9 %collective-permute-start.7 = (bf16[576,256]{1,0:T(8,128)(2,1)S(1)}, bf16[576,256]{1,0:T(8,128)(2,1)S(1)}, u32[]{:S(2)}, u32[]{:S(2)}) collective-permute-start(bf16[576,256]{1,0:T(8,128)(2,1)S(1)} %pack.1.refs_2_.refs_0_), channel_id=1, source_target_pairs={{0,6},{1,7},{2,4},{3,5},{4,2},{5,3},{6,0},{7,1},{8,14},{9,15},{10,... | collective-permute-start | bytes 884744 | tf_op jit(solution)/shard_map/ppermute | solution.py:488
  10.6 0.0 collective-permute-start.6
  10.6 0.0 collective-permute-done.twin_ref
  10.6 1.4 %scaled_queries.1 = (bf16[256,4096]{1,0:T(8,128)(2,1)S(1)}, s32[8,128]{1,0:T(8,128)S(1)}) custom-call(bf16[128,2048]{1,0:T(8,128)(2,1)S(1)} %collective-permute-done.twin_ref, bf16[128,2048]{1,0:T(8,128)(2,1)} %own_hbm.1, s32[128]{0:T(128)} %len_ref.1), custom_call_target="tpu_custom_call" | custom-call | tf_op jit(solution)/shard_map/scaled_queries/pallas_call | solution.py:496
  12.0 2.6 %flash_1.1 = (f32[8,4096]{1,0:T(8,128)S(1)}, f32[144,4096]{1,0:T(8,128)S(1)}) custom-call(s32[8,128]{1,0:T(8,128)S(1)} %get-tuple-element.37.refs_0_, bf16[256,4096]{1,0:T(8,128)(2,1)S(1)} %get-tuple-element.36.refs_1_.qt_ref, bf16[576,256]{1,0:T(8,128)(2,1)S(1)} %pack.1.refs_2_.refs_0_), custom_call_target="tpu_custom_call" | custom-call | flops 2147483648 | bytes 1048576 | tf_op jit(solution)/shard_map/flash_1/pallas_call | solution.py:284
  14.6 0.0 collective-permute-done.1.refs_2_.refs_1_
  14.6 2.1 %collective-permute-start.5 = (bf16[576,256]{1,0:T(8,128)(2,1)S(1)}, bf16[576,256]{1,0:T(8,128)(2,1)S(1)}, u32[]{:S(2)}, u32[]{:S(2)}) collective-permute-start(bf16[576,256]{1,0:T(8,128)(2,1)S(1)} %collective-permute-done.1.refs_2_.refs_1_), channel_id=1, source_target_pairs={{0,6},{1,7},{2,4},{3,5},{4,2},{5,3},{6,0},{7,1},{8,14},{9,15},{10,... | collective-permute-start | bytes 884744 | tf_op jit(solution)/shard_map/ppermute | solution.py:488
  16.7 0.6 %collective-permute-start.2 = (bf16[576,256]{1,0:T(8,128)(2,1)S(1)}, bf16[576,256]{1,0:T(8,128)(2,1)S(1)}, u32[]{:S(2)}, u32[]{:S(2)}) collective-permute-start(bf16[576,256]{1,0:T(8,128)(2,1)S(1)} %collective-permute-done.1.refs_2_.refs_1_), channel_id=1, source_target_pairs={{0,2},{1,3},{2,0},{3,1},{4,6},{5,7},{6,4},{7,5},{8,10},{9,11},{10,... | collective-permute-start | bytes 884744 | tf_op jit(solution)/shard_map/ppermute | solution.py:488
  17.3 0.0 collective-permute-done.3.refs_3_.refs_2_
  17.4 1.9 %collective-permute-start.4 = (bf16[576,256]{1,0:T(8,128)(2,1)S(1)}, bf16[576,256]{1,0:T(8,128)(2,1)S(1)}, u32[]{:S(2)}, u32[]{:S(2)}) collective-permute-start(bf16[576,256]{1,0:T(8,128)(2,1)S(1)} %collective-permute-done.3.refs_3_.refs_2_), channel_id=1, source_target_pairs={{0,24},{1,25},{2,26},{3,27},{4,28},{5,29},{6,30},{7,31},{8,16},{9,... | collective-permute-start | bytes 884744 | tf_op jit(solution)/shard_map/ppermute | solution.py:488
  19.2 4.4 %flash_2.2 = (f32[8,4096]{1,0:T(8,128)S(1)}, f32[144,4096]{1,0:T(8,128)S(1)}) custom-call(s32[8,128]{1,0:T(8,128)S(1)} %get-tuple-element.37.refs_0_, bf16[256,4096]{1,0:T(8,128)(2,1)S(1)} %get-tuple-element.36.refs_1_.qt_ref, bf16[576,256]{1,0:T(8,128)(2,1)S(1)} %collective-permute-done.1.refs_2_.refs_1_, ...), custom_call_target="tpu_custom_call" | custom-call | flops 3758096384 | bytes 1048576 | tf_op jit(solution)/shard_map/flash_2/pallas_call | solution.py:284
  23.6 0.1 collective-permute-done.7.refs_4_.refs_3_
  23.7 0.0 collective-permute-done.6.refs_3_.refs_2_
  23.8 5.1 %flash_2.3 = (f32[8,4096]{1,0:T(8,128)S(1)}, f32[144,4096]{1,0:T(8,128)S(1)}) custom-call(s32[8,128]{1,0:T(8,128)S(1)} %get-tuple-element.37.refs_0_, bf16[256,4096]{1,0:T(8,128)(2,1)S(1)} %get-tuple-element.36.refs_1_.qt_ref, bf16[576,256]{1,0:T(8,128)(2,1)S(1)} %collective-permute-done.6.refs_3_.refs_2_, ...), custom_call_target="tpu_custom_call" | custom-call | flops 4294967296 | bytes 1048576 | tf_op jit(solution)/shard_map/flash_2/pallas_call | solution.py:284
  28.9 0.0 collective-permute-done.4.refs_1_.refs_3_.refs_6_
  28.9 1.1 %collective-permute-done.5.refs_2_.refs_4_.refs_7_ = bf16[576,256]{1,0:T(8,128)(2,1)S(1)} collective-permute-done((bf16[576,256]{1,0:T(8,128)(2,1)S(1)}, bf16[576,256]{1,0:T(8,128)(2,1)S(1)}, u32[]{:S(2)}, u32[]{:S(2)}) %collective-permute-start.5) | collective-permute-done | bytes 294944 | tf_op jit(solution)/shard_map/ppermute | solution.py:488
  30.0 0.0 collective-permute-done.2.refs_0_.refs_2_.refs_5_
  30.1 4.0 %flash_twin.1 = (bf16[8,272,128]{2,1,0:T(8,128)(2,1)S(1)}, bf16[1408,256]{1,0:T(8,128)(2,1)S(1)}, bf16[144,1408]{1,0:T(8,128)(2,1)S(1)}, f32[1408,512]{1,0:T(8,128)S(1)}, f32[8,512]{1,0:T(8,128)S(1)}) custom-call(s32[8,128]{1,0:T(8,128)S(1)} %get-tuple-element.37.refs_0_, bf16[256,4096]{1,0:T(8,128)(2,1)S(1)} %get-tuple-element.36.refs_1_.qt_ref, ...), custom_call_target="tpu_custom_call" | custom-call | flops 2952790016 | bytes 1048576 | tf_op jit(solution)/shard_map/flash_twin/pallas_call | solution.py:284
  34.1 0.7 %collective-permute-start.8 = (bf16[8,272,128]{2,1,0:T(8,128)(2,1)S(1)}, bf16[8,272,128]{2,1,0:T(8,128)(2,1)S(1)}, u32[]{:S(2)}, u32[]{:S(2)}) collective-permute-start(bf16[8,272,128]{2,1,0:T(8,128)(2,1)S(1)} %get-tuple-element.67), channel_id=1, source_target_pairs={{0,1},{1,0},{2,3},{3,2},{4,5},{5,4},{6,7},{7,6},{8,9},{9,8},{10,11... | collective-permute-start | bytes 1671176 | tf_op jit(solution)/shard_map/ppermute | solution.py:488
  34.7 0.1 new_rows.1.own_ref
  34.9 0.1 collective-permute-start.9
  35.0 3.0 %flash_own.1.own_ref = bf16[8,272,128]{2,1,0:T(8,128)(2,1)S(1)} custom-call(bf16[256,4096]{1,0:T(8,128)(2,1)S(1)} %get-tuple-element.36.refs_1_.qt_ref, bf16[1408,256]{1,0:T(8,128)(2,1)S(1)} %get-tuple-element.63.keys, bf16[144,1408]{1,0:T(8,128)(2,1)S(1)} %get-tuple-element.64.vals_t, f32[1408,512]{1,0:T(8,128)S(1)} %get-tuple-element.65.scores_ref, ...), custom_call_target="tpu_custom_call" | custom-call | flops 2952790016 | bytes 1048576 | tf_op jit(solution)/shard_map/flash_own/pallas_call | solution.py:284
  38.0 0.0 copy-start
  38.0 0.0 copy-start.1
  38.0 0.0 copy-start.2
  38.0 0.0 collective-permute-done.8.twin_ref
  38.0 1.0 %merge_pair.1 = bf16[8,272,128]{2,1,0:T(8,128)(2,1)} custom-call(bf16[8,272,128]{2,1,0:T(8,128)(2,1)S(1)} %flash_own.1.own_ref, bf16[8,272,128]{2,1,0:T(8,128)(2,1)S(1)} %collective-permute-done.8.twin_ref), custom_call_target="tpu_custom_call" | custom-call | tf_op jit(solution)/shard_map/merge_pair/pallas_call | solution.py:452
  39.1 4.2 %all-to-all-start = ((bf16[8,272,128]{2,1,0:T(8,128)(2,1)}), bf16[8,272,128]{2,1,0:T(8,128)(2,1)S(1)}, u32[]{:S(2)}, u32[]{:S(2)}) async-start(bf16[8,272,128]{2,1,0:T(8,128)(2,1)} %merge_pair.1), calls=%async_computation | async-start | bytes 1114112 | tf_op jit(solution)/shard_map/all_to_all | solution.py:543
  43.3 0.0 collective-permute-done.9.twin_ref
  43.3 0.0 copy-done
  43.3 0.0 copy-done.1
  43.3 0.0 copy-done.2
  43.3 2.0 %write_pages.1 = bf16[512,256]{1,0:T(8,128)(2,1)} custom-call(s32[128]{0:T(128)S(1)} %copy-done.1, s32[1,256]{1,0:T(1,128)S(1)} %bitcast.1, bf16[512,256]{1,0:T(8,128)(2,1)S(1)} %copy-done, bf16[1024,256]{1,0:T(8,128)(2,1)S(1)} %new_rows.1.own_ref, bf16[1024,256]{1,0:T(8,128)(2,1)S(1)} %collective-permute-done.9.twin_ref), custom_call_target="tpu_custom_call" | custom-call | flops 1000000000 | bytes 2097152 | tf_op jit(solution)/shard_map/write_pages/pallas_call | solution.py:419
  45.4 7.4 %all-to-all-done.parts_ref = bf16[8,272,128]{2,1,0:T(8,128)(2,1)S(1)} async-done(((bf16[8,272,128]{2,1,0:T(8,128)(2,1)}), bf16[8,272,128]{2,1,0:T(8,128)(2,1)S(1)}, u32[]{:S(2)}, u32[]{:S(2)}) %all-to-all-start) | async-done | bytes 557088 | tf_op jit(solution)/shard_map/all_to_all | solution.py:543
  52.8 0.8 %merge.1 = bf16[128,256]{1,0:T(8,128)(2,1)} custom-call(bf16[8,272,128]{2,1,0:T(8,128)(2,1)S(1)} %all-to-all-done.parts_ref), custom_call_target="tpu_custom_call" | custom-call | tf_op jit(solution)/shard_map/merge/pallas_call | solution.py:477
  (2 shorter events, 0.1 us)
Async XLA Ops:
  1.6 9.0 %collective-permute-start = (bf16[128,2048]{1,0:T(8,128)(2,1)}, bf16[128,2048]{1,0:T(8,128)(2,1)S(1)}, u32[]{:S(2)}, u32[]{:S(2)}) collective-permute-start(bf16[128,2048]{1,0:T(8,128)(2,1)} %own_hbm.1), channel_id=1, source_target_pairs={{0,1},{1,0},{2,3},{3,2},{4,5},{5,4},{6,7},{7,6},{8,9},{9,8},{10,11... | collective-permute-start | bytes 1572872 | tf_op jit(solution)/shard_map/ppermute | solution.py:488
  3.1 11.5 %collective-permute-start.1 = (bf16[576,256]{1,0:T(8,128)(2,1)S(1)}, bf16[576,256]{1,0:T(8,128)(2,1)S(1)}, u32[]{:S(2)}, u32[]{:S(2)}) collective-permute-start(bf16[576,256]{1,0:T(8,128)(2,1)S(1)} %pack.1.refs_2_.refs_0_), channel_id=1, source_target_pairs={{0,24},{1,25},{2,26},{3,27},{4,28},{5,29},{6,30},{7,31},{8,16},{9,... | collective-permute-start | bytes 884744 | tf_op jit(solution)/shard_map/ppermute | solution.py:488
  7.0 10.4 %collective-permute-start.3 = (bf16[576,256]{1,0:T(8,128)(2,1)S(1)}, bf16[576,256]{1,0:T(8,128)(2,1)S(1)}, u32[]{:S(2)}, u32[]{:S(2)}) collective-permute-start(bf16[576,256]{1,0:T(8,128)(2,1)S(1)} %pack.1.refs_2_.refs_0_), channel_id=1, source_target_pairs={{0,4},{1,5},{2,6},{3,7},{4,0},{5,1},{6,2},{7,3},{8,12},{9,13},{10,... | collective-permute-start | bytes 884744 | tf_op jit(solution)/shard_map/ppermute | solution.py:488
  9.7 14.0 %collective-permute-start.7 = (bf16[576,256]{1,0:T(8,128)(2,1)S(1)}, bf16[576,256]{1,0:T(8,128)(2,1)S(1)}, u32[]{:S(2)}, u32[]{:S(2)}) collective-permute-start(bf16[576,256]{1,0:T(8,128)(2,1)S(1)} %pack.1.refs_2_.refs_0_), channel_id=1, source_target_pairs={{0,6},{1,7},{2,4},{3,5},{4,2},{5,3},{6,0},{7,1},{8,14},{9,15},{10,... | collective-permute-start | bytes 884744 | tf_op jit(solution)/shard_map/ppermute | solution.py:488
  10.6 13.2 %collective-permute-start.6 = (bf16[576,256]{1,0:T(8,128)(2,1)S(1)}, bf16[576,256]{1,0:T(8,128)(2,1)S(1)}, u32[]{:S(2)}, u32[]{:S(2)}) collective-permute-start(bf16[576,256]{1,0:T(8,128)(2,1)S(1)} %pack.1.refs_2_.refs_0_), channel_id=1, source_target_pairs={{0,2},{1,3},{2,0},{3,1},{4,6},{5,7},{6,4},{7,5},{8,10},{9,11},{10,... | collective-permute-start | bytes 884744 | tf_op jit(solution)/shard_map/ppermute | solution.py:488
  14.6 15.4 %collective-permute-start.5 = (bf16[576,256]{1,0:T(8,128)(2,1)S(1)}, bf16[576,256]{1,0:T(8,128)(2,1)S(1)}, u32[]{:S(2)}, u32[]{:S(2)}) collective-permute-start(bf16[576,256]{1,0:T(8,128)(2,1)S(1)} %collective-permute-done.1.refs_2_.refs_1_), channel_id=1, source_target_pairs={{0,6},{1,7},{2,4},{3,5},{4,2},{5,3},{6,0},{7,1},{8,14},{9,15},{10,... | collective-permute-start | bytes 884744 | tf_op jit(solution)/shard_map/ppermute | solution.py:488
  16.7 13.3 %collective-permute-start.2 = (bf16[576,256]{1,0:T(8,128)(2,1)S(1)}, bf16[576,256]{1,0:T(8,128)(2,1)S(1)}, u32[]{:S(2)}, u32[]{:S(2)}) collective-permute-start(bf16[576,256]{1,0:T(8,128)(2,1)S(1)} %collective-permute-done.1.refs_2_.refs_1_), channel_id=1, source_target_pairs={{0,2},{1,3},{2,0},{3,1},{4,6},{5,7},{6,4},{7,5},{8,10},{9,11},{10,... | collective-permute-start | bytes 884744 | tf_op jit(solution)/shard_map/ppermute | solution.py:488
  17.4 11.6 %collective-permute-start.4 = (bf16[576,256]{1,0:T(8,128)(2,1)S(1)}, bf16[576,256]{1,0:T(8,128)(2,1)S(1)}, u32[]{:S(2)}, u32[]{:S(2)}) collective-permute-start(bf16[576,256]{1,0:T(8,128)(2,1)S(1)} %collective-permute-done.3.refs_3_.refs_2_), channel_id=1, source_target_pairs={{0,24},{1,25},{2,26},{3,27},{4,28},{5,29},{6,30},{7,31},{8,16},{9,... | collective-permute-start | bytes 884744 | tf_op jit(solution)/shard_map/ppermute | solution.py:488
  34.1 4.0 %collective-permute-start.8 = (bf16[8,272,128]{2,1,0:T(8,128)(2,1)S(1)}, bf16[8,272,128]{2,1,0:T(8,128)(2,1)S(1)}, u32[]{:S(2)}, u32[]{:S(2)}) collective-permute-start(bf16[8,272,128]{2,1,0:T(8,128)(2,1)S(1)} %get-tuple-element.67), channel_id=1, source_target_pairs={{0,1},{1,0},{2,3},{3,2},{4,5},{5,4},{6,7},{7,6},{8,9},{9,8},{10,11... | collective-permute-start | bytes 1671176 | tf_op jit(solution)/shard_map/ppermute | solution.py:488
  34.9 8.5 %collective-permute-start.9 = (bf16[1024,256]{1,0:T(8,128)(2,1)S(1)}, bf16[1024,256]{1,0:T(8,128)(2,1)S(1)}, u32[]{:S(2)}, u32[]{:S(2)}) collective-permute-start(bf16[1024,256]{1,0:T(8,128)(2,1)S(1)} %new_rows.1.own_ref), channel_id=1, source_target_pairs={{0,1},{1,0},{2,3},{3,2},{4,5},{5,4},{6,7},{7,6},{8,9},{9,8},{10,11... | collective-permute-start | bytes 1572872 | tf_op jit(solution)/shard_map/ppermute | solution.py:488
  38.0 5.3 %copy-start = (bf16[512,256]{1,0:T(8,128)(2,1)S(1)}, bf16[512,256]{1,0:T(8,128)(2,1)}, u32[]{:S(2)}) copy-start(bf16[512,256]{1,0:T(8,128)(2,1)} %cache_ref.3) | copy-start | bytes 786436
  38.0 5.3 %copy-start.1 = (s32[128]{0:T(128)S(1)}, s32[128]{0:T(128)}, u32[]{:S(2)}) copy-start(s32[128]{0:T(128)} %len_ref.1) | copy-start | bytes 1540
  38.0 5.3 %copy-start.2 = (s32[256,1]{0,1:T(1,128)S(1)}, s32[256,1]{0,1:T(1,128)}, u32[]{:S(2)}) copy-start(s32[256,1]{0,1:T(1,128)} %param.9) | copy-start | bytes 3076
  39.1 13.7 %all-to-all-start = ((bf16[8,272,128]{2,1,0:T(8,128)(2,1)}), bf16[8,272,128]{2,1,0:T(8,128)(2,1)S(1)}, u32[]{:S(2)}, u32[]{:S(2)}) async-start(bf16[8,272,128]{2,1,0:T(8,128)(2,1)} %merge_pair.1), calls=%async_computation | async-start | bytes 1114112 | tf_op jit(solution)/shard_map/all_to_all | solution.py:543

commit v9 on v8

--- a/solution.py
+++ b/solution.py
@@ -72,7 +72,9 @@
             qt_ref[HD : 2 * HD, cols] = (scaled - high.astype(F32)).astype(BF16)
     len_copy.wait()
     for j, slot in enumerate(SLOT_ORDER):
-        filled_ref[j : j + 1, :] = jnp.full((1, 128), len_ref[origin(slot)], jnp.int32)
+        here = lax.broadcasted_iota(jnp.int32, len_ref.shape, 1) == origin(slot)
+        filled = jnp.sum(jnp.where(here, len_ref[...], 0).astype(F32), axis=1, keepdims=True)
+        filled_ref[j : j + 1, :] = jnp.broadcast_to(filled.astype(jnp.int32), (1, 128))
 
 
 def in_hbm(array):
@@ -503,12 +505,12 @@
         ],
         scratch_shapes=[
             pltpu.VMEM(own.shape, BF16),
-            pltpu.SMEM(cache_len.shape, jnp.int32),
+            pltpu.VMEM((1, cache_len.shape[0]), jnp.int32),
             pltpu.SemaphoreType.DMA((2,)),
         ],
         compiler_params=pltpu.CompilerParams(vmem_limit_bytes=4 << 20),
         name="scaled_queries",
-    )(twin, in_hbm(own), in_hbm(cache_len))
+    )(twin, in_hbm(own), in_hbm(cache_len.reshape(1, -1)))
 
 
 def on_device(queries, new_kv, cache_kv, cache_len, page_owner):

time: 53.8 us -> 53.8 us (level)
  no operation moved by 1% of the time
where the time goes in v9:
time: 53.8 us; the launch traced here: 53.6 us
  Pallas kernels  25.6 us (48%)
  starting transfers between devices  18.5 us (34%)
  waiting for transfers between devices  8.63 us (16%)
  between operations  0.79 us (1%)
    pallas_call x5, Pallas kernels, flash_call(): pl.pallas_call(kernel, in_specs=[VMEM] * len(operands), out_specs=jax.tre...  19.1 us
    ppermute x10, starting transfers between devices, shift(): return lax.ppermute(block, AXES, neighbours(dx, flip_z, flip_core))  14.3 us
    all_to_all x1, waiting for transfers between devices, on_device(): parts = lax.all_to_all(part, 'seg', 0, 0)  7.36 us
    all_to_all x1, starting transfers between devices, on_device(): parts = lax.all_to_all(part, 'seg', 0, 0)  4.23 us
    pallas_call x1, Pallas kernels, write_pages(): pl.pallas_call(pages_kernel, in_specs=[SMEM] + [VMEM] * 4, out_specs=VMEM...  2.04 us
    pallas_call x1, Pallas kernels, scaled_queries(): pl.pallas_call(queries_kernel, in_specs=[VMEM] + [pl.BlockSpec(memory_spa...  1.48 us
    ppermute x10, waiting for transfers between devices, shift(): return lax.ppermute(block, AXES, neighbours(dx, flip_z, flip_core))  1.27 us
  transfers between devices with their start and end apart: 11, of which 3 were waited for; matrix products, arithmetic and copies ran while one was open for 0% of the time, Pallas kernels for 37%

profile of v9, /device:TPU:1, one launch (start us, length us, event | category | flops | bytes accessed | tf_op | source)
XLA Modules:
  0.0 53.6 jit_solution(6361802625693375433)
XLA Ops:
  0.6 1.0 %pack.1.refs_2_.refs_0_ = bf16[576,256]{1,0:T(8,128)(2,1)S(1)} custom-call(bf16[512,256]{1,0:T(8,128)(2,1)} %cache_ref.3, bf16[128,256]{1,0:T(8,128)(2,1)} %new_ref.1), custom_call_target="tpu_custom_call" | custom-call | tf_op jit(solution)/shard_map/pack/pallas_call | solution.py:96
  1.6 1.5 %collective-permute-start = (bf16[128,2048]{1,0:T(8,128)(2,1)}, bf16[128,2048]{1,0:T(8,128)(2,1)S(1)}, u32[]{:S(2)}, u32[]{:S(2)}) collective-permute-start(bf16[128,2048]{1,0:T(8,128)(2,1)} %own_hbm.1), channel_id=1, source_target_pairs={{0,1},{1,0},{2,3},{3,2},{4,5},{5,4},{6,7},{7,6},{8,9},{9,8},{10,11... | collective-permute-start | bytes 1572872 | tf_op jit(solution)/shard_map/ppermute | solution.py:490
  3.1 3.9 %collective-permute-start.1 = (bf16[576,256]{1,0:T(8,128)(2,1)S(1)}, bf16[576,256]{1,0:T(8,128)(2,1)S(1)}, u32[]{:S(2)}, u32[]{:S(2)}) collective-permute-start(bf16[576,256]{1,0:T(8,128)(2,1)S(1)} %pack.1.refs_2_.refs_0_), channel_id=1, source_target_pairs={{0,24},{1,25},{2,26},{3,27},{4,28},{5,29},{6,30},{7,31},{8,16},{9,... | collective-permute-start | bytes 884744 | tf_op jit(solution)/shard_map/ppermute | solution.py:490
  7.0 2.7 %collective-permute-start.3 = (bf16[576,256]{1,0:T(8,128)(2,1)S(1)}, bf16[576,256]{1,0:T(8,128)(2,1)S(1)}, u32[]{:S(2)}, u32[]{:S(2)}) collective-permute-start(bf16[576,256]{1,0:T(8,128)(2,1)S(1)} %pack.1.refs_2_.refs_0_), channel_id=1, source_target_pairs={{0,4},{1,5},{2,6},{3,7},{4,0},{5,1},{6,2},{7,3},{8,12},{9,13},{10,... | collective-permute-start | bytes 884744 | tf_op jit(solution)/shard_map/ppermute | solution.py:490
  9.7 0.9 %collective-permute-start.7 = (bf16[576,256]{1,0:T(8,128)(2,1)S(1)}, bf16[576,256]{1,0:T(8,128)(2,1)S(1)}, u32[]{:S(2)}, u32[]{:S(2)}) collective-permute-start(bf16[576,256]{1,0:T(8,128)(2,1)S(1)} %pack.1.refs_2_.refs_0_), channel_id=1, source_target_pairs={{0,6},{1,7},{2,4},{3,5},{4,2},{5,3},{6,0},{7,1},{8,14},{9,15},{10,... | collective-permute-start | bytes 884744 | tf_op jit(solution)/shard_map/ppermute | solution.py:490
  10.6 0.0 collective-permute-start.6
  10.6 0.0 collective-permute-done.twin_ref
  10.6 1.5 %scaled_queries.1 = (bf16[256,4096]{1,0:T(8,128)(2,1)S(1)}, s32[8,128]{1,0:T(8,128)S(1)}) custom-call(bf16[128,2048]{1,0:T(8,128)(2,1)S(1)} %collective-permute-done.twin_ref, bf16[128,2048]{1,0:T(8,128)(2,1)} %own_hbm.1, s32[1,128]{1,0:T(1,128)} %bitcast.2), custom_call_target="tpu_custom_call" | custom-call | tf_op jit(solution)/shard_map/scaled_queries/pallas_call | solution.py:498
  12.1 2.6 %flash_1.1 = (f32[8,4096]{1,0:T(8,128)S(1)}, f32[144,4096]{1,0:T(8,128)S(1)}) custom-call(s32[8,128]{1,0:T(8,128)S(1)} %get-tuple-element.37.refs_0_, bf16[256,4096]{1,0:T(8,128)(2,1)S(1)} %get-tuple-element.36.refs_1_.qt_ref, bf16[576,256]{1,0:T(8,128)(2,1)S(1)} %pack.1.refs_2_.refs_0_), custom_call_target="tpu_custom_call" | custom-call | flops 2147483648 | bytes 1048576 | tf_op jit(solution)/shard_map/flash_1/pallas_call | solution.py:286
  14.6 0.0 collective-permute-done.1.refs_2_.refs_1_
  14.7 2.1 %collective-permute-start.5 = (bf16[576,256]{1,0:T(8,128)(2,1)S(1)}, bf16[576,256]{1,0:T(8,128)(2,1)S(1)}, u32[]{:S(2)}, u32[]{:S(2)}) collective-permute-start(bf16[576,256]{1,0:T(8,128)(2,1)S(1)} %collective-permute-done.1.refs_2_.refs_1_), channel_id=1, source_target_pairs={{0,6},{1,7},{2,4},{3,5},{4,2},{5,3},{6,0},{7,1},{8,14},{9,15},{10,... | collective-permute-start | bytes 884744 | tf_op jit(solution)/shard_map/ppermute | solution.py:490
  16.7 0.7 %collective-permute-start.2 = (bf16[576,256]{1,0:T(8,128)(2,1)S(1)}, bf16[576,256]{1,0:T(8,128)(2,1)S(1)}, u32[]{:S(2)}, u32[]{:S(2)}) collective-permute-start(bf16[576,256]{1,0:T(8,128)(2,1)S(1)} %collective-permute-done.1.refs_2_.refs_1_), channel_id=1, source_target_pairs={{0,2},{1,3},{2,0},{3,1},{4,6},{5,7},{6,4},{7,5},{8,10},{9,11},{10,... | collective-permute-start | bytes 884744 | tf_op jit(solution)/shard_map/ppermute | solution.py:490
  17.4 0.0 collective-permute-done.3.refs_3_.refs_2_
  17.4 1.8 %collective-permute-start.4 = (bf16[576,256]{1,0:T(8,128)(2,1)S(1)}, bf16[576,256]{1,0:T(8,128)(2,1)S(1)}, u32[]{:S(2)}, u32[]{:S(2)}) collective-permute-start(bf16[576,256]{1,0:T(8,128)(2,1)S(1)} %collective-permute-done.3.refs_3_.refs_2_), channel_id=1, source_target_pairs={{0,24},{1,25},{2,26},{3,27},{4,28},{5,29},{6,30},{7,31},{8,16},{9,... | collective-permute-start | bytes 884744 | tf_op jit(solution)/shard_map/ppermute | solution.py:490
  19.2 4.4 %flash_2.2 = (f32[8,4096]{1,0:T(8,128)S(1)}, f32[144,4096]{1,0:T(8,128)S(1)}) custom-call(s32[8,128]{1,0:T(8,128)S(1)} %get-tuple-element.37.refs_0_, bf16[256,4096]{1,0:T(8,128)(2,1)S(1)} %get-tuple-element.36.refs_1_.qt_ref, bf16[576,256]{1,0:T(8,128)(2,1)S(1)} %collective-permute-done.1.refs_2_.refs_1_, ...), custom_call_target="tpu_custom_call" | custom-call | flops 3758096384 | bytes 1048576 | tf_op jit(solution)/shard_map/flash_2/pallas_call | solution.py:286
  23.6 0.1 collective-permute-done.7.refs_4_.refs_3_
  23.7 0.0 collective-permute-done.6.refs_3_.refs_2_
  23.8 5.1 %flash_2.3 = (f32[8,4096]{1,0:T(8,128)S(1)}, f32[144,4096]{1,0:T(8,128)S(1)}) custom-call(s32[8,128]{1,0:T(8,128)S(1)} %get-tuple-element.37.refs_0_, bf16[256,4096]{1,0:T(8,128)(2,1)S(1)} %get-tuple-element.36.refs_1_.qt_ref, bf16[576,256]{1,0:T(8,128)(2,1)S(1)} %collective-permute-done.6.refs_3_.refs_2_, ...), custom_call_target="tpu_custom_call" | custom-call | flops 4294967296 | bytes 1048576 | tf_op jit(solution)/shard_map/flash_2/pallas_call | solution.py:286
  28.9 0.0 collective-permute-done.4.refs_1_.refs_3_.refs_6_
  28.9 1.1 %collective-permute-done.5.refs_2_.refs_4_.refs_7_ = bf16[576,256]{1,0:T(8,128)(2,1)S(1)} collective-permute-done((bf16[576,256]{1,0:T(8,128)(2,1)S(1)}, bf16[576,256]{1,0:T(8,128)(2,1)S(1)}, u32[]{:S(2)}, u32[]{:S(2)}) %collective-permute-start.5) | collective-permute-done | bytes 294944 | tf_op jit(solution)/shard_map/ppermute | solution.py:490
  30.0 0.0 collective-permute-done.2.refs_0_.refs_2_.refs_5_
  30.1 4.0 %flash_twin.1 = (bf16[8,272,128]{2,1,0:T(8,128)(2,1)S(1)}, bf16[1408,256]{1,0:T(8,128)(2,1)S(1)}, bf16[144,1408]{1,0:T(8,128)(2,1)S(1)}, f32[1408,512]{1,0:T(8,128)S(1)}, f32[8,512]{1,0:T(8,128)S(1)}) custom-call(s32[8,128]{1,0:T(8,128)S(1)} %get-tuple-element.37.refs_0_, bf16[256,4096]{1,0:T(8,128)(2,1)S(1)} %get-tuple-element.36.refs_1_.qt_ref, ...), custom_call_target="tpu_custom_call" | custom-call | flops 2952790016 | bytes 1048576 | tf_op jit(solution)/shard_map/flash_twin/pallas_call | solution.py:286
  34.1 0.7 %collective-permute-start.8 = (bf16[8,272,128]{2,1,0:T(8,128)(2,1)S(1)}, bf16[8,272,128]{2,1,0:T(8,128)(2,1)S(1)}, u32[]{:S(2)}, u32[]{:S(2)}) collective-permute-start(bf16[8,272,128]{2,1,0:T(8,128)(2,1)S(1)} %get-tuple-element.67), channel_id=1, source_target_pairs={{0,1},{1,0},{2,3},{3,2},{4,5},{5,4},{6,7},{7,6},{8,9},{9,8},{10,11... | collective-permute-start | bytes 1671176 | tf_op jit(solution)/shard_map/ppermute | solution.py:490
  34.7 0.1 new_rows.1.own_ref
  34.9 0.1 collective-permute-start.9
  35.0 3.0 %flash_own.1.own_ref = bf16[8,272,128]{2,1,0:T(8,128)(2,1)S(1)} custom-call(bf16[256,4096]{1,0:T(8,128)(2,1)S(1)} %get-tuple-element.36.refs_1_.qt_ref, bf16[1408,256]{1,0:T(8,128)(2,1)S(1)} %get-tuple-element.63.keys, bf16[144,1408]{1,0:T(8,128)(2,1)S(1)} %get-tuple-element.64.vals_t, f32[1408,512]{1,0:T(8,128)S(1)} %get-tuple-element.65.scores_ref, ...), custom_call_target="tpu_custom_call" | custom-call | flops 2952790016 | bytes 1048576 | tf_op jit(solution)/shard_map/flash_own/pallas_call | solution.py:286
  38.0 0.0 copy-start
  38.0 0.0 copy-start.1
  38.0 0.0 copy-start.2
  38.0 0.0 collective-permute-done.8.twin_ref
  38.0 1.0 %merge_pair.1 = bf16[8,272,128]{2,1,0:T(8,128)(2,1)} custom-call(bf16[8,272,128]{2,1,0:T(8,128)(2,1)S(1)} %flash_own.1.own_ref, bf16[8,272,128]{2,1,0:T(8,128)(2,1)S(1)} %collective-permute-done.8.twin_ref), custom_call_target="tpu_custom_call" | custom-call | tf_op jit(solution)/shard_map/merge_pair/pallas_call | solution.py:454
  39.1 4.2 %all-to-all-start = ((bf16[8,272,128]{2,1,0:T(8,128)(2,1)}), bf16[8,272,128]{2,1,0:T(8,128)(2,1)S(1)}, u32[]{:S(2)}, u32[]{:S(2)}) async-start(bf16[8,272,128]{2,1,0:T(8,128)(2,1)} %merge_pair.1), calls=%async_computation | async-start | bytes 1114112 | tf_op jit(solution)/shard_map/all_to_all | solution.py:545
  43.3 0.0 collective-permute-done.9.twin_ref
  43.3 0.0 copy-done
  43.3 0.0 copy-done.1
  43.3 0.0 copy-done.2
  43.3 2.0 %write_pages.1 = bf16[512,256]{1,0:T(8,128)(2,1)} custom-call(s32[128]{0:T(128)S(1)} %copy-done.1, s32[1,256]{1,0:T(1,128)S(1)} %bitcast.3, bf16[512,256]{1,0:T(8,128)(2,1)S(1)} %copy-done, bf16[1024,256]{1,0:T(8,128)(2,1)S(1)} %new_rows.1.own_ref, bf16[1024,256]{1,0:T(8,128)(2,1)S(1)} %collective-permute-done.9.twin_ref), custom_call_target="tpu_custom_call" | custom-call | flops 1000000000 | bytes 2097152 | tf_op jit(solution)/shard_map/write_pages/pallas_call | solution.py:421
  45.4 7.4 %all-to-all-done.parts_ref = bf16[8,272,128]{2,1,0:T(8,128)(2,1)S(1)} async-done(((bf16[8,272,128]{2,1,0:T(8,128)(2,1)}), bf16[8,272,128]{2,1,0:T(8,128)(2,1)S(1)}, u32[]{:S(2)}, u32[]{:S(2)}) %all-to-all-start) | async-done | bytes 557088 | tf_op jit(solution)/shard_map/all_to_all | solution.py:545
  52.8 0.8 %merge.1 = bf16[128,256]{1,0:T(8,128)(2,1)} custom-call(bf16[8,272,128]{2,1,0:T(8,128)(2,1)S(1)} %all-to-all-done.parts_ref), custom_call_target="tpu_custom_call" | custom-call | tf_op jit(solution)/shard_map/merge/pallas_call | solution.py:479
  (2 shorter events, 0.1 us)
Async XLA Ops:
  1.6 9.0 %collective-permute-start = (bf16[128,2048]{1,0:T(8,128)(2,1)}, bf16[128,2048]{1,0:T(8,128)(2,1)S(1)}, u32[]{:S(2)}, u32[]{:S(2)}) collective-permute-start(bf16[128,2048]{1,0:T(8,128)(2,1)} %own_hbm.1), channel_id=1, source_target_pairs={{0,1},{1,0},{2,3},{3,2},{4,5},{5,4},{6,7},{7,6},{8,9},{9,8},{10,11... | collective-permute-start | bytes 1572872 | tf_op jit(solution)/shard_map/ppermute | solution.py:490
  3.1 11.5 %collective-permute-start.1 = (bf16[576,256]{1,0:T(8,128)(2,1)S(1)}, bf16[576,256]{1,0:T(8,128)(2,1)S(1)}, u32[]{:S(2)}, u32[]{:S(2)}) collective-permute-start(bf16[576,256]{1,0:T(8,128)(2,1)S(1)} %pack.1.refs_2_.refs_0_), channel_id=1, source_target_pairs={{0,24},{1,25},{2,26},{3,27},{4,28},{5,29},{6,30},{7,31},{8,16},{9,... | collective-permute-start | bytes 884744 | tf_op jit(solution)/shard_map/ppermute | solution.py:490
  7.0 10.5 %collective-permute-start.3 = (bf16[576,256]{1,0:T(8,128)(2,1)S(1)}, bf16[576,256]{1,0:T(8,128)(2,1)S(1)}, u32[]{:S(2)}, u32[]{:S(2)}) collective-permute-start(bf16[576,256]{1,0:T(8,128)(2,1)S(1)} %pack.1.refs_2_.refs_0_), channel_id=1, source_target_pairs={{0,4},{1,5},{2,6},{3,7},{4,0},{5,1},{6,2},{7,3},{8,12},{9,13},{10,... | collective-permute-start | bytes 884744 | tf_op jit(solution)/shard_map/ppermute | solution.py:490
  9.7 14.0 %collective-permute-start.7 = (bf16[576,256]{1,0:T(8,128)(2,1)S(1)}, bf16[576,256]{1,0:T(8,128)(2,1)S(1)}, u32[]{:S(2)}, u32[]{:S(2)}) collective-permute-start(bf16[576,256]{1,0:T(8,128)(2,1)S(1)} %pack.1.refs_2_.refs_0_), channel_id=1, source_target_pairs={{0,6},{1,7},{2,4},{3,5},{4,2},{5,3},{6,0},{7,1},{8,14},{9,15},{10,... | collective-permute-start | bytes 884744 | tf_op jit(solution)/shard_map/ppermute | solution.py:490
  10.6 13.2 %collective-permute-start.6 = (bf16[576,256]{1,0:T(8,128)(2,1)S(1)}, bf16[576,256]{1,0:T(8,128)(2,1)S(1)}, u32[]{:S(2)}, u32[]{:S(2)}) collective-permute-start(bf16[576,256]{1,0:T(8,128)(2,1)S(1)} %pack.1.refs_2_.refs_0_), channel_id=1, source_target_pairs={{0,2},{1,3},{2,0},{3,1},{4,6},{5,7},{6,4},{7,5},{8,10},{9,11},{10,... | collective-permute-start | bytes 884744 | tf_op jit(solution)/shard_map/ppermute | solution.py:490
  14.7 15.4 %collective-permute-start.5 = (bf16[576,256]{1,0:T(8,128)(2,1)S(1)}, bf16[576,256]{1,0:T(8,128)(2,1)S(1)}, u32[]{:S(2)}, u32[]{:S(2)}) collective-permute-start(bf16[576,256]{1,0:T(8,128)(2,1)S(1)} %collective-permute-done.1.refs_2_.refs_1_), channel_id=1, source_target_pairs={{0,6},{1,7},{2,4},{3,5},{4,2},{5,3},{6,0},{7,1},{8,14},{9,15},{10,... | collective-permute-start | bytes 884744 | tf_op jit(solution)/shard_map/ppermute | solution.py:490
  16.7 13.3 %collective-permute-start.2 = (bf16[576,256]{1,0:T(8,128)(2,1)S(1)}, bf16[576,256]{1,0:T(8,128)(2,1)S(1)}, u32[]{:S(2)}, u32[]{:S(2)}) collective-permute-start(bf16[576,256]{1,0:T(8,128)(2,1)S(1)} %collective-permute-done.1.refs_2_.refs_1_), channel_id=1, source_target_pairs={{0,2},{1,3},{2,0},{3,1},{4,6},{5,7},{6,4},{7,5},{8,10},{9,11},{10,... | collective-permute-start | bytes 884744 | tf_op jit(solution)/shard_map/ppermute | solution.py:490
  17.4 11.5 %collective-permute-start.4 = (bf16[576,256]{1,0:T(8,128)(2,1)S(1)}, bf16[576,256]{1,0:T(8,128)(2,1)S(1)}, u32[]{:S(2)}, u32[]{:S(2)}) collective-permute-start(bf16[576,256]{1,0:T(8,128)(2,1)S(1)} %collective-permute-done.3.refs_3_.refs_2_), channel_id=1, source_target_pairs={{0,24},{1,25},{2,26},{3,27},{4,28},{5,29},{6,30},{7,31},{8,16},{9,... | collective-permute-start | bytes 884744 | tf_op jit(solution)/shard_map/ppermute | solution.py:490
  34.1 4.0 %collective-permute-start.8 = (bf16[8,272,128]{2,1,0:T(8,128)(2,1)S(1)}, bf16[8,272,128]{2,1,0:T(8,128)(2,1)S(1)}, u32[]{:S(2)}, u32[]{:S(2)}) collective-permute-start(bf16[8,272,128]{2,1,0:T(8,128)(2,1)S(1)} %get-tuple-element.67), channel_id=1, source_target_pairs={{0,1},{1,0},{2,3},{3,2},{4,5},{5,4},{6,7},{7,6},{8,9},{9,8},{10,11... | collective-permute-start | bytes 1671176 | tf_op jit(solution)/shard_map/ppermute | solution.py:490
  34.9 8.5 %collective-permute-start.9 = (bf16[1024,256]{1,0:T(8,128)(2,1)S(1)}, bf16[1024,256]{1,0:T(8,128)(2,1)S(1)}, u32[]{:S(2)}, u32[]{:S(2)}) collective-permute-start(bf16[1024,256]{1,0:T(8,128)(2,1)S(1)} %new_rows.1.own_ref), channel_id=1, source_target_pairs={{0,1},{1,0},{2,3},{3,2},{4,5},{5,4},{6,7},{7,6},{8,9},{9,8},{10,11... | collective-permute-start | bytes 1572872 | tf_op jit(solution)/shard_map/ppermute | solution.py:490
  38.0 5.3 %copy-start = (bf16[512,256]{1,0:T(8,128)(2,1)S(1)}, bf16[512,256]{1,0:T(8,128)(2,1)}, u32[]{:S(2)}) copy-start(bf16[512,256]{1,0:T(8,128)(2,1)} %cache_ref.3) | copy-start | bytes 786436
  38.0 5.3 %copy-start.1 = (s32[128]{0:T(128)S(1)}, s32[128]{0:T(128)}, u32[]{:S(2)}) copy-start(s32[128]{0:T(128)} %len_ref.1) | copy-start | bytes 1540
  38.0 5.3 %copy-start.2 = (s32[256,1]{0,1:T(1,128)S(1)}, s32[256,1]{0,1:T(1,128)}, u32[]{:S(2)}) copy-start(s32[256,1]{0,1:T(1,128)} %param.9) | copy-start | bytes 3076
  39.1 13.7 %all-to-all-start = ((bf16[8,272,128]{2,1,0:T(8,128)(2,1)}), bf16[8,272,128]{2,1,0:T(8,128)(2,1)S(1)}, u32[]{:S(2)}, u32[]{:S(2)}) async-start(bf16[8,272,128]{2,1,0:T(8,128)(2,1)} %merge_pair.1), calls=%async_computation | async-start | bytes 1114112 | tf_op jit(solution)/shard_map/all_to_all | solution.py:545
